TPU v7x, 32 devices: a whole 2x2x4 slice. The times are simulated.
32 devices in a mesh: dp: 8 (over z, core), blk: 4 (over y, x).
Axes of the slice: x: 2, y: 2, z: 4, core: 2. Of those that a mesh axis runs over, the one named last changes fastest.
Arguments:
- frames: bfloat16 [32, 1280, 256], P('dp', 'blk'), may hold values from -6 to 6
- weight: bfloat16 [1280, 11520], P('blk'), may hold values from -0.0546875 to 0.0546875
- bias: float32 [1280], P('blk'), may hold values from -3 to 3
- cotangent: bfloat16 [32, 1280, 256], P('dp', 'blk'), may hold values from -6 to 6
Outputs:
- response: bfloat16 [32, 1280, 256], P('dp', 'blk')
- frame_grad: bfloat16 [32, 1280, 256], P('dp', 'blk')
- weight_grad: float32 [1280, 11520], P(('blk', 'dp'))
All inputs are finite; a program needn't handle non-finite values.
Results may differ from a plain program's by a relative error of at most 0.001.
Values may be sent and summed in bfloat16 or wider, within the bound.
No kernel may reach another device: no remote copies, remote signals or barrier semaphores. Data moves between devices by JAX's collectives and lax.ppermute only.
A program may use at most 128 MiB of HBM per device.

v0:
```python
import functools

import jax
import jax.numpy as jnp
from jax import lax
from jax.experimental import pallas as pl
from jax.experimental.pallas import tpu as pltpu
from jax.sharding import PartitionSpec as P

WD = 16
TAPS = 9
F32, BF16 = jnp.float32, jnp.bfloat16
NT = (((1,), (1,)), ((), ()))
TN = (((0,), (0,)), ((), ()))
VMEM = pl.BlockSpec(memory_space=pltpu.VMEM)
ANY = pl.BlockSpec(memory_space=pl.ANY)
HBM = pl.BlockSpec(memory_space=pltpu.HBM)
SPAN = 125.0
RATE = 1e9
ORDER = ("a", "ka", "fx", "a2", "b", "c", "fy", "kb", "b2", "d", "kd", "c2", "resp", "f2", "d2", "fl", "wab", "wcd")
COST = dict(a=45, ka=40, fx=85, a2=7, b=40, c=40, d=40, kb=50, kd=40, fy=85, b2=7, c2=7, resp=110, f2=15, d2=7, fl=12, wab=24, wcd=24)


def shift_cells(maps, step_row, step_col):
    cells = maps.shape[-1]
    margin = WD + 1
    widths = [(0, 0)] * (maps.ndim - 1) + [(margin, margin)]
    flat = jnp.pad(maps, widths)
    begin = margin + step_row * WD + step_col
    moved = lax.slice_in_dim(flat, begin, begin + cells, axis=maps.ndim - 1)
    column = jnp.arange(cells, dtype=jnp.int32) % WD + step_col
    keeper = ((column >= 0) & (column < WD)).astype(maps.dtype)
    return moved * keeper


def general_body(frames, weight, bias, cotangent):
    nframe = frames.shape[0]
    local_ch = frames.shape[1]
    cells = frames.shape[2]
    whole = lax.all_gather(frames, "blk", axis=1, tiled=True)
    all_ch = whole.shape[1]
    total = jnp.zeros((nframe, local_ch, cells), F32)
    grads = []
    for tap in range(TAPS):
        ky, kx = divmod(tap, 3)
        piece = shift_cells(whole, ky - 1, kx - 1)
        w_tap = weight[:, tap * all_ch : (tap + 1) * all_ch]
        total = total + jnp.einsum("oi,fic->foc", w_tap, piece, preferred_element_type=F32)
        grads.append(
            lax.dot_general(cotangent, piece, (((0, 2), (0, 2)), ((), ())), preferred_element_type=F32)
        )
    response = (total + bias[None, :, None]).astype(BF16)
    local_grad = jnp.concatenate(grads, axis=1)
    weight_grad = lax.psum_scatter(local_grad, "dp", scatter_dimension=0, tiled=True)
    cot_moved = [shift_cells(cotangent, 1 - tap // 3, 1 - tap % 3) for tap in range(TAPS)]
    accum = jnp.zeros((all_ch, nframe, cells), F32)
    for tap in range(TAPS):
        w_cols = lax.slice_in_dim(weight, tap * all_ch, (tap + 1) * all_ch, axis=1)
        accum = accum + jnp.einsum("oi,foc->ifc", w_cols, cot_moved[tap], preferred_element_type=F32)
    shares = lax.psum_scatter(accum, "blk", scatter_dimension=0, tiled=True)
    frame_grad = jnp.transpose(shares, (1, 0, 2)).astype(BF16)
    return (response, frame_grad, weight_grad)


def scale_of(largest):
    return (jnp.maximum(largest, 1e-30) * 1.01).astype(BF16).astype(F32)


def encode(x, s):
    y = jnp.exp2(jnp.abs(x) * (2 * SPAN / s) - SPAN)
    return jnp.where(x < 0, -y, y)


def decode(code, s):
    y = code.astype(F32)
    v = (jnp.log2(jnp.abs(y)) + SPAN) * (s * (0.5 / SPAN))
    return jnp.where(y < 0, -v, v)


def cell_masks(rows, cells):
    lane = lax.broadcasted_iota(jnp.int32, (rows, cells), 1)
    return lane // WD, lane % WD


def moved(x, step, row, col, ky, kx):
    cells = x.shape[1]
    dy, dx = step * (ky - 1), step * (kx - 1)
    off = (dy * WD + dx) % cells
    out = pltpu.roll(x, off, 1) if off else x
    ok = None
    if dy:
        ok = (row >= dy) if dy > 0 else (row < cells // WD + dy)
    if dx:
        okx = (col >= dx) if dx > 0 else (col < WD + dx)
        ok = okx if ok is None else ok & okx
    return out if ok is None else jnp.where(ok, out, 0.0)


def put_rows_coded(out_ref, lead, values, width):
    rows, padded = values.shape
    s = scale_of(jnp.max(jnp.abs(values), axis=1, keepdims=True))
    codes = encode(values, s)
    last = padded - 128
    lane = lax.broadcasted_iota(jnp.int32, (rows, 128), 1) + last
    out_ref[lead + (slice(None), slice(0, last))] = codes[:, :last].astype(BF16)
    tail = jnp.where(lane < width, codes[:, last:], s)
    out_ref[lead + (slice(None), slice(last, padded))] = tail.astype(BF16)


def take_rows_coded(code, width):
    s = code[:, width : width + 1].astype(F32)
    return decode(code, s)


def weight_sums(width, cs_ref, xs_ref, f_ref):
    pieces, rows, padded = f_ref.shape
    ch = xs_ref.shape[0] // pieces
    for p in range(pieces):
        f_ref[p, :, width:] = jnp.zeros((rows, padded - width), F32)
    got = lax.dot_general(cs_ref[...], xs_ref[...], NT, preferred_element_type=F32)
    for t in range(TAPS):
        for p in range(pieces):
            f_ref[p, :, t * ch : (t + 1) * ch] = got[t * rows : (t + 1) * rows, p * ch : (p + 1) * ch]


def shifted_rows(far, cot_ref, base, cs_ref):
    nf, ch, cells = cot_ref.shape
    rows = cs_ref.shape[0] // TAPS
    block = rows // 2
    me = lax.axis_index("dp")
    z, core = me // 2, me % 2
    a = lax.broadcasted_iota(jnp.int32, (rows, ch), 0)
    o = lax.broadcasted_iota(jnp.int32, (rows, ch), 1)
    near = z ^ 1 if far else z
    layer = jnp.where(a < block, near, near ^ 2)
    want = (2 * layer + core) * block + jnp.where(a < block, a, a - block)
    pick = (o == want).astype(F32).astype(BF16)
    row, col = cell_masks(rows, cells)
    for f in range(nf):
        chosen = jnp.dot(pick, cot_ref[f], preferred_element_type=F32)
        at = (base + f) * cells
        for t in range(TAPS):
            ky, kx = divmod(t, 3)
            cs_ref[t * rows : (t + 1) * rows, at : at + cells] = moved(chosen, 1, row, col, ky, kx).astype(BF16)


def frames_in_a_row(x_ref, base, xs_ref):
    nf, _, cells = x_ref.shape
    for f in range(nf):
        xs_ref[:, (base + f) * cells : (base + f + 1) * cells] = x_ref[f]


def first_send_kernel(width, cot_hbm, cot2_hbm, x_hbm, x2_hbm, send_ref, cs_ref, xs_ref, v_ref, f_ref, sem):
    nf = cot_hbm.shape[0]
    loads = [
        pltpu.make_async_copy(src, v_ref.at[k], sem.at[k])
        for k, src in enumerate((cot_hbm, cot2_hbm, x_hbm, x2_hbm))
    ]
    for c in loads:
        c.start()
    for k in range(2):
        loads[k].wait()
        shifted_rows(True, v_ref.at[k], k * nf, cs_ref)
    for k in range(2):
        loads[2 + k].wait()
        frames_in_a_row(v_ref.at[2 + k], k * nf, xs_ref)
    weight_sums(width, cs_ref, xs_ref, f_ref)
    put_rows_coded(send_ref, (0,), f_ref[0], width)


def first_keep_kernel(width, cot_ref, cot2_ref, xs_ref, keep_ref, cs_ref):
    nf = cot_ref.shape[0]
    shifted_rows(False, cot_ref, 0, cs_ref)
    shifted_rows(False, cot2_ref, nf, cs_ref)
    weight_sums(width, cs_ref, xs_ref, keep_ref)


def later_send_kernel(width, cs_ref, x_ref, x2_ref, send_ref, xs_ref, f_ref):
    frames_in_a_row(x_ref, 0, xs_ref)
    frames_in_a_row(x2_ref, x_ref.shape[0], xs_ref)
    weight_sums(width, cs_ref, xs_ref, f_ref)
    put_rows_coded(send_ref, (0,), f_ref[0], width)


def later_keep_kernel(width, cs_ref, *refs):
    if len(refs) == 2:
        xs_ref, keep_ref = refs
        weight_sums(width, cs_ref, xs_ref, keep_ref)
    else:
        x0_ref, x1_ref, keep0_ref, keep1_ref, xs_ref, f_ref = refs
        ch = x0_ref.shape[0]
        xs_ref[:ch] = x0_ref[...]
        xs_ref[ch:] = x1_ref[...]
        weight_sums(width, cs_ref, xs_ref, f_ref)
        keep0_ref[0] = f_ref[0]
        keep1_ref[0] = f_ref[1]


def second_weight_kernel(width, keep_ref, recv_ref, send_ref, keep2_ref):
    pieces, rows, padded = keep_ref.shape
    half = rows // 2
    for p in range(pieces):
        total = keep_ref[p] + take_rows_coded(recv_ref[p], width)
        keep2_ref[p] = total[:half]
        lane = lax.broadcasted_iota(jnp.int32, (half, padded), 1)
        far = jnp.where(lane < width, total[half:], 0.0)
        s = scale_of(jnp.max(jnp.abs(far), axis=1, keepdims=True))
        codes = jnp.where(lane < width, encode(far, s), s)
        if pieces == 1:
            left = send_ref.shape[1]
            fill = jnp.broadcast_to(s, (half, 2 * left - padded))
            right = jnp.concatenate([codes[:, left:], fill], axis=1)
            send_ref[...] = jnp.concatenate([codes[:, :left], right], axis=0).astype(BF16)
        else:
            f = codes
            if p == 0:
                held = f
            else:
                send_ref[...] = jnp.concatenate([held, f], axis=0).astype(BF16)


def last_weight_kernel(width, side, *refs):
    ka, ra, kb, rb = refs[:4]
    out_hbm, acc, stage, sem = refs[-4:]
    blk = lax.axis_index("blk")
    half = ka.shape[1]
    padded = ka.shape[2]
    ch = width // TAPS
    for jj, (k, r) in enumerate(((ka, ra), (kb, rb))):
        left = r.shape[1]
        code = r[...].astype(F32)
        code = jnp.concatenate([code[:half], code[half:, : padded - left]], axis=1)
        acc[(blk % 2) ^ jj] = k[0] + take_rows_coded(code, width)
    start = pl.multiple_of((blk ^ side) // 2 * (2 * ch), 128)
    copies = []
    for t in range(TAPS):
        for q in range(2):
            stage[t, :, q * ch : (q + 1) * ch] = acc[q, :, t * ch : (t + 1) * ch]
        copies.append(
            pltpu.make_async_copy(
                stage.at[t], out_hbm.at[:, pl.ds(pl.multiple_of(t * 4 * ch + start, 128), 2 * ch)], sem.at[t]
            )
        )
        copies[-1].start()
    for c in copies:
        c.wait()


def put_columns_coded(send_ref, lead, left, right):
    ch, cells = left.shape
    scales = []
    for k, v in enumerate((left, right)):
        s = scale_of(jnp.max(jnp.abs(v), axis=0, keepdims=True))
        send_ref[lead + (slice(k * ch, (k + 1) * ch),)] = encode(v, s).astype(BF16)
        scales.append(jnp.broadcast_to(s, (8, cells)))
    send_ref[lead + (slice(2 * ch, 2 * ch + 16),)] = jnp.concatenate(scales, axis=0).astype(BF16)


def take_columns_coded(ref, lead, ch):
    scales = ref[lead + (slice(2 * ch, 2 * ch + 16),)].astype(F32)
    return [
        decode(ref[lead + (slice(k * ch, (k + 1) * ch),)], scales[8 * k : 8 * k + 1]) for k in range(2)
    ]


def load_taps(w_hbm, w_ref, sem, rows, all_ch):
    copies = [
        pltpu.make_async_copy(
            w_hbm.at[:, pl.ds(t * all_ch, all_ch)], w_ref.at[pl.ds(t * rows, rows)], sem.at[t]
        )
        for t in range(TAPS)
    ]
    for c in copies:
        c.start()
    return copies


def frame_grad_kernel(mask, f0, w_in, cot_hbm, send_ref, keep_ref, *refs):
    w_out = refs[:-4]
    cot_ref, cs_ref, out_ref, sem = refs[-4:]
    _, ch, cells = cot_hbm.shape
    w_ref = w_out[0] if w_out else w_in
    all_ch = w_ref.shape[1]
    load = pltpu.make_async_copy(cot_hbm.at[pl.ds(f0, 2)], cot_ref, sem.at[TAPS])
    load.start()
    copies = load_taps(w_in, w_ref, sem, ch, all_ch) if w_out else []
    row, col = cell_masks(ch, cells)
    load.wait()
    for f in range(2):
        x = cot_ref[f].astype(F32)
        for t in range(TAPS):
            ky, kx = divmod(t, 3)
            cs_ref[t * ch : (t + 1) * ch, f * cells : (f + 1) * cells] = moved(x, 1, row, col, ky, kx).astype(BF16)
    for c in copies:
        c.wait()
    tile = 256
    for i0 in range(0, all_ch, tile):
        out_ref[i0 : i0 + tile, :] = lax.dot_general(
            w_ref[:, i0 : i0 + tile], cs_ref[...], TN, preferred_element_type=F32
        )
    blk = lax.axis_index("blk")

    def block(q, f):
        return out_ref[pl.ds(pl.multiple_of(q * ch, 16), ch), f * cells : (f + 1) * cells]

    for k, q in enumerate((blk ^ mask, blk ^ 3)):
        put_columns_coded(send_ref, (k,), block(q, 0), block(q, 1))
    for k, q in enumerate((blk, blk ^ (3 - mask))):
        for f in range(2):
            keep_ref[k, f * ch : (f + 1) * ch, :] = block(q, f)


def second_frame_kernel(kx, rx, ky, ry, sx, k2x, sy, k2y):
    ch = kx.shape[1] // 2
    for k, r, s, k2 in ((kx, rx, sx, k2x), (ky, ry, sy, k2y)):
        for b in range(2):
            got = take_columns_coded(r, (b,), ch)
            sums = [k[b, f * ch : (f + 1) * ch, :] + got[f] for f in range(2)]
            if b == 0:
                for f in range(2):
                    k2[f * ch : (f + 1) * ch, :] = sums[f]
            else:
                put_columns_coded(s, (), sums[0], sums[1])


def last_frame_kernel(kx, rx, ky, ry, out_ref):
    ch = out_ref.shape[1]
    for h, (k, r) in enumerate(((kx, rx), (ky, ry))):
        got = take_columns_coded(r, (), ch)
        for f in range(2):
            out_ref[2 * h + f] = (k[f * ch : (f + 1) * ch, :] + got[f]).astype(BF16)


def response_kernel(w_ref, bias_ref, x0, x1, x2, x3, out_ref, x_ref, y_ref, sem):
    nf, ch, cells = x0.shape
    f = pl.program_id(0)
    blk = lax.axis_index("blk")

    def load(frame):
        for jj, x in enumerate((x0, x1, x2, x3)):
            at = pl.multiple_of((blk ^ jj) * ch, 16)
            yield pltpu.make_async_copy(x.at[frame], x_ref.at[frame, pl.ds(at, ch)], sem.at[frame, jj])

    @pl.when(f == 0)
    def _():
        for frame in range(nf):
            for c in load(frame):
                c.start()

    for c in load(f):
        c.wait()
    y_ref[...] = jnp.dot(w_ref[...], x_ref[f], preferred_element_type=F32)
    row, col = cell_masks(ch, cells)
    total = jnp.transpose(jnp.broadcast_to(bias_ref[...][None, :], (cells, ch)), (1, 0))
    for t in range(TAPS):
        ky, kx = divmod(t, 3)
        total = total + moved(y_ref[t * ch : (t + 1) * ch, :], -1, row, col, ky, kx)
    out_ref[0] = total.astype(BF16)


def params(mib=20):
    return pltpu.CompilerParams(vmem_limit_bytes=mib * 2**20)


def shape(dims, dtype):
    return jax.ShapeDtypeStruct(dims, dtype)


def swap_core(x):
    return lax.ppermute(x, "dp", [(d, d ^ 1) for d in range(8)])


def swap_layer(x, mask):
    return lax.ppermute(x, "dp", [(d, d ^ (2 * mask)) for d in range(8)])


def swap_block(x, mask):
    return lax.ppermute(x, "blk", [(d, d ^ mask) for d in range(4)])


def run(kernel, name, key, after, args, in_specs, out_shape, out_specs, scratch=(), **more):
    outs = out_shape if isinstance(out_shape, tuple) else (out_shape,)
    specs = out_specs if isinstance(out_specs, tuple) else (out_specs,)
    waits = [] if after is None else [after]
    n = len(waits)
    mark = pl.BlockSpec((8, 128), lambda *_: (0, 0))

    def body(*refs):
        ins = n + len(args)
        refs[ins + len(outs)][...] = jnp.zeros((8, 128), F32)
        kernel(*refs[n : ins + len(outs)], *refs[ins + len(outs) + 1 :])

    *got, token = pl.pallas_call(
        body,
        out_shape=(*outs, shape((8, 128), F32)),
        in_specs=[mark] * n + list(in_specs),
        out_specs=(*specs, mark),
        scratch_shapes=list(scratch),
        compiler_params=params(),
        cost_estimate=pl.CostEstimate(flops=int(COST[key] * RATE), bytes_accessed=1024, transcendentals=0),
        name=name,
        **more,
    )(*waits, *args)
    return (*got, token)


def small_body(frames, weight, bias, cotangent):
    nf, ch, cells = frames.shape
    all_ch = 4 * ch
    rows = ch // 2
    half, quarter = rows // 2, rows // 4
    width = TAPS * ch
    padded = -(-(width + 1) // 128) * 128
    left = -(-(padded // 2) // 128) * 128
    deep = 2 * nf * cells

    sums = shape((1, half, padded), F32)
    code = shape((1, half, padded), BF16)
    row_cs = shape((TAPS * half, deep), BF16)
    row_xs = shape((ch, deep), BF16)

    def first_send(after, *args):
        return run(
            functools.partial(first_send_kernel, width),
            "weight_send",
            "a",
            after,
            args,
            [HBM, ANY, HBM, ANY],
            (code, row_cs, row_xs),
            (VMEM, VMEM, VMEM),
            [
                pltpu.VMEM((4, nf, ch, cells), BF16),
                pltpu.VMEM((1, half, padded), F32),
                pltpu.SemaphoreType.DMA((4,)),
            ],
        )

    def first_keep(after, *args):
        return run(
            functools.partial(first_keep_kernel, width),
            "weight_keep",
            "ka",
            after,
            args,
            [VMEM] * 3,
            (sums, row_cs),
            (VMEM, VMEM),
        )

    def later_send(key, after, *args):
        return run(
            functools.partial(later_send_kernel, width),
            "weight_send",
            key,
            after,
            args,
            [VMEM] * 3,
            (code, row_xs),
            (VMEM, VMEM),
            [pltpu.VMEM((1, half, padded), F32)],
        )

    def later_keep(key, after, *args):
        n = len(args) - 1
        return run(
            functools.partial(later_keep_kernel, width),
            "weight_keep",
            key,
            after,
            args,
            [VMEM] * (n + 1),
            (sums,) * n,
            (VMEM,) * n,
            [pltpu.VMEM((2 * ch, deep), BF16), pltpu.VMEM((2, half, padded), F32)] if n == 2 else [],
        )

    def second(key, after, keep, recv):
        n = keep.shape[0]
        out = (2 * quarter, padded) if n == 2 else (2 * quarter, left)
        return run(
            functools.partial(second_weight_kernel, width),
            "weight_second",
            key,
            after,
            (keep, recv),
            [VMEM] * 2,
            (shape(out, BF16), shape((n, quarter, padded), F32)),
            (VMEM, VMEM),
        )

    def frame_part(key, after, mask, f0, w, rearrange):
        return run(
            functools.partial(frame_grad_kernel, mask, f0),
            "frame_part",
            key,
            after,
            (w, cotangent),
            [ANY if rearrange else VMEM, HBM],
            (shape((2, 2 * ch + 16, cells), BF16), shape((2, 2 * ch, cells), F32))
            + ((shape((TAPS * ch, all_ch), BF16),) if rearrange else ()),
            (VMEM,) * (3 if rearrange else 2),
            [
                pltpu.VMEM((2, ch, cells), BF16),
                pltpu.VMEM((TAPS * ch, 2 * cells), BF16),
                pltpu.VMEM((all_ch, 2 * cells), F32),
                pltpu.SemaphoreType.DMA((TAPS + 1,)),
            ],
        )

    def second_frame(key, after, *args):
        return run(
            second_frame_kernel,
            "frame_second",
            key,
            after,
            args,
            [VMEM] * 4,
            (
                shape((2 * ch + 16, cells), BF16),
                shape((2 * ch, cells), F32),
                shape((2 * ch + 16, cells), BF16),
                shape((2 * ch, cells), F32),
            ),
            (VMEM,) * 4,
        )

    def last_frame(key, after, *args):
        return run(
            last_frame_kernel, "frame_last", key, after, args, [VMEM] * 4, shape((nf, ch, cells), BF16), VMEM
        )

    def respond(key, after, *xs):
        return run(
            response_kernel,
            "response",
            key,
            after,
            (taps, bias, *xs),
            [VMEM, VMEM] + [ANY] * 4,
            shape((nf, ch, cells), BF16),
            pl.BlockSpec((1, ch, cells), lambda f: (f, 0, 0)),
            [
                pltpu.VMEM((nf, all_ch, cells), BF16),
                pltpu.VMEM((TAPS * ch, cells), F32),
                pltpu.SemaphoreType.DMA((nf, 4)),
            ],
            grid=(nf,),
        )

    def last_weight(key, after, side, parts, held):
        more = {} if held is None else {"input_output_aliases": {5: 0}}
        return run(
            functools.partial(last_weight_kernel, width, side),
            "weight_last",
            key,
            after,
            (*parts,) if held is None else (*parts, held),
            [VMEM] * 4 + ([] if held is None else [HBM]),
            shape((quarter, TAPS * all_ch), F32),
            HBM,
            [
                pltpu.VMEM((2, quarter, padded), F32),
                pltpu.VMEM((TAPS, quarter, 2 * ch), F32),
                pltpu.SemaphoreType.DMA((TAPS,)),
            ],
            **more,
        )

    cot2 = swap_core(cotangent)
    own2 = swap_core(frames)
    near_x = swap_block(frames, 1)
    near_y = swap_block(frames, 2)
    near_x2 = swap_core(near_x)
    near_y2 = swap_core(near_y)

    t = taps = None
    send, keep, recv, xs = {}, {}, {}, {}
    fsend, fkeep, frecv = {}, {}, {}
    diag = swap_block(near_x, 2)
    near = {"b": (near_x, near_x2), "c": (near_y, near_y2), "d": (diag, swap_core(diag))}
    for step in ORDER:
        if step == "a":
            send["a"], cs_far, xs["a"], t = first_send(t, cotangent, cot2, frames, own2)
            recv["a"] = swap_layer(send["a"], 1)
        elif step in ("b", "c", "d"):
            send[step], xs[step], t = later_send(step, t, cs_far, *near[step])
            recv[step] = swap_layer(send[step], 1)
        elif step == "ka":
            keep["a"], cs_near, t = first_keep(t, cotangent, cot2, xs["a"])
        elif step == "kb":
            keep["b"], keep["c"], t = later_keep(step, t, cs_near, xs["b"], xs["c"])
        elif step == "kd":
            keep["d"], t = later_keep(step, t, cs_near, xs["d"])
        elif step in ("a2", "b2", "c2", "d2"):
            k = step[0]
            send[step], keep[step], t = second(step, t, keep[k], recv[k])
            recv[step] = swap_layer(send[step], 2)
        elif step in ("fx", "fy"):
            k = 1 if step == "fx" else 2
            if taps is None:
                fsend[k], fkeep[k], taps, t = frame_part(step, t, k, 2 * k - 2, weight, True)
            else:
                fsend[k], fkeep[k], t = frame_part(step, t, k, 2 * k - 2, taps, False)
            frecv[k] = swap_block(fsend[k], k)
        elif step == "f2":
            sx, fkeep[3], sy, fkeep[4], t = second_frame(step, t, fkeep[1], frecv[1], fkeep[2], frecv[2])
            frecv[3] = swap_block(sx, 2)
            frecv[4] = swap_block(sy, 1)
        elif step == "fl":
            frame_grad, t = last_frame(step, t, fkeep[3], frecv[3], fkeep[4], frecv[4])
        elif step == "resp":
            response, t = respond(step, t, frames, near_x, near_y, diag)
        elif step == "wab":
            held, t = last_weight(step, t, 0, (keep["a2"], recv["a2"], keep["b2"], recv["b2"]), None)
        else:
            weight_grad, t = last_weight(step, t, 2, (keep["c2"], recv["c2"], keep["d2"], recv["d2"]), held)
    return (response, frame_grad, weight_grad)


def solution(mesh):
    small = mesh.shape["dp"] == 8 and mesh.shape["blk"] == 4
    return jax.shard_map(
        small_body if small else general_body,
        mesh=mesh,
        in_specs=(P("dp", "blk", None), P("blk", None), P("blk"), P("dp", "blk", None)),
        out_specs=(P("dp", "blk", None), P("dp", "blk", None), P(("blk", "dp"), None)),
        check_vma=False,
    )
```

profile of v0, /device:TPU:0, one launch (start us, length us, event | category | flops | bytes accessed | tf_op | source)
XLA Modules:
  0.0 104.0 jit_solution(10589519249841419207)
XLA Ops:
  0.6 0.5 collective-permute-start
  1.1 0.1 collective-permute-start.1
  1.2 2.9 %collective-permute-start.3 = (bf16[4,320,256]{2,1,0:T(8,128)(2,1)}, bf16[4,320,256]{2,1,0:T(8,128)(2,1)}, u32[]{:S(2)}, u32[]{:S(2)}) collective-permute-start(bf16[4,320,256]{2,1,0:T(8,128)(2,1)} %refs_3_.1), channel_id=1, source_target_pairs={{0,1},{1,0},{2,3},{3,2},{4,5},{5,4},{6,7},{7,6},{8,9},{9,8},{10,11... | collective-permute-start | bytes 1966088 | tf_op jit(solution)/shard_map/ppermute | solution.py:378
  4.1 1.5 %collective-permute-start.5 = (bf16[4,320,256]{2,1,0:T(8,128)(2,1)}, bf16[4,320,256]{2,1,0:T(8,128)(2,1)}, u32[]{:S(2)}, u32[]{:S(2)}) collective-permute-start(bf16[4,320,256]{2,1,0:T(8,128)(2,1)} %refs_3_.1), channel_id=1, source_target_pairs={{0,2},{1,3},{2,0},{3,1},{4,6},{5,7},{6,4},{7,5},{8,10},{9,11},{10,... | collective-permute-start | bytes 1966088 | tf_op jit(solution)/shard_map/ppermute | solution.py:378
  5.7 0.0 collective-permute-done.refs_1_.refs_2_
  5.7 0.0 collective-permute-done.1.refs_3_
  5.7 1.1 %copy-done.1 = bf16[4,320,256]{2,1,0:T(8,128)(2,1)S(1)} copy-done((bf16[4,320,256]{2,1,0:T(8,128)(2,1)S(1)}, bf16[4,320,256]{2,1,0:T(8,128)(2,1)}, u32[]{:S(2)}) %copy-start.1) | copy-done | bytes 655384
  6.8 1.1 %copy-done.3 = bf16[4,320,256]{2,1,0:T(8,128)(2,1)S(1)} copy-done((bf16[4,320,256]{2,1,0:T(8,128)(2,1)S(1)}, bf16[4,320,256]{2,1,0:T(8,128)(2,1)}, u32[]{:S(2)}) %copy-start.3) | copy-done | bytes 655384
  7.8 4.3 %weight_send.4 = (bf16[1,80,2944]{2,1,0:T(8,128)(2,1)S(1)}, bf16[720,2048]{1,0:T(8,128)(2,1)S(1)}, bf16[320,2048]{1,0:T(8,128)(2,1)S(1)}, f32[8,128]{1,0:T(8,128)S(1)}) custom-call(bf16[4,320,256]{2,1,0:T(8,128)(2,1)S(1)} %copy-done.1, bf16[4,320,256]{2,1,0:T(8,128)(2,1)S(1)} %collective-permute-done.refs_1_.refs_2_, bf16[4,320,256]{2,1,0:T(8,128)(2,1)S(1)} %copy-done.3, ...), custom_call_target="tpu_custom_call" | custom-call | flops 44999999488 | bytes 1024 | tf_op jit(solution)/shard_map/weight_send/pallas_call | solution.py:393
  12.2 1.6 %collective-permute-start.2 = (bf16[1,80,2944]{2,1,0:T(8,128)(2,1)S(1)}, bf16[1,80,2944]{2,1,0:T(8,128)(2,1)S(1)}, u32[]{:S(2)}, u32[]{:S(2)}) collective-permute-start(bf16[1,80,2944]{2,1,0:T(8,128)(2,1)S(1)} %get-tuple-element.60), channel_id=1, source_target_pairs={{0,8},{4,12},{8,0},{12,4},{16,24},{20,28},{24,16},{28,20},{1,9},{5... | collective-permute-start | bytes 1413128 | tf_op jit(solution)/shard_map/ppermute | solution.py:374
  13.8 2.1 %weight_keep.3 = (f32[1,80,2944]{2,1,0:T(8,128)S(1)}, bf16[720,2048]{1,0:T(8,128)(2,1)S(1)}, f32[8,128]{1,0:T(8,128)S(1)}) custom-call(f32[8,128]{1,0:T(8,128)S(1)} %get-tuple-element.55.refs_0_, bf16[4,320,256]{2,1,0:T(8,128)(2,1)S(1)} %copy-done.1, bf16[4,320,256]{2,1,0:T(8,128)(2,1)S(1)} %collective-permute-done.refs_1_.refs_2_, ...), custom_call_target="tpu_custom_call" | custom-call | flops 40000000000 | bytes 1024 | tf_op jit(solution)/shard_map/weight_keep/pallas_call | solution.py:393
  16.0 0.9 copy-done
  16.9 7.3 %frame_part.2 = (bf16[2,656,256]{2,1,0:T(8,128)(2,1)}, f32[2,640,256]{2,1,0:T(8,128)S(1)}, bf16[2880,1280]{1,0:T(8,128)(2,1)S(1)}, f32[8,128]{1,0:T(8,128)S(1)}) custom-call(f32[8,128]{1,0:T(8,128)S(1)} %get-tuple-element.57.refs_0_, bf16[320,11520]{1,0:T(8,128)(2,1)S(1)} %copy-done, bf16[4,320,256]{2,1,0:T(8,128)(2,1)S(1)} %copy-done.1), custom_call_target="tpu_custom_call" | custom-call | flops 85000003584 | bytes 1024 | tf_op jit(solution)/shard_map/frame_part/pallas_call | solution.py:393
  24.2 1.3 %collective-permute-start.11 = (bf16[2,656,256]{2,1,0:T(8,128)(2,1)}, bf16[2,656,256]{2,1,0:T(8,128)(2,1)}, u32[]{:S(2)}, u32[]{:S(2)}) collective-permute-start(bf16[2,656,256]{2,1,0:T(8,128)(2,1)} %get-tuple-element.83), channel_id=1, source_target_pairs={{0,1},{1,0},{2,3},{3,2},{4,5},{5,4},{6,7},{7,6},{8,9},{9,8},{10,11... | collective-permute-start | bytes 2015240 | tf_op jit(solution)/shard_map/ppermute | solution.py:378
  25.4 0.0 collective-permute-start.4
  25.4 1.5 %collective-permute-start.8 = (bf16[4,320,256]{2,1,0:T(8,128)(2,1)}, bf16[4,320,256]{2,1,0:T(8,128)(2,1)}, u32[]{:S(2)}, u32[]{:S(2)}) collective-permute-start(bf16[4,320,256]{2,1,0:T(8,128)(2,1)} %collective-permute-done.3.refs_2_.refs_4_), channel_id=1, source_target_pairs={{0,2},{1,3},{2,0},{3,1},{4,6},{5,7},{6,4},{7,5},{8,10},{9,11},{10,... | collective-permute-start | bytes 1966088 | tf_op jit(solution)/shard_map/ppermute | solution.py:378
  26.9 0.2 collective-permute-start.6
  27.2 0.0 collective-permute-done.2.refs_2_
  27.2 1.3 %weight_second.4 = (bf16[80,1536]{1,0:T(8,128)(2,1)}, f32[1,40,2944]{2,1,0:T(8,128)S(1)}, f32[8,128]{1,0:T(8,128)S(1)}) custom-call(f32[8,128]{1,0:T(8,128)S(1)} %get-tuple-element.58.refs_0_, f32[1,80,2944]{2,1,0:T(8,128)S(1)} %get-tuple-element.59.refs_1_, bf16[1,80,2944]{2,1,0:T(8,128)(2,1)S(1)} %collective-permute-done.2.refs_2_), custom_call_target="tpu_custom_call" | custom-call | flops 7000000000 | bytes 1024 | tf_op jit(solution)/shard_map/weight_second/pallas_call | solution.py:393
  28.5 2.6 %collective-permute-start.16 = (bf16[80,1536]{1,0:T(8,128)(2,1)}, bf16[80,1536]{1,0:T(8,128)(2,1)}, u32[]{:S(2)}, u32[]{:S(2)}) collective-permute-start(bf16[80,1536]{1,0:T(8,128)(2,1)} %get-tuple-element.97), channel_id=1, source_target_pairs={{0,16},{4,20},{8,24},{12,28},{16,0},{20,4},{24,8},{28,12},{1,17},{... | collective-permute-start | bytes 737288 | tf_op jit(solution)/shard_map/ppermute | solution.py:374
  31.1 0.0 collective-permute-done.4.refs_3_
  31.1 4.0 %weight_send.5 = (bf16[1,80,2944]{2,1,0:T(8,128)(2,1)}, bf16[320,2048]{1,0:T(8,128)(2,1)S(1)}, f32[8,128]{1,0:T(8,128)S(1)}) custom-call(f32[8,128]{1,0:T(8,128)S(1)} %get-tuple-element.61.refs_0_, bf16[720,2048]{1,0:T(8,128)(2,1)S(1)} %get-tuple-element.62.refs_1_, bf16[4,320,256]{2,1,0:T(8,128)(2,1)} %collective-permute-done.3.refs_2_.refs_4_, ...), custom_call_target="tpu_custom_call" | custom-call | flops 40000000000 | bytes 1024 | tf_op jit(solution)/shard_map/weight_send/pallas_call | solution.py:393
  35.1 0.5 collective-permute-start.7
  35.5 0.0 collective-permute-done.6.refs_3_
  35.5 4.0 %weight_send.6 = (bf16[1,80,2944]{2,1,0:T(8,128)(2,1)}, bf16[320,2048]{1,0:T(8,128)(2,1)S(1)}, f32[8,128]{1,0:T(8,128)S(1)}) custom-call(f32[8,128]{1,0:T(8,128)S(1)} %get-tuple-element.63.refs_0_, bf16[720,2048]{1,0:T(8,128)(2,1)S(1)} %get-tuple-element.62.refs_1_, bf16[4,320,256]{2,1,0:T(8,128)(2,1)} %collective-permute-done.5.refs_2_.refs_5_, ...), custom_call_target="tpu_custom_call" | custom-call | flops 40000000000 | bytes 1024 | tf_op jit(solution)/shard_map/weight_send/pallas_call | solution.py:393
  39.6 1.6 %collective-permute-start.10 = (bf16[1,80,2944]{2,1,0:T(8,128)(2,1)}, bf16[1,80,2944]{2,1,0:T(8,128)(2,1)}, u32[]{:S(2)}, u32[]{:S(2)}) collective-permute-start(bf16[1,80,2944]{2,1,0:T(8,128)(2,1)} %get-tuple-element.78), channel_id=1, source_target_pairs={{0,8},{4,12},{8,0},{12,4},{16,24},{20,28},{24,16},{28,20},{1,9},{5... | collective-permute-start | bytes 1413128 | tf_op jit(solution)/shard_map/ppermute | solution.py:374
  41.1 6.4 %frame_part.3 = (bf16[2,656,256]{2,1,0:T(8,128)(2,1)}, f32[2,640,256]{2,1,0:T(8,128)S(1)}, f32[8,128]{1,0:T(8,128)S(1)}) custom-call(f32[8,128]{1,0:T(8,128)S(1)} %get-tuple-element.64.refs_0_, bf16[2880,1280]{1,0:T(8,128)(2,1)S(1)} %get-tuple-element.65.refs_1_, bf16[4,320,256]{2,1,0:T(8,128)(2,1)S(1)} %copy-done.2), custom_call_target="tpu_custom_call" | custom-call | flops 85000003584 | bytes 1024 | tf_op jit(solution)/shard_map/frame_part/pallas_call | solution.py:393
  47.6 2.6 %weight_keep.4 = (f32[1,80,2944]{2,1,0:T(8,128)S(1)}, f32[1,80,2944]{2,1,0:T(8,128)S(1)}, f32[8,128]{1,0:T(8,128)S(1)}) custom-call(f32[8,128]{1,0:T(8,128)S(1)} %get-tuple-element.66.refs_0_, bf16[720,2048]{1,0:T(8,128)(2,1)S(1)} %get-tuple-element.67.refs_1_, bf16[320,2048]{1,0:T(8,128)(2,1)S(1)} %get-tuple-element.68.refs_2_, ...), custom_call_target="tpu_custom_call" | custom-call | flops 49999998976 | bytes 1024 | tf_op jit(solution)/shard_map/weight_keep/pallas_call | solution.py:393
  50.2 0.0 collective-permute-done.8.refs_2_.refs_6_
  50.2 0.6 collective-permute-start.12
  50.8 2.4 %collective-permute-done.7.refs_2_ = bf16[1,80,2944]{2,1,0:T(8,128)(2,1)} collective-permute-done((bf16[1,80,2944]{2,1,0:T(8,128)(2,1)}, bf16[1,80,2944]{2,1,0:T(8,128)(2,1)}, u32[]{:S(2)}, u32[]{:S(2)}) %collective-permute-start.7) | collective-permute-done | bytes 471072 | tf_op jit(solution)/shard_map/ppermute | solution.py:374
  53.2 2.3 %weight_second.5 = (bf16[80,1536]{1,0:T(8,128)(2,1)}, f32[1,40,2944]{2,1,0:T(8,128)S(1)}, f32[8,128]{1,0:T(8,128)S(1)}) custom-call(f32[8,128]{1,0:T(8,128)S(1)} %get-tuple-element.70.refs_0_, f32[1,80,2944]{2,1,0:T(8,128)S(1)} %get-tuple-element.71.refs_1_, bf16[1,80,2944]{2,1,0:T(8,128)(2,1)} %collective-permute-done.7.refs_2_), custom_call_target="tpu_custom_call" | custom-call | flops 7000000000 | bytes 1024 | tf_op jit(solution)/shard_map/weight_second/pallas_call | solution.py:393
  55.5 3.2 %weight_send.7 = (bf16[1,80,2944]{2,1,0:T(8,128)(2,1)S(1)}, bf16[320,2048]{1,0:T(8,128)(2,1)S(1)}, f32[8,128]{1,0:T(8,128)S(1)}) custom-call(f32[8,128]{1,0:T(8,128)S(1)} %get-tuple-element.73.refs_0_, bf16[720,2048]{1,0:T(8,128)(2,1)S(1)} %get-tuple-element.62.refs_1_, bf16[4,320,256]{2,1,0:T(8,128)(2,1)} %collective-permute-done.8.refs_2_.refs_6_, ...), custom_call_target="tpu_custom_call" | custom-call | flops 40000000000 | bytes 1024 | tf_op jit(solution)/shard_map/weight_send/pallas_call | solution.py:393
  58.7 1.8 %weight_keep.5 = (f32[1,80,2944]{2,1,0:T(8,128)S(1)}, f32[8,128]{1,0:T(8,128)S(1)}) custom-call(f32[8,128]{1,0:T(8,128)S(1)} %get-tuple-element.74.refs_0_, bf16[720,2048]{1,0:T(8,128)(2,1)S(1)} %get-tuple-element.67.refs_1_, bf16[320,2048]{1,0:T(8,128)(2,1)S(1)} %get-tuple-element.75.refs_2_), custom_call_target="tpu_custom_call" | custom-call | flops 40000000000 | bytes 1024 | tf_op jit(solution)/shard_map/weight_keep/pallas_call | solution.py:393
  60.5 2.8 %collective-permute-done.10.refs_2_ = bf16[1,80,2944]{2,1,0:T(8,128)(2,1)} collective-permute-done((bf16[1,80,2944]{2,1,0:T(8,128)(2,1)}, bf16[1,80,2944]{2,1,0:T(8,128)(2,1)}, u32[]{:S(2)}, u32[]{:S(2)}) %collective-permute-start.10) | collective-permute-done | bytes 471072 | tf_op jit(solution)/shard_map/ppermute | solution.py:374
  63.3 1.7 %weight_second.6 = (bf16[80,1536]{1,0:T(8,128)(2,1)S(1)}, f32[1,40,2944]{2,1,0:T(8,128)S(1)}, f32[8,128]{1,0:T(8,128)S(1)}) custom-call(f32[8,128]{1,0:T(8,128)S(1)} %get-tuple-element.76.refs_0_, f32[1,80,2944]{2,1,0:T(8,128)S(1)} %get-tuple-element.77.refs_1_, bf16[1,80,2944]{2,1,0:T(8,128)(2,1)} %collective-permute-done.10.refs_2_), custom_call_target="tpu_custom_call" | custom-call | flops 7000000000 | bytes 1024 | tf_op jit(solution)/shard_map/weight_second/pallas_call | solution.py:393
  65.1 11.1 %response.1 = (bf16[4,320,256]{2,1,0:T(8,128)(2,1)}, f32[8,128]{1,0:T(8,128)S(1)}) custom-call(f32[8,128]{1,0:T(8,128)S(1)} %get-tuple-element.79.refs_0_, bf16[2880,1280]{1,0:T(8,128)(2,1)S(1)} %get-tuple-element.65.refs_1_, f32[320]{0:T(512)S(1)} %copy-done.5, bf16[4,320,256]{2,1,0:T(8,128)(2,1)S(1)} %copy-done.4, ...), custom_call_target="tpu_custom_call" | custom-call | flops 109999996928 | bytes 1024 | tf_op jit(solution)/shard_map/response/pallas_call | solution.py:393
  76.2 1.5 %collective-permute-start.18 = (bf16[80,1536]{1,0:T(8,128)(2,1)S(1)}, bf16[80,1536]{1,0:T(8,128)(2,1)S(1)}, u32[]{:S(2)}, u32[]{:S(2)}) collective-permute-start(bf16[80,1536]{1,0:T(8,128)(2,1)S(1)} %get-tuple-element.102), channel_id=1, source_target_pairs={{0,16},{4,20},{8,24},{12,28},{16,0},{20,4},{24,8},{28,12},{1,17},{... | collective-permute-start | bytes 737288 | tf_op jit(solution)/shard_map/ppermute | solution.py:374
  77.7 2.7 %frame_second.1 = (bf16[656,256]{1,0:T(8,128)(2,1)S(1)}, f32[640,256]{1,0:T(8,128)S(1)}, bf16[656,256]{1,0:T(8,128)(2,1)S(1)}, f32[640,256]{1,0:T(8,128)S(1)}, f32[8,128]{1,0:T(8,128)S(1)}) custom-call(f32[8,128]{1,0:T(8,128)S(1)} %get-tuple-element.81.refs_0_, f32[2,640,256]{2,1,0:T(8,128)S(1)} %get-tuple-element.82.refs_1_, ...), custom_call_target="tpu_custom_call" | custom-call | flops 15000000512 | bytes 1024 | tf_op jit(solution)/shard_map/frame_second/pallas_call | solution.py:393
  80.3 0.6 collective-permute-start.14
  81.0 0.4 collective-permute-start.15
  81.3 0.6 weight_second.7
  82.0 7.0 %collective-permute-done.14.refs_2_ = bf16[656,256]{1,0:T(8,128)(2,1)S(1)} collective-permute-done((bf16[656,256]{1,0:T(8,128)(2,1)S(1)}, bf16[656,256]{1,0:T(8,128)(2,1)S(1)}, u32[]{:S(2)}, u32[]{:S(2)}) %collective-permute-start.14) | collective-permute-done | bytes 335904 | tf_op jit(solution)/shard_map/ppermute | solution.py:378
  89.0 2.5 %collective-permute-start.19 = (bf16[80,1536]{1,0:T(8,128)(2,1)S(1)}, bf16[80,1536]{1,0:T(8,128)(2,1)S(1)}, u32[]{:S(2)}, u32[]{:S(2)}) collective-permute-start(bf16[80,1536]{1,0:T(8,128)(2,1)S(1)} %get-tuple-element.104), channel_id=1, source_target_pairs={{0,16},{4,20},{8,24},{12,28},{16,0},{20,4},{24,8},{28,12},{1,17},{... | collective-permute-start | bytes 737288 | tf_op jit(solution)/shard_map/ppermute | solution.py:374
  91.5 1.3 %frame_last.1 = (bf16[4,320,256]{2,1,0:T(8,128)(2,1)}, f32[8,128]{1,0:T(8,128)S(1)}) custom-call(f32[8,128]{1,0:T(8,128)S(1)} %get-tuple-element.89.refs_0_, f32[640,256]{1,0:T(8,128)S(1)} %get-tuple-element.90.refs_1_, bf16[656,256]{1,0:T(8,128)(2,1)S(1)} %collective-permute-done.14.refs_2_, f32[640,256]{1,0:T(8,128)S(1)} %get-tuple-element.92.refs_3_, ...), custom_call_target="tpu_custom_call" | custom-call | flops 12000000000 | bytes 1024 | tf_op jit(solution)/shard_map/frame_last/pallas_call | solution.py:393
  92.7 2.5 %weight_last.2 = (f32[40,11520]{1,0:T(8,128)}, f32[8,128]{1,0:T(8,128)S(1)}) custom-call(f32[8,128]{1,0:T(8,128)S(1)} %get-tuple-element.95.refs_0_, f32[1,40,2944]{2,1,0:T(8,128)S(1)} %get-tuple-element.96.refs_1_, bf16[80,1536]{1,0:T(8,128)(2,1)} %collective-permute-done.16.refs_2_, f32[1,40,2944]{2,1,0:T(8,128)S(1)} %get-tuple-element.98.refs_3_, ...), custom_call_target="tpu_custom_call" | custom-call | flops 24000000000 | bytes 1024 | tf_op jit(solution)/shard_map/weight_last/pallas_call | solution.py:393
  95.3 6.4 %collective-permute-done.19.refs_4_ = bf16[80,1536]{1,0:T(8,128)(2,1)S(1)} collective-permute-done((bf16[80,1536]{1,0:T(8,128)(2,1)S(1)}, bf16[80,1536]{1,0:T(8,128)(2,1)S(1)}, u32[]{:S(2)}, u32[]{:S(2)}) %collective-permute-start.19) | collective-permute-done | bytes 245792 | tf_op jit(solution)/shard_map/ppermute | solution.py:374
  101.7 2.1 %weight_last.3 = (f32[40,11520]{1,0:T(8,128)}, f32[8,128]{1,0:T(8,128)}) custom-call(f32[8,128]{1,0:T(8,128)S(1)} %get-tuple-element.100.refs_0_, f32[1,40,2944]{2,1,0:T(8,128)S(1)} %get-tuple-element.101.refs_1_, bf16[80,1536]{1,0:T(8,128)(2,1)S(1)} %collective-permute-done.18.refs_2_, ...), custom_call_target="tpu_custom_call", output_to_operand_aliasing={{0}: (5, {})} | custom-call | flops 24000000000 | bytes 1024 | tf_op jit(solution)/shard_map/weight_last/pallas_call | solution.py:393
  (22 shorter events, 0.0 us)
Async XLA Ops:
  0.6 5.0 %collective-permute-start = (bf16[4,320,256]{2,1,0:T(8,128)(2,1)}, bf16[4,320,256]{2,1,0:T(8,128)(2,1)S(1)}, u32[]{:S(2)}, u32[]{:S(2)}) collective-permute-start(bf16[4,320,256]{2,1,0:T(8,128)(2,1)} %refs_2_.6), channel_id=1, source_target_pairs={{0,4},{4,0},{8,12},{12,8},{16,20},{20,16},{24,28},{28,24},{1,5},{5... | collective-permute-start | bytes 1966088 | tf_op jit(solution)/shard_map/ppermute | solution.py:370
  1.1 4.5 %collective-permute-start.1 = (bf16[4,320,256]{2,1,0:T(8,128)(2,1)}, bf16[4,320,256]{2,1,0:T(8,128)(2,1)S(1)}, u32[]{:S(2)}, u32[]{:S(2)}) collective-permute-start(bf16[4,320,256]{2,1,0:T(8,128)(2,1)} %refs_3_.1), channel_id=1, source_target_pairs={{0,4},{4,0},{8,12},{12,8},{16,20},{20,16},{24,28},{28,24},{1,5},{5... | collective-permute-start | bytes 1966088 | tf_op jit(solution)/shard_map/ppermute | solution.py:370
  1.2 24.2 %collective-permute-start.3 = (bf16[4,320,256]{2,1,0:T(8,128)(2,1)}, bf16[4,320,256]{2,1,0:T(8,128)(2,1)}, u32[]{:S(2)}, u32[]{:S(2)}) collective-permute-start(bf16[4,320,256]{2,1,0:T(8,128)(2,1)} %refs_3_.1), channel_id=1, source_target_pairs={{0,1},{1,0},{2,3},{3,2},{4,5},{5,4},{6,7},{7,6},{8,9},{9,8},{10,11... | collective-permute-start | bytes 1966088 | tf_op jit(solution)/shard_map/ppermute | solution.py:378
  4.1 22.8 %collective-permute-start.5 = (bf16[4,320,256]{2,1,0:T(8,128)(2,1)}, bf16[4,320,256]{2,1,0:T(8,128)(2,1)}, u32[]{:S(2)}, u32[]{:S(2)}) collective-permute-start(bf16[4,320,256]{2,1,0:T(8,128)(2,1)} %refs_3_.1), channel_id=1, source_target_pairs={{0,2},{1,3},{2,0},{3,1},{4,6},{5,7},{6,4},{7,5},{8,10},{9,11},{10,... | collective-permute-start | bytes 1966088 | tf_op jit(solution)/shard_map/ppermute | solution.py:378
  5.7 1.1 %copy-start.1 = (bf16[4,320,256]{2,1,0:T(8,128)(2,1)S(1)}, bf16[4,320,256]{2,1,0:T(8,128)(2,1)}, u32[]{:S(2)}) copy-start(bf16[4,320,256]{2,1,0:T(8,128)(2,1)} %refs_2_.6) | copy-start | bytes 1966084
  6.8 1.1 %copy-start.3 = (bf16[4,320,256]{2,1,0:T(8,128)(2,1)S(1)}, bf16[4,320,256]{2,1,0:T(8,128)(2,1)}, u32[]{:S(2)}) copy-start(bf16[4,320,256]{2,1,0:T(8,128)(2,1)} %refs_3_.1) | copy-start | bytes 1966084
  12.2 15.0 %collective-permute-start.2 = (bf16[1,80,2944]{2,1,0:T(8,128)(2,1)S(1)}, bf16[1,80,2944]{2,1,0:T(8,128)(2,1)S(1)}, u32[]{:S(2)}, u32[]{:S(2)}) collective-permute-start(bf16[1,80,2944]{2,1,0:T(8,128)(2,1)S(1)} %get-tuple-element.60), channel_id=1, source_target_pairs={{0,8},{4,12},{8,0},{12,4},{16,24},{20,28},{24,16},{28,20},{1,9},{5... | collective-permute-start | bytes 1413128 | tf_op jit(solution)/shard_map/ppermute | solution.py:374
  13.8 3.1 %copy-start = (bf16[320,11520]{1,0:T(8,128)(2,1)S(1)}, bf16[320,11520]{1,0:T(8,128)(2,1)}, u32[]{:S(2)}) copy-start(bf16[320,11520]{1,0:T(8,128)(2,1)} %refs_1_.3) | copy-start | bytes 22118404
  24.2 52.1 %collective-permute-start.11 = (bf16[2,656,256]{2,1,0:T(8,128)(2,1)}, bf16[2,656,256]{2,1,0:T(8,128)(2,1)}, u32[]{:S(2)}, u32[]{:S(2)}) collective-permute-start(bf16[2,656,256]{2,1,0:T(8,128)(2,1)} %get-tuple-element.83), channel_id=1, source_target_pairs={{0,1},{1,0},{2,3},{3,2},{4,5},{5,4},{6,7},{7,6},{8,9},{9,8},{10,11... | collective-permute-start | bytes 2015240 | tf_op jit(solution)/shard_map/ppermute | solution.py:378
  25.4 5.7 %collective-permute-start.4 = (bf16[4,320,256]{2,1,0:T(8,128)(2,1)}, bf16[4,320,256]{2,1,0:T(8,128)(2,1)S(1)}, u32[]{:S(2)}, u32[]{:S(2)}) collective-permute-start(bf16[4,320,256]{2,1,0:T(8,128)(2,1)} %collective-permute-done.3.refs_2_.refs_4_), channel_id=1, source_target_pairs={{0,4},{4,0},{8,12},{12,8},{16,20},{20,16},{24,28},{28,24},{1,5},{5... | collective-permute-start | bytes 1966088 | tf_op jit(solution)/shard_map/ppermute | solution.py:370
  25.4 24.8 %collective-permute-start.8 = (bf16[4,320,256]{2,1,0:T(8,128)(2,1)}, bf16[4,320,256]{2,1,0:T(8,128)(2,1)}, u32[]{:S(2)}, u32[]{:S(2)}) collective-permute-start(bf16[4,320,256]{2,1,0:T(8,128)(2,1)} %collective-permute-done.3.refs_2_.refs_4_), channel_id=1, source_target_pairs={{0,2},{1,3},{2,0},{3,1},{4,6},{5,7},{6,4},{7,5},{8,10},{9,11},{10,... | collective-permute-start | bytes 1966088 | tf_op jit(solution)/shard_map/ppermute | solution.py:378
  26.9 8.6 %collective-permute-start.6 = (bf16[4,320,256]{2,1,0:T(8,128)(2,1)}, bf16[4,320,256]{2,1,0:T(8,128)(2,1)S(1)}, u32[]{:S(2)}, u32[]{:S(2)}) collective-permute-start(bf16[4,320,256]{2,1,0:T(8,128)(2,1)} %collective-permute-done.5.refs_2_.refs_5_), channel_id=1, source_target_pairs={{0,4},{4,0},{8,12},{12,8},{16,20},{20,16},{24,28},{28,24},{1,5},{5... | collective-permute-start | bytes 1966088 | tf_op jit(solution)/shard_map/ppermute | solution.py:370
  28.5 64.2 %collective-permute-start.16 = (bf16[80,1536]{1,0:T(8,128)(2,1)}, bf16[80,1536]{1,0:T(8,128)(2,1)}, u32[]{:S(2)}, u32[]{:S(2)}) collective-permute-start(bf16[80,1536]{1,0:T(8,128)(2,1)} %get-tuple-element.97), channel_id=1, source_target_pairs={{0,16},{4,20},{8,24},{12,28},{16,0},{20,4},{24,8},{28,12},{1,17},{... | collective-permute-start | bytes 737288 | tf_op jit(solution)/shard_map/ppermute | solution.py:374
  35.1 18.1 %collective-permute-start.7 = (bf16[1,80,2944]{2,1,0:T(8,128)(2,1)}, bf16[1,80,2944]{2,1,0:T(8,128)(2,1)}, u32[]{:S(2)}, u32[]{:S(2)}) collective-permute-start(bf16[1,80,2944]{2,1,0:T(8,128)(2,1)} %get-tuple-element.72), channel_id=1, source_target_pairs={{0,8},{4,12},{8,0},{12,4},{16,24},{20,28},{24,16},{28,20},{1,9},{5... | collective-permute-start | bytes 1413128 | tf_op jit(solution)/shard_map/ppermute | solution.py:374
  35.5 5.6 %copy-start.2 = (bf16[4,320,256]{2,1,0:T(8,128)(2,1)S(1)}, bf16[4,320,256]{2,1,0:T(8,128)(2,1)}, u32[]{:S(2)}) copy-start(bf16[4,320,256]{2,1,0:T(8,128)(2,1)} %refs_2_.6) | copy-start | bytes 1966084
  39.6 23.7 %collective-permute-start.10 = (bf16[1,80,2944]{2,1,0:T(8,128)(2,1)}, bf16[1,80,2944]{2,1,0:T(8,128)(2,1)}, u32[]{:S(2)}, u32[]{:S(2)}) collective-permute-start(bf16[1,80,2944]{2,1,0:T(8,128)(2,1)} %get-tuple-element.78), channel_id=1, source_target_pairs={{0,8},{4,12},{8,0},{12,4},{16,24},{20,28},{24,16},{28,20},{1,9},{5... | collective-permute-start | bytes 1413128 | tf_op jit(solution)/shard_map/ppermute | solution.py:374
  50.2 27.5 %collective-permute-start.12 = (bf16[2,656,256]{2,1,0:T(8,128)(2,1)}, bf16[2,656,256]{2,1,0:T(8,128)(2,1)}, u32[]{:S(2)}, u32[]{:S(2)}) collective-permute-start(bf16[2,656,256]{2,1,0:T(8,128)(2,1)} %get-tuple-element.85), channel_id=1, source_target_pairs={{0,2},{1,3},{2,0},{3,1},{4,6},{5,7},{6,4},{7,5},{8,10},{9,11},{10,... | collective-permute-start | bytes 2015240 | tf_op jit(solution)/shard_map/ppermute | solution.py:378
  53.2 2.3 %collective-permute-start.9 = (bf16[4,320,256]{2,1,0:T(8,128)(2,1)}, bf16[4,320,256]{2,1,0:T(8,128)(2,1)S(1)}, u32[]{:S(2)}, u32[]{:S(2)}) collective-permute-start(bf16[4,320,256]{2,1,0:T(8,128)(2,1)} %collective-permute-done.8.refs_2_.refs_6_), channel_id=1, source_target_pairs={{0,4},{4,0},{8,12},{12,8},{16,20},{20,16},{24,28},{28,24},{1,5},{5... | collective-permute-start | bytes 1966088 | tf_op jit(solution)/shard_map/ppermute | solution.py:370
  55.5 37.2 %collective-permute-start.17 = (bf16[80,1536]{1,0:T(8,128)(2,1)}, bf16[80,1536]{1,0:T(8,128)(2,1)}, u32[]{:S(2)}, u32[]{:S(2)}) collective-permute-start(bf16[80,1536]{1,0:T(8,128)(2,1)} %get-tuple-element.99), channel_id=1, source_target_pairs={{0,16},{4,20},{8,24},{12,28},{16,0},{20,4},{24,8},{28,12},{1,17},{... | collective-permute-start | bytes 737288 | tf_op jit(solution)/shard_map/ppermute | solution.py:374
  63.3 17.7 %collective-permute-start.13 = (bf16[1,80,2944]{2,1,0:T(8,128)(2,1)S(1)}, bf16[1,80,2944]{2,1,0:T(8,128)(2,1)S(1)}, u32[]{:S(2)}, u32[]{:S(2)}) collective-permute-start(bf16[1,80,2944]{2,1,0:T(8,128)(2,1)S(1)} %get-tuple-element.88), channel_id=1, source_target_pairs={{0,8},{4,12},{8,0},{12,4},{16,24},{20,28},{24,16},{28,20},{1,9},{5... | collective-permute-start | bytes 1413128 | tf_op jit(solution)/shard_map/ppermute | solution.py:374
  63.3 1.7 %copy-start.4 = (bf16[4,320,256]{2,1,0:T(8,128)(2,1)S(1)}, bf16[4,320,256]{2,1,0:T(8,128)(2,1)}, u32[]{:S(2)}) copy-start(bf16[4,320,256]{2,1,0:T(8,128)(2,1)} %refs_3_.1) | copy-start | bytes 1966084
  63.3 1.7 %copy-start.5 = (f32[320]{0:T(512)S(1)}, f32[320]{0:T(512)}, u32[]{:S(2)}) copy-start(f32[320]{0:T(512)} %refs_2_.7) | copy-start | bytes 3844
  76.2 19.1 %collective-permute-start.18 = (bf16[80,1536]{1,0:T(8,128)(2,1)S(1)}, bf16[80,1536]{1,0:T(8,128)(2,1)S(1)}, u32[]{:S(2)}, u32[]{:S(2)}) collective-permute-start(bf16[80,1536]{1,0:T(8,128)(2,1)S(1)} %get-tuple-element.102), channel_id=1, source_target_pairs={{0,16},{4,20},{8,24},{12,28},{16,0},{20,4},{24,8},{28,12},{1,17},{... | collective-permute-start | bytes 737288 | tf_op jit(solution)/shard_map/ppermute | solution.py:374
  80.3 8.6 %collective-permute-start.14 = (bf16[656,256]{1,0:T(8,128)(2,1)S(1)}, bf16[656,256]{1,0:T(8,128)(2,1)S(1)}, u32[]{:S(2)}, u32[]{:S(2)}) collective-permute-start(bf16[656,256]{1,0:T(8,128)(2,1)S(1)} %get-tuple-element.91), channel_id=1, source_target_pairs={{0,2},{1,3},{2,0},{3,1},{4,6},{5,7},{6,4},{7,5},{8,10},{9,11},{10,... | collective-permute-start | bytes 1007624 | tf_op jit(solution)/shard_map/ppermute | solution.py:378
  81.0 10.5 %collective-permute-start.15 = (bf16[656,256]{1,0:T(8,128)(2,1)S(1)}, bf16[656,256]{1,0:T(8,128)(2,1)S(1)}, u32[]{:S(2)}, u32[]{:S(2)}) collective-permute-start(bf16[656,256]{1,0:T(8,128)(2,1)S(1)} %get-tuple-element.93), channel_id=1, source_target_pairs={{0,1},{1,0},{2,3},{3,2},{4,5},{5,4},{6,7},{7,6},{8,9},{9,8},{10,11... | collective-permute-start | bytes 1007624 | tf_op jit(solution)/shard_map/ppermute | solution.py:378
  89.0 12.7 %collective-permute-start.19 = (bf16[80,1536]{1,0:T(8,128)(2,1)S(1)}, bf16[80,1536]{1,0:T(8,128)(2,1)S(1)}, u32[]{:S(2)}, u32[]{:S(2)}) collective-permute-start(bf16[80,1536]{1,0:T(8,128)(2,1)S(1)} %get-tuple-element.104), channel_id=1, source_target_pairs={{0,16},{4,20},{8,24},{12,28},{16,0},{20,4},{24,8},{28,12},{1,17},{... | collective-permute-start | bytes 737288 | tf_op jit(solution)/shard_map/ppermute | solution.py:374
where the time goes:
time: 104 us
  Pallas kernels  61.4 us (59%)
  starting transfers between devices  19.8 us (19%)
  waiting for transfers between devices  18.7 us (18%)
  local copies, waits for them, and re-layouts  3.13 us (3%)
    pallas_call x18, Pallas kernels, run(): pl.pallas_call(body, out_shape=(*outs, shape((8, 128), F32)), in_specs=[m...  61.4 us
    ppermute x8, waiting for transfers between devices, swap_layer(): return lax.ppermute(x, 'dp', [(d, d ^ 2 * mask) for d in range(8)])  11.6 us
    ppermute x8, starting transfers between devices, swap_layer(): return lax.ppermute(x, 'dp', [(d, d ^ 2 * mask) for d in range(8)])  10.2 us
    ppermute x7, starting transfers between devices, swap_block(): return lax.ppermute(x, 'blk', [(d, d ^ mask) for d in range(4)])  8.78 us
    ppermute x7, waiting for transfers between devices, swap_block(): return lax.ppermute(x, 'blk', [(d, d ^ mask) for d in range(4)])  7.01 us
    unnamed x12, local copies, waits for them, and re-layouts  3.13 us
  transfers between devices with their start and end apart: 20, of which 4 were waited for; matrix products, arithmetic and copies ran while one was open for 0% of the time, Pallas kernels for 57%

commit v1 on v0

v1 whole, which is shorter than its diff:
```python
import functools

import jax
import jax.numpy as jnp
from jax import lax
from jax.experimental import pallas as pl
from jax.experimental.pallas import tpu as pltpu
from jax.sharding import PartitionSpec as P

WD = 16
TAPS = 9
F32, BF16 = jnp.float32, jnp.bfloat16
NT = (((1,), (1,)), ((), ()))
TN = (((0,), (0,)), ((), ()))
VMEM = pl.BlockSpec(memory_space=pltpu.VMEM)
ANY = pl.BlockSpec(memory_space=pl.ANY)
HBM = pl.BlockSpec(memory_space=pltpu.HBM)
SPAN = 125.0
RATE = 5e8
ROOM = dict(pre=8, a=12, fx=18, gx=4, gy=4, gd=4, ka=20, a2=8, b=10, fy=18, c=10, kb=18, f2x=8, b2=8, ab2=10, kd=10, c2=8, d=10, f2y=8, wab=10, flx=6, d2=8, resp=18, fly=6, wcd=10)
ORDER = ("pre", "a", "ka", "fx", "gx", "gy", "a2", "b", "c", "kb", "gd", "f2x", "fy", "b2", "kd", "c2", "d", "f2y", "wab", "flx", "d2", "resp", "fly", "wcd")
COST = dict(pre=20, a=45, ka=40, fx=85, gx=10, gy=10, gd=10, b=30, c=40, d=40, kb=50, kd=40, fy=10, a2=7, b2=7, c2=7, resp=110, f2x=12, f2y=12, d2=7, flx=10, fly=10, wab=24, wcd=24)


def shift_cells(maps, step_row, step_col):
    cells = maps.shape[-1]
    margin = WD + 1
    widths = [(0, 0)] * (maps.ndim - 1) + [(margin, margin)]
    flat = jnp.pad(maps, widths)
    begin = margin + step_row * WD + step_col
    moved = lax.slice_in_dim(flat, begin, begin + cells, axis=maps.ndim - 1)
    column = jnp.arange(cells, dtype=jnp.int32) % WD + step_col
    keeper = ((column >= 0) & (column < WD)).astype(maps.dtype)
    return moved * keeper


def general_body(frames, weight, bias, cotangent):
    nframe = frames.shape[0]
    local_ch = frames.shape[1]
    cells = frames.shape[2]
    whole = lax.all_gather(frames, "blk", axis=1, tiled=True)
    all_ch = whole.shape[1]
    total = jnp.zeros((nframe, local_ch, cells), F32)
    grads = []
    for tap in range(TAPS):
        ky, kx = divmod(tap, 3)
        piece = shift_cells(whole, ky - 1, kx - 1)
        w_tap = weight[:, tap * all_ch : (tap + 1) * all_ch]
        total = total + jnp.einsum("oi,fic->foc", w_tap, piece, preferred_element_type=F32)
        grads.append(
            lax.dot_general(cotangent, piece, (((0, 2), (0, 2)), ((), ())), preferred_element_type=F32)
        )
    response = (total + bias[None, :, None]).astype(BF16)
    local_grad = jnp.concatenate(grads, axis=1)
    weight_grad = lax.psum_scatter(local_grad, "dp", scatter_dimension=0, tiled=True)
    cot_moved = [shift_cells(cotangent, 1 - tap // 3, 1 - tap % 3) for tap in range(TAPS)]
    accum = jnp.zeros((all_ch, nframe, cells), F32)
    for tap in range(TAPS):
        w_cols = lax.slice_in_dim(weight, tap * all_ch, (tap + 1) * all_ch, axis=1)
        accum = accum + jnp.einsum("oi,foc->ifc", w_cols, cot_moved[tap], preferred_element_type=F32)
    shares = lax.psum_scatter(accum, "blk", scatter_dimension=0, tiled=True)
    frame_grad = jnp.transpose(shares, (1, 0, 2)).astype(BF16)
    return (response, frame_grad, weight_grad)


def scale_of(largest):
    return (jnp.maximum(largest, 1e-30) * 1.01).astype(BF16).astype(F32)


def encode(x, s):
    y = jnp.exp2(jnp.abs(x) * (2 * SPAN / s) - SPAN)
    return jnp.where(x < 0, -y, y)


def decode(code, s):
    y = code.astype(F32)
    v = (jnp.log2(jnp.abs(y)) + SPAN) * (s * (0.5 / SPAN))
    return jnp.where(y < 0, -v, v)


LANES = 128


def col_moved(x, dx):
    if dx == 0:
        return x
    rows, cells = x.shape
    col = lax.broadcasted_iota(jnp.int32, (rows, LANES), 1) % WD
    ok = (col >= dx) if dx > 0 else (col < WD + dx)
    parts = [
        jnp.where(ok, pltpu.roll(x[:, at : at + LANES], dx % LANES, 1), 0.0) for at in range(0, cells, LANES)
    ]
    return jnp.concatenate(parts, axis=1)


def row_moved(x, dy):
    if dy == 0:
        return x
    rows, cells = x.shape
    by = dy * WD
    lane = lax.broadcasted_iota(jnp.int32, (rows, LANES), 1)
    parts = [pltpu.roll(x[:, at : at + LANES], by % LANES, 1) for at in range(0, cells, LANES)]
    if dy > 0:
        parts = [jnp.where(lane < by, parts[k - 1] if k else 0.0, parts[k]) for k in range(len(parts))]
    else:
        after = parts[1:] + [0.0]
        parts = [jnp.where(lane >= LANES + by, after[k], parts[k]) for k in range(len(parts))]
    return jnp.concatenate(parts, axis=1)


def all_moved(x):
    for kx in range(3):
        along = col_moved(x, kx - 1)
        for ky in range(3):
            yield 3 * ky + kx, row_moved(along, ky - 1)


def put_rows_coded(out_ref, lead, values, width):
    rows, padded = values.shape
    s = scale_of(jnp.max(jnp.abs(values), axis=1, keepdims=True))
    codes = encode(values, s)
    last = padded - 128
    lane = lax.broadcasted_iota(jnp.int32, (rows, 128), 1) + last
    out_ref[lead + (slice(None), slice(0, last))] = codes[:, :last].astype(BF16)
    tail = jnp.where(lane < width, codes[:, last:], s)
    out_ref[lead + (slice(None), slice(last, padded))] = tail.astype(BF16)


def take_rows_coded(code, width):
    s = code[:, width : width + 1].astype(F32)
    return decode(code, s)


def weight_sums(width, cs_refs, xs_refs, f_ref):
    pieces, rows, padded = f_ref.shape
    ch = xs_refs[0].shape[0] // pieces
    for p in range(pieces):
        f_ref[p, :, width:] = jnp.zeros((rows, padded - width), F32)
    got = lax.dot_general(cs_refs[0][...], xs_refs[0][...], NT, preferred_element_type=F32)
    got = got + lax.dot_general(cs_refs[1][...], xs_refs[1][...], NT, preferred_element_type=F32)
    for t in range(TAPS):
        for p in range(pieces):
            f_ref[p, :, t * ch : (t + 1) * ch] = got[t * rows : (t + 1) * rows, p * ch : (p + 1) * ch]


def shifted_rows(far, cot_ref, cs_ref):
    nf, ch, cells = cot_ref.shape
    rows = cs_ref.shape[0] // TAPS
    block = rows // 2
    me = lax.axis_index("dp")
    z, core = me // 2, me % 2
    a = lax.broadcasted_iota(jnp.int32, (rows, ch), 0)
    o = lax.broadcasted_iota(jnp.int32, (rows, ch), 1)
    near = z ^ 1 if far else z
    layer = jnp.where(a < block, near, near ^ 2)
    want = (2 * layer + core) * block + jnp.where(a < block, a, a - block)
    pick = (o == want).astype(F32).astype(BF16)
    for f in range(nf):
        chosen = jnp.dot(pick, cot_ref[f], preferred_element_type=F32)
        at = f * cells
        for t, tap in all_moved(chosen):
            cs_ref[t * rows : (t + 1) * rows, at : at + cells] = tap.astype(BF16)


def frames_in_a_row(x_ref, xs_ref):
    nf, _, cells = x_ref.shape
    for f in range(nf):
        xs_ref[:, f * cells : (f + 1) * cells] = x_ref[f]


def own_rows_kernel(cot_ref, x_ref, cs_ref, xs_ref):
    shifted_rows(True, cot_ref, cs_ref)
    frames_in_a_row(x_ref, xs_ref)


def first_send_kernel(width, cs_ref, xs_ref, cot2_ref, x2_ref, x_ref, send_ref, cs2_ref, xs2_ref, copy_ref, f_ref):
    shifted_rows(True, cot2_ref, cs2_ref)
    frames_in_a_row(x2_ref, xs2_ref)
    copy_ref[...] = x_ref[...]
    weight_sums(width, (cs_ref, cs2_ref), (xs_ref, xs2_ref), f_ref)
    put_rows_coded(send_ref, (0,), f_ref[0], width)


def first_keep_kernel(width, cot_ref, cot2_ref, xs_ref, xs2_ref, w_hbm, keep_ref, cs_ref, cs2_ref, w_ref, sem):
    copies = load_taps(w_hbm, w_ref, sem, xs_ref.shape[0], w_ref.shape[1])
    shifted_rows(False, cot_ref, cs_ref)
    shifted_rows(False, cot2_ref, cs2_ref)
    weight_sums(width, (cs_ref, cs2_ref), (xs_ref, xs2_ref), keep_ref)
    for c in copies:
        c.wait()


def later_send_kernel(width, cs_ref, cs2_ref, xs_ref, xs2_ref, send_ref, f_ref):
    weight_sums(width, (cs_ref, cs2_ref), (xs_ref, xs2_ref), f_ref)
    put_rows_coded(send_ref, (0,), f_ref[0], width)


def later_keep_kernel(width, cs_ref, cs2_ref, *refs):
    if len(refs) == 3:
        xs_ref, xs2_ref, keep_ref = refs
        weight_sums(width, (cs_ref, cs2_ref), (xs_ref, xs2_ref), keep_ref)
    else:
        x0, x02, x1, x12, keep0_ref, keep1_ref, xs_ref, xs2_ref, f_ref = refs
        ch = x0.shape[0]
        xs_ref[:ch] = x0[...]
        xs_ref[ch:] = x1[...]
        xs2_ref[:ch] = x02[...]
        xs2_ref[ch:] = x12[...]
        weight_sums(width, (cs_ref, cs2_ref), (xs_ref, xs2_ref), f_ref)
        keep0_ref[0] = f_ref[0]
        keep1_ref[0] = f_ref[1]


def second_weight_kernel(width, pieces, *refs):
    ins, send_ref, keep_refs = refs[: 2 * pieces], refs[2 * pieces], refs[2 * pieces + 1 :]
    parts = []
    for p in range(pieces):
        keep_ref, recv_ref = ins[2 * p : 2 * p + 2]
        _, rows, padded = keep_ref.shape
        half = rows // 2
        total = keep_ref[0] + take_rows_coded(recv_ref[0], width)
        keep_refs[p][...] = total[:half]
        lane = lax.broadcasted_iota(jnp.int32, (half, padded), 1)
        far = jnp.where(lane < width, total[half:], 0.0)
        s = scale_of(jnp.max(jnp.abs(far), axis=1, keepdims=True))
        parts.append(jnp.where(lane < width, encode(far, s), s))
    if pieces == 1:
        left = send_ref.shape[1]
        fill = jnp.broadcast_to(s, (half, 2 * left - padded))
        parts = [parts[0][:, :left], jnp.concatenate([parts[0][:, left:], fill], axis=1)]
    send_ref[...] = jnp.concatenate(parts, axis=0).astype(BF16)


def last_weight_kernel(width, side, *refs):
    out_hbm, acc, stage, sem = refs[-4:]
    keeps = refs[:2]
    blk = lax.axis_index("blk")
    half, padded = keeps[0].shape
    ch = width // TAPS
    if refs[2].shape[1] == padded:
        code = refs[2][...].astype(F32)
        codes = (code[:half], code[half:])
    else:
        codes = []
        for r in refs[2:4]:
            code = r[...].astype(F32)
            codes.append(jnp.concatenate([code[:half], code[half:, : padded - r.shape[1]]], axis=1))
    for jj in range(2):
        acc[(blk % 2) ^ jj] = keeps[jj][...] + take_rows_coded(codes[jj], width)
    start = pl.multiple_of((blk ^ side) // 2 * (2 * ch), 128)
    copies = []
    for t in range(TAPS):
        for q in range(2):
            stage[t, :, q * ch : (q + 1) * ch] = acc[q, :, t * ch : (t + 1) * ch]
        copies.append(
            pltpu.make_async_copy(
                stage.at[t], out_hbm.at[:, pl.ds(pl.multiple_of(t * 4 * ch + start, 128), 2 * ch)], sem.at[t]
            )
        )
        copies[-1].start()
    for c in copies:
        c.wait()


def put_columns_coded(send_ref, lead, left, right):
    ch, cells = left.shape
    scales = []
    for k, v in enumerate((left, right)):
        s = scale_of(jnp.max(jnp.abs(v), axis=0, keepdims=True))
        send_ref[lead + (slice(k * ch, (k + 1) * ch),)] = encode(v, s).astype(BF16)
        scales.append(jnp.broadcast_to(s, (8, cells)))
    send_ref[lead + (slice(2 * ch, 2 * ch + 16),)] = jnp.concatenate(scales, axis=0).astype(BF16)


def take_columns_coded(ref, lead, ch):
    scales = ref[lead + (slice(2 * ch, 2 * ch + 16),)].astype(F32)
    return [
        decode(ref[lead + (slice(k * ch, (k + 1) * ch),)], scales[8 * k : 8 * k + 1]) for k in range(2)
    ]


def load_taps(w_hbm, w_ref, sem, rows, all_ch):
    copies = [
        pltpu.make_async_copy(
            w_hbm.at[:, pl.ds(t * all_ch, all_ch)], w_ref.at[pl.ds(t * rows, rows)], sem.at[t]
        )
        for t in range(TAPS)
    ]
    for c in copies:
        c.start()
    return copies


def frame_grad_kernel(mask, f0, w_ref, cot_hbm, send_ref, keep_ref, cot_ref, cs_ref, out_ref, sem):
    _, ch, cells = cot_hbm.shape
    all_ch = w_ref.shape[1]
    load = pltpu.make_async_copy(cot_hbm.at[pl.ds(f0, 2)], cot_ref, sem)
    load.start()
    load.wait()
    for f in range(2):
        for t, tap in all_moved(cot_ref[f].astype(F32)):
            cs_ref[t * ch : (t + 1) * ch, f * cells : (f + 1) * cells] = tap.astype(BF16)
    tile = 256
    for i0 in range(0, all_ch, tile):
        out_ref[i0 : i0 + tile, :] = lax.dot_general(
            w_ref[:, i0 : i0 + tile], cs_ref[...], TN, preferred_element_type=F32
        )
    blk = lax.axis_index("blk")

    def block(q, f):
        return out_ref[pl.ds(pl.multiple_of(q * ch, 16), ch), f * cells : (f + 1) * cells]

    for k, q in enumerate((blk ^ mask, blk ^ 3)):
        put_columns_coded(send_ref, (k,), block(q, 0), block(q, 1))
    for k, q in enumerate((blk, blk ^ (3 - mask))):
        for f in range(2):
            keep_ref[k, f * ch : (f + 1) * ch, :] = block(q, f)


def second_frame_kernel(k, r, s, k2):
    ch = k.shape[1] // 2
    for b in range(2):
        got = take_columns_coded(r, (b,), ch)
        sums = [k[b, f * ch : (f + 1) * ch, :] + got[f] for f in range(2)]
        if b == 0:
            for f in range(2):
                k2[f * ch : (f + 1) * ch, :] = sums[f]
        else:
            put_columns_coded(s, (), sums[0], sums[1])


def last_frame_kernel(f0, k, r, *refs):
    out_hbm, stage, sem = refs[-3:]
    ch = stage.shape[1]
    got = take_columns_coded(r, (), ch)
    for f in range(2):
        stage[f] = (k[f * ch : (f + 1) * ch, :] + got[f]).astype(BF16)
    copy = pltpu.make_async_copy(stage, out_hbm.at[pl.ds(f0, 2)], sem)
    copy.start()
    copy.wait()


def response_kernel(w_ref, bias_ref, x0, x1, x2, x3, out_ref, x_ref, y_ref):
    nf, ch, cells = x0.shape
    blk = lax.axis_index("blk")
    base = jnp.transpose(jnp.broadcast_to(bias_ref[...][None, :], (cells, ch)), (1, 0))

    @pl.loop(0, nf)
    def _(f):
        for jj, x in enumerate((x0, x1, x2, x3)):
            x_ref[pl.ds(pl.multiple_of((blk ^ jj) * ch, 16), ch), :] = x[f]
        y_ref[...] = jnp.dot(w_ref[...], x_ref[...], preferred_element_type=F32)
        total = base
        for ky in range(3):
            line = None
            for kx in range(3):
                t = 3 * ky + kx
                part = col_moved(y_ref[t * ch : (t + 1) * ch, :], 1 - kx)
                line = part if line is None else line + part
            total = total + row_moved(line, 1 - ky)
        out_ref[f] = total.astype(BF16)


def params(mib):
    return pltpu.CompilerParams(vmem_limit_bytes=mib * 2**20)


def shape(dims, dtype):
    return jax.ShapeDtypeStruct(dims, dtype)


def swap_core(x):
    return lax.ppermute(x, "dp", [(d, d ^ 1) for d in range(8)])


def swap_layer(x, mask):
    return lax.ppermute(x, "dp", [(d, d ^ (2 * mask)) for d in range(8)])


def swap_block(x, mask):
    return lax.ppermute(x, "blk", [(d, d ^ mask) for d in range(4)])


def run(kernel, name, key, after, args, in_specs, out_shape, out_specs, scratch=(), **more):
    outs = out_shape if isinstance(out_shape, tuple) else (out_shape,)
    specs = out_specs if isinstance(out_specs, tuple) else (out_specs,)
    waits = [] if after is None else [after]
    n = len(waits)
    mark = pl.BlockSpec((8, 128), lambda *_: (0, 0))

    def body(*refs):
        ins = n + len(args)
        refs[ins + len(outs)][...] = jnp.zeros((8, 128), F32)
        kernel(*refs[n : ins + len(outs)], *refs[ins + len(outs) + 1 :])

    *got, token = pl.pallas_call(
        body,
        out_shape=(*outs, shape((8, 128), F32)),
        in_specs=[mark] * n + list(in_specs),
        out_specs=(*specs, mark),
        scratch_shapes=list(scratch),
        compiler_params=params(ROOM[key]),
        cost_estimate=pl.CostEstimate(flops=int(COST[key] * RATE), bytes_accessed=1024, transcendentals=0),
        name=name,
        **more,
    )(*waits, *args)
    return (*got, token)


def small_body(frames, weight, bias, cotangent):
    nf, ch, cells = frames.shape
    all_ch = 4 * ch
    rows = ch // 2
    half, quarter = rows // 2, rows // 4
    width = TAPS * ch
    padded = -(-(width + 1) // 128) * 128
    left = -(-(padded // 2) // 128) * 128

    sums = shape((1, half, padded), F32)
    code = shape((1, half, padded), BF16)
    row_cs = shape((TAPS * half, nf * cells), BF16)
    row_xs = shape((ch, nf * cells), BF16)
    kept = shape((quarter, padded), F32)

    def simple(kernel, name, key, after, args, outs, scratch=()):
        return run(kernel, name, key, after, args, [VMEM] * len(args), outs, (VMEM,) * len(outs), scratch)

    def later_keep(key, after, *args):
        n = (len(args) - 2) // 2
        scratch = [pltpu.VMEM((2 * ch, nf * cells), BF16)] * 2 + [pltpu.VMEM((2, half, padded), F32)]
        return simple(
            functools.partial(later_keep_kernel, width),
            "weight_keep",
            key,
            after,
            args,
            (sums,) * n,
            scratch if n == 2 else (),
        )

    def second(key, after, *args):
        n = len(args) // 2
        out = (2 * quarter, padded) if n == 2 else (2 * quarter, left)
        return simple(
            functools.partial(second_weight_kernel, width, n),
            "weight_second",
            key,
            after,
            args,
            (shape(out, BF16),) + (kept,) * n,
        )

    def frame_part(key, after, mask, f0):
        return run(
            functools.partial(frame_grad_kernel, mask, f0),
            "frame_part",
            key,
            after,
            (taps, cotangent),
            [VMEM, HBM],
            (shape((2, 2 * ch + 16, cells), BF16), shape((2, 2 * ch, cells), F32)),
            (VMEM, VMEM),
            [
                pltpu.VMEM((2, ch, cells), BF16),
                pltpu.VMEM((TAPS * ch, 2 * cells), BF16),
                pltpu.VMEM((all_ch, 2 * cells), F32),
                pltpu.SemaphoreType.DMA,
            ],
        )

    def second_frame(key, after, *args):
        outs = (shape((2 * ch + 16, cells), BF16), shape((2 * ch, cells), F32))
        return simple(second_frame_kernel, "frame_second", key, after, args, outs)

    def last_frame(key, after, f0, parts, held):
        more = {} if held is None else {"input_output_aliases": {3: 0}}
        return run(
            functools.partial(last_frame_kernel, f0),
            "frame_last",
            key,
            after,
            parts if held is None else (*parts, held),
            [VMEM] * 2 + ([] if held is None else [HBM]),
            shape((nf, ch, cells), BF16),
            HBM,
            [pltpu.VMEM((2, ch, cells), BF16), pltpu.SemaphoreType.DMA],
            **more,
        )

    def respond(key, after, *xs):
        return run(
            response_kernel,
            "response",
            key,
            after,
            (taps, bias, *xs),
            [VMEM] * 6,
            shape((nf, ch, cells), BF16),
            VMEM,
            [pltpu.VMEM((all_ch, cells), BF16), pltpu.VMEM((TAPS * ch, cells), F32)],
        )

    def last_weight(key, after, side, parts, held):
        more = {} if held is None else {"input_output_aliases": {len(parts) + 1: 0}}
        return run(
            functools.partial(last_weight_kernel, width, side),
            "weight_last",
            key,
            after,
            parts if held is None else (*parts, held),
            [VMEM] * len(parts) + ([] if held is None else [HBM]),
            shape((quarter, TAPS * all_ch), F32),
            HBM,
            [
                pltpu.VMEM((2, quarter, padded), F32),
                pltpu.VMEM((TAPS, quarter, 2 * ch), F32),
                pltpu.SemaphoreType.DMA((TAPS,)),
            ],
            **more,
        )

    cot2 = swap_core(cotangent)
    own2 = swap_core(frames)
    near = {"x": swap_block(frames, 1)}

    t = None
    send, keep, recv, xs, cs = {}, {}, {}, {}, {}
    fsend, fkeep, frecv = {}, {}, {}
    for step in ORDER:
        if step == "pre":
            cs_own, xs_own, t = simple(own_rows_kernel, "own_rows", step, t, (cotangent, frames), (row_cs, row_xs))
        elif step == "a":
            send["a"], cs2, xs2, again, t = simple(
                functools.partial(first_send_kernel, width),
                "weight_send",
                step,
                t,
                (cs_own, xs_own, cot2, own2, frames),
                (code, row_cs, row_xs, shape((nf, ch, cells), BF16)),
                [pltpu.VMEM((1, half, padded), F32)],
            )
            cs["far"], xs["a"] = (cs_own, cs2), (xs_own, xs2)
            recv["a"] = swap_layer(send["a"], 1)
            near["y"] = swap_block(frames, 2)
        elif step in ("gx", "gy", "gd"):
            k = step[1]
            row, t = simple(frames_in_a_row, "rows", step, t, (near[k],), (row_xs,))
            xs["bcd"["xyd".index(k)]] = (row, swap_core(row))
            if k == "x":
                near["d"] = swap_block(near["x"], 2)
        elif step in ("b", "c", "d"):
            send[step], t = simple(
                functools.partial(later_send_kernel, width),
                "weight_send",
                step,
                t,
                (*cs["far"], *xs[step]),
                (code,),
                [pltpu.VMEM((1, half, padded), F32)],
            )
            recv[step] = swap_layer(send[step], 1)
        elif step == "ka":
            keep["a"], cs_near, cs2_near, taps, t = run(
                functools.partial(first_keep_kernel, width),
                "weight_keep",
                step,
                t,
                (cotangent, cot2, *xs["a"], weight),
                [VMEM] * 4 + [ANY],
                (sums, row_cs, row_cs, shape((TAPS * ch, all_ch), BF16)),
                (VMEM,) * 4,
                [pltpu.SemaphoreType.DMA((TAPS,))],
            )
            cs["near"] = (cs_near, cs2_near)
        elif step == "kb":
            keep["b"], keep["c"], t = later_keep(step, t, *cs["near"], *xs["b"], *xs["c"])
        elif step == "kd":
            keep["d"], t = later_keep(step, t, *cs["near"], *xs["d"])
        elif step == "ab2":
            send[step], keep["a2"], keep["b2"], t = second(step, t, keep["a"], recv["a"], keep["b"], recv["b"])
            recv[step] = swap_layer(send[step], 2)
        elif step in ("a2", "b2", "c2", "d2"):
            k = step[0]
            send[step], keep[step], t = second(step, t, keep[k], recv[k])
            recv[step] = swap_layer(send[step], 2)
        elif step in ("fx", "fy"):
            k = 1 if step == "fx" else 2
            fsend[k], fkeep[k], t = frame_part(step, t, k, 2 * k - 2)
            frecv[k] = swap_block(fsend[k], k)
        elif step in ("f2x", "f2y"):
            k = 1 if step == "f2x" else 2
            fsend[k + 2], fkeep[k + 2], t = second_frame(step, t, fkeep[k], frecv[k])
            frecv[k + 2] = swap_block(fsend[k + 2], 3 - k)
        elif step == "flx":
            fheld, t = last_frame(step, t, 0, (fkeep[3], frecv[3]), None)
        elif step == "fly":
            frame_grad, t = last_frame(step, t, 2, (fkeep[4], frecv[4]), fheld)
        elif step == "resp":
            response, t = respond(step, t, again, near["x"], near["y"], near["d"])
        elif step == "wab":
            codes = (recv["ab2"],) if "ab2" in recv else (recv["a2"], recv["b2"])
            held, t = last_weight(step, t, 0, (keep["a2"], keep["b2"], *codes), None)
        else:
            weight_grad, t = last_weight(step, t, 2, (keep["c2"], keep["d2"], recv["c2"], recv["d2"]), held)
    return (response, frame_grad, weight_grad)


def solution(mesh):
    small = mesh.shape["dp"] == 8 and mesh.shape["blk"] == 4
    return jax.shard_map(
        small_body if small else general_body,
        mesh=mesh,
        in_specs=(P("dp", "blk", None), P("blk", None), P("blk"), P("dp", "blk", None)),
        out_specs=(P("dp", "blk", None), P("dp", "blk", None), P(("blk", "dp"), None)),
        check_vma=False,
    )
```

time: 104 us -> 94.6 us (0.910)
  Pallas kernels: 61.4 us -> 48.3 us
  starting transfers between devices: 19.8 us -> 23.8 us
    pallas_call x18 -> x24, Pallas kernels: 61.4 us -> 48.3 us  [run(): pl.pallas_call(body, out_shape=(*outs, shape((8, 128), F32)), in_specs=[m...]
    ppermute x8, starting transfers between devices: 10.2 us -> 13.4 us  [swap_layer(): return lax.ppermute(x, 'dp', [(d, d ^ 2 * mask) for d in range(8)])]
    unnamed x12 -> x14, local copies, waits for them, and re-layouts: 3.13 us -> 2.6 us
  transfers between devices with their start and end apart: 20 -> 20, of which waited for: 4 -> 6; matrix products, arithmetic and copies ran while one was open for 0% -> 0% of each run, Pallas kernels for 57% -> 49%
where the time goes in v1:
time: 94.6 us; the launch traced here: 94.4 us
  Pallas kernels  48.3 us (51%)
  starting transfers between devices  23.8 us (25%)
  waiting for transfers between devices  18.6 us (20%)
  local copies, waits for them, and re-layouts  2.6 us (3%)
  between operations  1.08 us (1%)
    pallas_call x24, Pallas kernels, run(): pl.pallas_call(body, out_shape=(*outs, shape((8, 128), F32)), in_specs=[m...  48.3 us
    ppermute x8, starting transfers between devices, swap_layer(): return lax.ppermute(x, 'dp', [(d, d ^ 2 * mask) for d in range(8)])  13.4 us
    ppermute x8, waiting for transfers between devices, swap_layer(): return lax.ppermute(x, 'dp', [(d, d ^ 2 * mask) for d in range(8)])  12 us
    ppermute x7, starting transfers between devices, swap_block(): return lax.ppermute(x, 'blk', [(d, d ^ mask) for d in range(4)])  9.12 us
    ppermute x7, waiting for transfers between devices, swap_block(): return lax.ppermute(x, 'blk', [(d, d ^ mask) for d in range(4)])  6.64 us
    unnamed x14, local copies, waits for them, and re-layouts  2.6 us
  transfers between devices with their start and end apart: 20, of which 6 were waited for; matrix products, arithmetic and copies ran while one was open for 0% of the time, Pallas kernels for 49%

profile of v1, /device:TPU:0, one launch (start us, length us, event | category | flops | bytes accessed | tf_op | source)
XLA Modules:
  0.0 94.4 jit_solution(4674218907876408619)
XLA Ops:
  0.6 0.5 collective-permute-start.1
  1.1 2.6 %collective-permute-start.2 = (bf16[4,320,256]{2,1,0:T(8,128)(2,1)}, bf16[4,320,256]{2,1,0:T(8,128)(2,1)S(1)}, u32[]{:S(2)}, u32[]{:S(2)}) collective-permute-start(bf16[4,320,256]{2,1,0:T(8,128)(2,1)} %refs_5_.2), channel_id=1, source_target_pairs={{0,1},{1,0},{2,3},{3,2},{4,5},{5,4},{6,7},{7,6},{8,9},{9,8},{10,11... | collective-permute-start | bytes 1966088 | tf_op jit(solution)/shard_map/ppermute | solution.py:381
  3.7 1.5 %collective-permute-start.3 = (bf16[4,320,256]{2,1,0:T(8,128)(2,1)}, bf16[4,320,256]{2,1,0:T(8,128)(2,1)S(1)}, u32[]{:S(2)}, u32[]{:S(2)}) collective-permute-start(bf16[4,320,256]{2,1,0:T(8,128)(2,1)} %refs_5_.2), channel_id=1, source_target_pairs={{0,2},{1,3},{2,0},{3,1},{4,6},{5,7},{6,4},{7,5},{8,10},{9,11},{10,... | collective-permute-start | bytes 1966088 | tf_op jit(solution)/shard_map/ppermute | solution.py:381
  5.2 1.1 %copy-done = bf16[4,320,256]{2,1,0:T(8,128)(2,1)S(1)} copy-done((bf16[4,320,256]{2,1,0:T(8,128)(2,1)S(1)}, bf16[4,320,256]{2,1,0:T(8,128)(2,1)}, u32[]{:S(2)}) %copy-start) | copy-done | bytes 655384
  6.4 1.1 %copy-done.2 = bf16[4,320,256]{2,1,0:T(8,128)(2,1)S(1)} copy-done((bf16[4,320,256]{2,1,0:T(8,128)(2,1)S(1)}, bf16[4,320,256]{2,1,0:T(8,128)(2,1)}, u32[]{:S(2)}) %copy-start.2) | copy-done | bytes 655384
  7.4 0.7 own_rows.1
  8.2 0.4 copy-done.1
  8.5 2.4 %weight_send.4 = (bf16[1,80,2944]{2,1,0:T(8,128)(2,1)S(1)}, bf16[720,1024]{1,0:T(8,128)(2,1)S(1)}, bf16[320,1024]{1,0:T(8,128)(2,1)S(1)}, bf16[4,320,256]{2,1,0:T(8,128)(2,1)S(1)}, f32[8,128]{1,0:T(8,128)S(1)}) custom-call(f32[8,128]{1,0:T(8,128)S(1)} %get-tuple-element.66.refs_0_, bf16[720,1024]{1,0:T(8,128)(2,1)S(1)} %get-tuple-element.67.refs_1_, ...), custom_call_target="tpu_custom_call" | custom-call | flops 22499999744 | bytes 1024 | tf_op jit(solution)/shard_map/weight_send/pallas_call | solution.py:396
  11.0 1.6 %collective-permute-start.4 = (bf16[1,80,2944]{2,1,0:T(8,128)(2,1)S(1)}, bf16[1,80,2944]{2,1,0:T(8,128)(2,1)S(1)}, u32[]{:S(2)}, u32[]{:S(2)}) collective-permute-start(bf16[1,80,2944]{2,1,0:T(8,128)(2,1)S(1)} %get-tuple-element.77), channel_id=1, source_target_pairs={{0,8},{4,12},{8,0},{12,4},{16,24},{20,28},{24,16},{28,20},{1,9},{5... | collective-permute-start | bytes 1413128 | tf_op jit(solution)/shard_map/ppermute | solution.py:377
  12.6 2.8 %weight_keep.3 = (f32[1,80,2944]{2,1,0:T(8,128)S(1)}, bf16[720,1024]{1,0:T(8,128)(2,1)S(1)}, bf16[720,1024]{1,0:T(8,128)(2,1)S(1)}, bf16[2880,1280]{1,0:T(8,128)(2,1)S(1)}, f32[8,128]{1,0:T(8,128)S(1)}) custom-call(f32[8,128]{1,0:T(8,128)S(1)} %get-tuple-element.69.refs_0_, bf16[4,320,256]{2,1,0:T(8,128)(2,1)S(1)} %copy-done.3, ...), custom_call_target="tpu_custom_call" | custom-call | flops 20000000000 | bytes 1024 | tf_op jit(solution)/shard_map/weight_keep/pallas_call | solution.py:396
  15.4 5.7 %frame_part.2 = (bf16[2,656,256]{2,1,0:T(8,128)(2,1)S(1)}, f32[2,640,256]{2,1,0:T(8,128)S(1)}, f32[8,128]{1,0:T(8,128)S(1)}) custom-call(f32[8,128]{1,0:T(8,128)S(1)} %get-tuple-element.71.refs_0_, bf16[2880,1280]{1,0:T(8,128)(2,1)S(1)} %get-tuple-element.72.refs_1_, bf16[4,320,256]{2,1,0:T(8,128)(2,1)S(1)} %copy-done.3), custom_call_target="tpu_custom_call" | custom-call | flops 42500001792 | bytes 1024 | tf_op jit(solution)/shard_map/frame_part/pallas_call | solution.py:396
  21.1 0.1 rows.3
  21.2 0.3 collective-permute-start.5
  21.6 0.4 collective-permute-start.6
  21.9 0.5 collective-permute-start.8
  22.5 0.8 collective-permute-start.7
  23.3 0.9 collective-permute-done.4.refs_2_
  24.2 0.6 weight_second.4
  24.8 2.7 %collective-permute-start.13 = (bf16[80,1536]{1,0:T(8,128)(2,1)S(1)}, bf16[80,1536]{1,0:T(8,128)(2,1)S(1)}, u32[]{:S(2)}, u32[]{:S(2)}) collective-permute-start(bf16[80,1536]{1,0:T(8,128)(2,1)S(1)} %get-tuple-element.106), channel_id=1, source_target_pairs={{0,16},{4,20},{8,24},{12,28},{16,0},{20,4},{24,8},{28,12},{1,17},{... | collective-permute-start | bytes 737288 | tf_op jit(solution)/shard_map/ppermute | solution.py:377
  27.5 2.1 %weight_send.5 = (bf16[1,80,2944]{2,1,0:T(8,128)(2,1)S(1)}, f32[8,128]{1,0:T(8,128)S(1)}) custom-call(f32[8,128]{1,0:T(8,128)S(1)} %get-tuple-element.78.refs_0_, bf16[720,1024]{1,0:T(8,128)(2,1)S(1)} %get-tuple-element.67.refs_1_, bf16[720,1024]{1,0:T(8,128)(2,1)S(1)} %get-tuple-element.79.refs_2_, bf16[320,1024]{1,0:T(8,128)(2,1)S(1)} %get-tuple-element.80.refs_3_, ...), custom_call_target="tpu_custom_call" | custom-call | flops 15000000512 | bytes 1024 | tf_op jit(solution)/shard_map/weight_send/pallas_call | solution.py:396
  29.6 1.6 %collective-permute-start.9 = (bf16[1,80,2944]{2,1,0:T(8,128)(2,1)S(1)}, bf16[1,80,2944]{2,1,0:T(8,128)(2,1)S(1)}, u32[]{:S(2)}, u32[]{:S(2)}) collective-permute-start(bf16[1,80,2944]{2,1,0:T(8,128)(2,1)S(1)} %get-tuple-element.93), channel_id=1, source_target_pairs={{0,8},{4,12},{8,0},{12,4},{16,24},{20,28},{24,16},{28,20},{1,9},{5... | collective-permute-start | bytes 1413128 | tf_op jit(solution)/shard_map/ppermute | solution.py:377
  31.2 2.1 %weight_send.6 = (bf16[1,80,2944]{2,1,0:T(8,128)(2,1)S(1)}, f32[8,128]{1,0:T(8,128)S(1)}) custom-call(f32[8,128]{1,0:T(8,128)S(1)} %get-tuple-element.81.refs_0_, bf16[720,1024]{1,0:T(8,128)(2,1)S(1)} %get-tuple-element.67.refs_1_, bf16[720,1024]{1,0:T(8,128)(2,1)S(1)} %get-tuple-element.79.refs_2_, bf16[320,1024]{1,0:T(8,128)(2,1)S(1)} %get-tuple-element.82.refs_3_.refs_5_, ...), custom_call_target="tpu_custom_call" | custom-call | flops 20000000000 | bytes 1024 | tf_op jit(solution)/shard_map/weight_send/pallas_call | solution.py:396
  33.3 2.6 %weight_keep.4 = (f32[1,80,2944]{2,1,0:T(8,128)S(1)}, f32[1,80,2944]{2,1,0:T(8,128)S(1)}, f32[8,128]{1,0:T(8,128)S(1)}) custom-call(f32[8,128]{1,0:T(8,128)S(1)} %get-tuple-element.83.refs_0_, bf16[720,1024]{1,0:T(8,128)(2,1)S(1)} %get-tuple-element.84.refs_1_, bf16[720,1024]{1,0:T(8,128)(2,1)S(1)} %get-tuple-element.85.refs_2_, ...), custom_call_target="tpu_custom_call" | custom-call | flops 24999999488 | bytes 1024 | tf_op jit(solution)/shard_map/weight_keep/pallas_call | solution.py:396
  36.0 3.1 %collective-permute-done.7.refs_1_.refs_6_ = bf16[4,320,256]{2,1,0:T(8,128)(2,1)S(1)} collective-permute-done((bf16[4,320,256]{2,1,0:T(8,128)(2,1)S(1)}, bf16[4,320,256]{2,1,0:T(8,128)(2,1)S(1)}, u32[]{:S(2)}, u32[]{:S(2)}) %collective-permute-start.7) | collective-permute-done | bytes 655392 | tf_op jit(solution)/shard_map/ppermute | solution.py:381
  39.2 0.9 collective-permute-start.11
  40.1 0.7 frame_second.2
  40.8 5.7 %frame_part.3 = (bf16[2,656,256]{2,1,0:T(8,128)(2,1)S(1)}, f32[2,640,256]{2,1,0:T(8,128)S(1)}, f32[8,128]{1,0:T(8,128)S(1)}) custom-call(f32[8,128]{1,0:T(8,128)S(1)} %get-tuple-element.90.refs_0_, bf16[2880,1280]{1,0:T(8,128)(2,1)S(1)} %get-tuple-element.72.refs_1_, bf16[4,320,256]{2,1,0:T(8,128)(2,1)S(1)} %copy-done.3), custom_call_target="tpu_custom_call" | custom-call | flops 5000000000 | bytes 1024 | tf_op jit(solution)/shard_map/frame_part/pallas_call | solution.py:396
  46.5 1.6 %collective-permute-start.12 = (bf16[2,656,256]{2,1,0:T(8,128)(2,1)S(1)}, bf16[2,656,256]{2,1,0:T(8,128)(2,1)S(1)}, u32[]{:S(2)}, u32[]{:S(2)}) collective-permute-start(bf16[2,656,256]{2,1,0:T(8,128)(2,1)S(1)} %get-tuple-element.102), channel_id=1, source_target_pairs={{0,2},{1,3},{2,0},{3,1},{4,6},{5,7},{6,4},{7,5},{8,10},{9,11},{10,... | collective-permute-start | bytes 2015240 | tf_op jit(solution)/shard_map/ppermute | solution.py:381
  48.1 0.5 collective-permute-start.15
  48.6 0.6 weight_second.5
  49.2 2.7 %collective-permute-start.14 = (bf16[80,1536]{1,0:T(8,128)(2,1)S(1)}, bf16[80,1536]{1,0:T(8,128)(2,1)S(1)}, u32[]{:S(2)}, u32[]{:S(2)}) collective-permute-start(bf16[80,1536]{1,0:T(8,128)(2,1)S(1)} %get-tuple-element.107), channel_id=1, source_target_pairs={{0,16},{4,20},{8,24},{12,28},{16,0},{20,4},{24,8},{28,12},{1,17},{... | collective-permute-start | bytes 737288 | tf_op jit(solution)/shard_map/ppermute | solution.py:377
  51.9 1.7 %weight_keep.5 = (f32[1,80,2944]{2,1,0:T(8,128)S(1)}, f32[8,128]{1,0:T(8,128)S(1)}) custom-call(f32[8,128]{1,0:T(8,128)S(1)} %get-tuple-element.94.refs_0_, bf16[720,1024]{1,0:T(8,128)(2,1)S(1)} %get-tuple-element.84.refs_1_, bf16[720,1024]{1,0:T(8,128)(2,1)S(1)} %get-tuple-element.85.refs_2_, bf16[320,1024]{1,0:T(8,128)(2,1)S(1)} %get-tuple-element.95.refs_3_, ...), custom_call_target="tpu_custom_call" | custom-call | flops 20000000000 | bytes 1024 | tf_op jit(solution)/shard_map/weight_keep/pallas_call | solution.py:396
  53.6 4.6 %collective-permute-done.11.refs_2_ = bf16[1,80,2944]{2,1,0:T(8,128)(2,1)S(1)} collective-permute-done((bf16[1,80,2944]{2,1,0:T(8,128)(2,1)S(1)}, bf16[1,80,2944]{2,1,0:T(8,128)(2,1)S(1)}, u32[]{:S(2)}, u32[]{:S(2)}) %collective-permute-start.11) | collective-permute-done | bytes 471072 | tf_op jit(solution)/shard_map/ppermute | solution.py:377
  58.2 0.6 weight_second.6
  58.9 2.1 %weight_send.7 = (bf16[1,80,2944]{2,1,0:T(8,128)(2,1)S(1)}, f32[8,128]{1,0:T(8,128)S(1)}) custom-call(f32[8,128]{1,0:T(8,128)S(1)} %get-tuple-element.99.refs_0_, bf16[720,1024]{1,0:T(8,128)(2,1)S(1)} %get-tuple-element.67.refs_1_, bf16[720,1024]{1,0:T(8,128)(2,1)S(1)} %get-tuple-element.79.refs_2_, bf16[320,1024]{1,0:T(8,128)(2,1)S(1)} %get-tuple-element.95.refs_3_, ...), custom_call_target="tpu_custom_call" | custom-call | flops 20000000000 | bytes 1024 | tf_op jit(solution)/shard_map/weight_send/pallas_call | solution.py:396
  61.0 3.5 %collective-permute-done.12.refs_2_ = bf16[2,656,256]{2,1,0:T(8,128)(2,1)S(1)} collective-permute-done((bf16[2,656,256]{2,1,0:T(8,128)(2,1)S(1)}, bf16[2,656,256]{2,1,0:T(8,128)(2,1)S(1)}, u32[]{:S(2)}, u32[]{:S(2)}) %collective-permute-start.12) | collective-permute-done | bytes 671776 | tf_op jit(solution)/shard_map/ppermute | solution.py:381
  64.5 2.6 %collective-permute-start.18 = (bf16[80,1536]{1,0:T(8,128)(2,1)S(1)}, bf16[80,1536]{1,0:T(8,128)(2,1)S(1)}, u32[]{:S(2)}, u32[]{:S(2)}) collective-permute-start(bf16[80,1536]{1,0:T(8,128)(2,1)S(1)} %get-tuple-element.125), channel_id=1, source_target_pairs={{0,16},{4,20},{8,24},{12,28},{16,0},{20,4},{24,8},{28,12},{1,17},{... | collective-permute-start | bytes 737288 | tf_op jit(solution)/shard_map/ppermute | solution.py:377
  67.1 0.7 frame_second.3
  67.8 1.6 %collective-permute-start.17 = (bf16[656,256]{1,0:T(8,128)(2,1)S(1)}, bf16[656,256]{1,0:T(8,128)(2,1)S(1)}, u32[]{:S(2)}, u32[]{:S(2)}) collective-permute-start(bf16[656,256]{1,0:T(8,128)(2,1)S(1)} %get-tuple-element.119), channel_id=1, source_target_pairs={{0,1},{1,0},{2,3},{3,2},{4,5},{5,4},{6,7},{7,6},{8,9},{9,8},{10,11... | collective-permute-start | bytes 1007624 | tf_op jit(solution)/shard_map/ppermute | solution.py:381
  69.4 1.5 %weight_last.2 = (f32[40,11520]{1,0:T(8,128)}, f32[8,128]{1,0:T(8,128)S(1)}) custom-call(f32[8,128]{1,0:T(8,128)S(1)} %get-tuple-element.103.refs_0_, f32[40,2944]{1,0:T(8,128)S(1)} %get-tuple-element.104.refs_1_, f32[40,2944]{1,0:T(8,128)S(1)} %get-tuple-element.105.refs_2_, bf16[80,1536]{1,0:T(8,128)(2,1)S(1)} %collective-permute-done.13.refs_3_, ...), custom_call_target="tpu_custom_call" | custom-call | flops 12000000000 | bytes 1024 | tf_op jit(solution)/shard_map/weight_last/pallas_call | solution.py:396
  70.8 0.1 collective-permute-done.15.refs_2_
  70.9 0.9 frame_last.2
  71.9 6.5 %collective-permute-done.16.refs_2_ = bf16[1,80,2944]{2,1,0:T(8,128)(2,1)S(1)} collective-permute-done((bf16[1,80,2944]{2,1,0:T(8,128)(2,1)S(1)}, bf16[1,80,2944]{2,1,0:T(8,128)(2,1)S(1)}, u32[]{:S(2)}, u32[]{:S(2)}) %collective-permute-start.16) | collective-permute-done | bytes 471072 | tf_op jit(solution)/shard_map/ppermute | solution.py:377
  78.4 0.6 weight_second.7
  79.0 1.3 %collective-permute-start.19 = (bf16[80,1536]{1,0:T(8,128)(2,1)S(1)}, bf16[80,1536]{1,0:T(8,128)(2,1)S(1)}, u32[]{:S(2)}, u32[]{:S(2)}) collective-permute-start(bf16[80,1536]{1,0:T(8,128)(2,1)S(1)} %get-tuple-element.126), channel_id=1, source_target_pairs={{0,16},{4,20},{8,24},{12,28},{16,0},{20,4},{24,8},{28,12},{1,17},{... | collective-permute-start | bytes 737288 | tf_op jit(solution)/shard_map/ppermute | solution.py:377
  80.3 10.8 %response.1 = (bf16[4,320,256]{2,1,0:T(8,128)(2,1)}, f32[8,128]{1,0:T(8,128)S(1)}) custom-call(f32[8,128]{1,0:T(8,128)S(1)} %get-tuple-element.114.refs_0_, bf16[2880,1280]{1,0:T(8,128)(2,1)S(1)} %get-tuple-element.72.refs_1_, f32[320]{0:T(512)S(1)} %copy-done.4, bf16[4,320,256]{2,1,0:T(8,128)(2,1)S(1)} %get-tuple-element.115.refs_3_, ...), custom_call_target="tpu_custom_call" | custom-call | flops 54999998464 | bytes 1024 | tf_op jit(solution)/shard_map/response/pallas_call | solution.py:396
  91.1 0.9 %frame_last.3 = (bf16[4,320,256]{2,1,0:T(8,128)(2,1)}, f32[8,128]{1,0:T(8,128)S(1)}) custom-call(f32[8,128]{1,0:T(8,128)S(1)} %get-tuple-element.117.refs_0_, f32[640,256]{1,0:T(8,128)S(1)} %get-tuple-element.118.refs_1_, bf16[656,256]{1,0:T(8,128)(2,1)S(1)} %collective-permute-done.17.refs_2_, ...), custom_call_target="tpu_custom_call", output_to_operand_aliasing={{0}: (3, {})} | custom-call | flops 5000000000 | bytes 1024 | tf_op jit(solution)/shard_map/frame_last/pallas_call | solution.py:396
  92.1 2.1 %weight_last.3 = (f32[40,11520]{1,0:T(8,128)}, f32[8,128]{1,0:T(8,128)}) custom-call(f32[8,128]{1,0:T(8,128)S(1)} %get-tuple-element.122.refs_0_, f32[40,2944]{1,0:T(8,128)S(1)} %get-tuple-element.123.refs_1_, f32[40,2944]{1,0:T(8,128)S(1)} %get-tuple-element.124.refs_2_, ...), custom_call_target="tpu_custom_call", output_to_operand_aliasing={{0}: (5, {})} | custom-call | flops 12000000000 | bytes 1024 | tf_op jit(solution)/shard_map/weight_last/pallas_call | solution.py:396
  (31 shorter events, 0.3 us)
Async XLA Ops:
  0.6 7.5 %collective-permute-start.1 = (bf16[4,320,256]{2,1,0:T(8,128)(2,1)}, bf16[4,320,256]{2,1,0:T(8,128)(2,1)S(1)}, u32[]{:S(2)}, u32[]{:S(2)}) collective-permute-start(bf16[4,320,256]{2,1,0:T(8,128)(2,1)} %refs_5_.2), channel_id=1, source_target_pairs={{0,4},{4,0},{8,12},{12,8},{16,20},{20,16},{24,28},{28,24},{1,5},{5... | collective-permute-start | bytes 1966088 | tf_op jit(solution)/shard_map/ppermute | solution.py:373
  1.1 20.0 %collective-permute-start.2 = (bf16[4,320,256]{2,1,0:T(8,128)(2,1)}, bf16[4,320,256]{2,1,0:T(8,128)(2,1)S(1)}, u32[]{:S(2)}, u32[]{:S(2)}) collective-permute-start(bf16[4,320,256]{2,1,0:T(8,128)(2,1)} %refs_5_.2), channel_id=1, source_target_pairs={{0,1},{1,0},{2,3},{3,2},{4,5},{5,4},{6,7},{7,6},{8,9},{9,8},{10,11... | collective-permute-start | bytes 1966088 | tf_op jit(solution)/shard_map/ppermute | solution.py:381
  3.7 17.8 %collective-permute-start.3 = (bf16[4,320,256]{2,1,0:T(8,128)(2,1)}, bf16[4,320,256]{2,1,0:T(8,128)(2,1)S(1)}, u32[]{:S(2)}, u32[]{:S(2)}) collective-permute-start(bf16[4,320,256]{2,1,0:T(8,128)(2,1)} %refs_5_.2), channel_id=1, source_target_pairs={{0,2},{1,3},{2,0},{3,1},{4,6},{5,7},{6,4},{7,5},{8,10},{9,11},{10,... | collective-permute-start | bytes 1966088 | tf_op jit(solution)/shard_map/ppermute | solution.py:381
  5.2 2.9 %collective-permute-start = (bf16[4,320,256]{2,1,0:T(8,128)(2,1)}, bf16[4,320,256]{2,1,0:T(8,128)(2,1)S(1)}, u32[]{:S(2)}, u32[]{:S(2)}) collective-permute-start(bf16[4,320,256]{2,1,0:T(8,128)(2,1)} %refs_2_.4), channel_id=1, source_target_pairs={{0,4},{4,0},{8,12},{12,8},{16,20},{20,16},{24,28},{28,24},{1,5},{5... | collective-permute-start | bytes 1966088 | tf_op jit(solution)/shard_map/ppermute | solution.py:373
  5.2 1.1 %copy-start = (bf16[4,320,256]{2,1,0:T(8,128)(2,1)S(1)}, bf16[4,320,256]{2,1,0:T(8,128)(2,1)}, u32[]{:S(2)}) copy-start(bf16[4,320,256]{2,1,0:T(8,128)(2,1)} %refs_5_.2) | copy-start | bytes 1966084
  6.4 1.1 %copy-start.2 = (bf16[4,320,256]{2,1,0:T(8,128)(2,1)S(1)}, bf16[4,320,256]{2,1,0:T(8,128)(2,1)}, u32[]{:S(2)}) copy-start(bf16[4,320,256]{2,1,0:T(8,128)(2,1)} %refs_2_.4) | copy-start | bytes 1966084
  7.4 1.1 %copy-start.1 = (bf16[4,320,256]{2,1,0:T(8,128)(2,1)S(1)}, bf16[4,320,256]{2,1,0:T(8,128)(2,1)}, u32[]{:S(2)}) copy-start(bf16[4,320,256]{2,1,0:T(8,128)(2,1)} %refs_5_.2) | copy-start | bytes 1966084
  7.4 5.2 %slice-start = ((s8[7372800]{0:T(1024)(128)(4,1)}), s8[4194304]{0:T(1024)(128)(4,1)S(1)}, s32[]{:S(2)}) async-start(s8[7372800]{0:T(1024)(128)(4,1)} %bitcast), calls=%async_computation | async-start | bytes 8388608
  8.5 4.1 %slice-start.1 = ((s8[7372800]{0:T(1024)(128)(4,1)}), s8[3178496]{0:T(1024)(128)(4,1)S(1)}, s32[]{:S(2)}) async-start(s8[7372800]{0:T(1024)(128)(4,1)} %bitcast), calls=%async_computation.1 | async-start | bytes 6356992
  8.5 4.1 %copy-start.3 = (bf16[4,320,256]{2,1,0:T(8,128)(2,1)S(1)}, bf16[4,320,256]{2,1,0:T(8,128)(2,1)}, u32[]{:S(2)}) copy-start(bf16[4,320,256]{2,1,0:T(8,128)(2,1)} %refs_2_.4) | copy-start | bytes 1966084
  11.0 13.2 %collective-permute-start.4 = (bf16[1,80,2944]{2,1,0:T(8,128)(2,1)S(1)}, bf16[1,80,2944]{2,1,0:T(8,128)(2,1)S(1)}, u32[]{:S(2)}, u32[]{:S(2)}) collective-permute-start(bf16[1,80,2944]{2,1,0:T(8,128)(2,1)S(1)} %get-tuple-element.77), channel_id=1, source_target_pairs={{0,8},{4,12},{8,0},{12,4},{16,24},{20,28},{24,16},{28,20},{1,9},{5... | collective-permute-start | bytes 1413128 | tf_op jit(solution)/shard_map/ppermute | solution.py:377
  21.2 6.3 %collective-permute-start.5 = (bf16[320,1024]{1,0:T(8,128)(2,1)S(1)}, bf16[320,1024]{1,0:T(8,128)(2,1)S(1)}, u32[]{:S(2)}, u32[]{:S(2)}) collective-permute-start(bf16[320,1024]{1,0:T(8,128)(2,1)S(1)} %get-tuple-element.80.refs_3_), channel_id=1, source_target_pairs={{0,4},{4,0},{8,12},{12,8},{16,20},{20,16},{24,28},{28,24},{1,5},{5... | collective-permute-start | bytes 1966088 | tf_op jit(solution)/shard_map/ppermute | solution.py:373
  21.6 9.7 %collective-permute-start.6 = (bf16[320,1024]{1,0:T(8,128)(2,1)S(1)}, bf16[320,1024]{1,0:T(8,128)(2,1)S(1)}, u32[]{:S(2)}, u32[]{:S(2)}) collective-permute-start(bf16[320,1024]{1,0:T(8,128)(2,1)S(1)} %get-tuple-element.82.refs_3_.refs_5_), channel_id=1, source_target_pairs={{0,4},{4,0},{8,12},{12,8},{16,20},{20,16},{24,28},{28,24},{1,5},{5... | collective-permute-start | bytes 1966088 | tf_op jit(solution)/shard_map/ppermute | solution.py:373
  21.9 18.1 %collective-permute-start.8 = (bf16[2,656,256]{2,1,0:T(8,128)(2,1)S(1)}, bf16[2,656,256]{2,1,0:T(8,128)(2,1)S(1)}, u32[]{:S(2)}, u32[]{:S(2)}) collective-permute-start(bf16[2,656,256]{2,1,0:T(8,128)(2,1)S(1)} %get-tuple-element.89), channel_id=1, source_target_pairs={{0,1},{1,0},{2,3},{3,2},{4,5},{5,4},{6,7},{7,6},{8,9},{9,8},{10,11... | collective-permute-start | bytes 2015240 | tf_op jit(solution)/shard_map/ppermute | solution.py:381
  22.5 16.6 %collective-permute-start.7 = (bf16[4,320,256]{2,1,0:T(8,128)(2,1)S(1)}, bf16[4,320,256]{2,1,0:T(8,128)(2,1)S(1)}, u32[]{:S(2)}, u32[]{:S(2)}) collective-permute-start(bf16[4,320,256]{2,1,0:T(8,128)(2,1)S(1)} %collective-permute-done.2.refs_1_.refs_4_), channel_id=1, source_target_pairs={{0,2},{1,3},{2,0},{3,1},{4,6},{5,7},{6,4},{7,5},{8,10},{9,11},{10,... | collective-permute-start | bytes 1966088 | tf_op jit(solution)/shard_map/ppermute | solution.py:381
  24.8 42.9 %collective-permute-start.13 = (bf16[80,1536]{1,0:T(8,128)(2,1)S(1)}, bf16[80,1536]{1,0:T(8,128)(2,1)S(1)}, u32[]{:S(2)}, u32[]{:S(2)}) collective-permute-start(bf16[80,1536]{1,0:T(8,128)(2,1)S(1)} %get-tuple-element.106), channel_id=1, source_target_pairs={{0,16},{4,20},{8,24},{12,28},{16,0},{20,4},{24,8},{28,12},{1,17},{... | collective-permute-start | bytes 737288 | tf_op jit(solution)/shard_map/ppermute | solution.py:377
  29.6 18.5 %collective-permute-start.9 = (bf16[1,80,2944]{2,1,0:T(8,128)(2,1)S(1)}, bf16[1,80,2944]{2,1,0:T(8,128)(2,1)S(1)}, u32[]{:S(2)}, u32[]{:S(2)}) collective-permute-start(bf16[1,80,2944]{2,1,0:T(8,128)(2,1)S(1)} %get-tuple-element.93), channel_id=1, source_target_pairs={{0,8},{4,12},{8,0},{12,4},{16,24},{20,28},{24,16},{28,20},{1,9},{5... | collective-permute-start | bytes 1413128 | tf_op jit(solution)/shard_map/ppermute | solution.py:377
  39.1 10.1 %collective-permute-start.10 = (bf16[320,1024]{1,0:T(8,128)(2,1)S(1)}, bf16[320,1024]{1,0:T(8,128)(2,1)S(1)}, u32[]{:S(2)}, u32[]{:S(2)}) collective-permute-start(bf16[320,1024]{1,0:T(8,128)(2,1)S(1)} %get-tuple-element.95.refs_3_), channel_id=1, source_target_pairs={{0,4},{4,0},{8,12},{12,8},{16,20},{20,16},{24,28},{28,24},{1,5},{5... | collective-permute-start | bytes 1966088 | tf_op jit(solution)/shard_map/ppermute | solution.py:373
  39.2 19.0 %collective-permute-start.11 = (bf16[1,80,2944]{2,1,0:T(8,128)(2,1)S(1)}, bf16[1,80,2944]{2,1,0:T(8,128)(2,1)S(1)}, u32[]{:S(2)}, u32[]{:S(2)}) collective-permute-start(bf16[1,80,2944]{2,1,0:T(8,128)(2,1)S(1)} %get-tuple-element.98), channel_id=1, source_target_pairs={{0,8},{4,12},{8,0},{12,4},{16,24},{20,28},{24,16},{28,20},{1,9},{5... | collective-permute-start | bytes 1413128 | tf_op jit(solution)/shard_map/ppermute | solution.py:377
  46.5 18.0 %collective-permute-start.12 = (bf16[2,656,256]{2,1,0:T(8,128)(2,1)S(1)}, bf16[2,656,256]{2,1,0:T(8,128)(2,1)S(1)}, u32[]{:S(2)}, u32[]{:S(2)}) collective-permute-start(bf16[2,656,256]{2,1,0:T(8,128)(2,1)S(1)} %get-tuple-element.102), channel_id=1, source_target_pairs={{0,2},{1,3},{2,0},{3,1},{4,6},{5,7},{6,4},{7,5},{8,10},{9,11},{10,... | collective-permute-start | bytes 2015240 | tf_op jit(solution)/shard_map/ppermute | solution.py:381
  48.1 22.8 %collective-permute-start.15 = (bf16[656,256]{1,0:T(8,128)(2,1)S(1)}, bf16[656,256]{1,0:T(8,128)(2,1)S(1)}, u32[]{:S(2)}, u32[]{:S(2)}) collective-permute-start(bf16[656,256]{1,0:T(8,128)(2,1)S(1)} %get-tuple-element.110), channel_id=1, source_target_pairs={{0,2},{1,3},{2,0},{3,1},{4,6},{5,7},{6,4},{7,5},{8,10},{9,11},{10,... | collective-permute-start | bytes 1007624 | tf_op jit(solution)/shard_map/ppermute | solution.py:381
  49.2 20.1 %collective-permute-start.14 = (bf16[80,1536]{1,0:T(8,128)(2,1)S(1)}, bf16[80,1536]{1,0:T(8,128)(2,1)S(1)}, u32[]{:S(2)}, u32[]{:S(2)}) collective-permute-start(bf16[80,1536]{1,0:T(8,128)(2,1)S(1)} %get-tuple-element.107), channel_id=1, source_target_pairs={{0,16},{4,20},{8,24},{12,28},{16,0},{20,4},{24,8},{28,12},{1,17},{... | collective-permute-start | bytes 737288 | tf_op jit(solution)/shard_map/ppermute | solution.py:377
  61.0 17.4 %collective-permute-start.16 = (bf16[1,80,2944]{2,1,0:T(8,128)(2,1)S(1)}, bf16[1,80,2944]{2,1,0:T(8,128)(2,1)S(1)}, u32[]{:S(2)}, u32[]{:S(2)}) collective-permute-start(bf16[1,80,2944]{2,1,0:T(8,128)(2,1)S(1)} %get-tuple-element.113), channel_id=1, source_target_pairs={{0,8},{4,12},{8,0},{12,4},{16,24},{20,28},{24,16},{28,20},{1,9},{5... | collective-permute-start | bytes 1413128 | tf_op jit(solution)/shard_map/ppermute | solution.py:377
  64.5 27.6 %collective-permute-start.18 = (bf16[80,1536]{1,0:T(8,128)(2,1)S(1)}, bf16[80,1536]{1,0:T(8,128)(2,1)S(1)}, u32[]{:S(2)}, u32[]{:S(2)}) collective-permute-start(bf16[80,1536]{1,0:T(8,128)(2,1)S(1)} %get-tuple-element.125), channel_id=1, source_target_pairs={{0,16},{4,20},{8,24},{12,28},{16,0},{20,4},{24,8},{28,12},{1,17},{... | collective-permute-start | bytes 737288 | tf_op jit(solution)/shard_map/ppermute | solution.py:377
  67.8 23.3 %collective-permute-start.17 = (bf16[656,256]{1,0:T(8,128)(2,1)S(1)}, bf16[656,256]{1,0:T(8,128)(2,1)S(1)}, u32[]{:S(2)}, u32[]{:S(2)}) collective-permute-start(bf16[656,256]{1,0:T(8,128)(2,1)S(1)} %get-tuple-element.119), channel_id=1, source_target_pairs={{0,1},{1,0},{2,3},{3,2},{4,5},{5,4},{6,7},{7,6},{8,9},{9,8},{10,11... | collective-permute-start | bytes 1007624 | tf_op jit(solution)/shard_map/ppermute | solution.py:381
  78.4 2.0 %copy-start.4 = (f32[320]{0:T(512)S(1)}, f32[320]{0:T(512)}, u32[]{:S(2)}) copy-start(f32[320]{0:T(512)} %refs_2_.5) | copy-start | bytes 3844
  79.0 13.1 %collective-permute-start.19 = (bf16[80,1536]{1,0:T(8,128)(2,1)S(1)}, bf16[80,1536]{1,0:T(8,128)(2,1)S(1)}, u32[]{:S(2)}, u32[]{:S(2)}) collective-permute-start(bf16[80,1536]{1,0:T(8,128)(2,1)S(1)} %get-tuple-element.126), channel_id=1, source_target_pairs={{0,16},{4,20},{8,24},{12,28},{16,0},{20,4},{24,8},{28,12},{1,17},{... | collective-permute-start | bytes 737288 | tf_op jit(solution)/shard_map/ppermute | solution.py:377

commit v2 on v1

--- a/solution.py
+++ b/solution.py
@@ -17,9 +17,9 @@
 HBM = pl.BlockSpec(memory_space=pltpu.HBM)
 SPAN = 125.0
 RATE = 5e8
-ROOM = dict(pre=8, a=12, fx=18, gx=4, gy=4, gd=4, ka=20, a2=8, b=10, fy=18, c=10, kb=18, f2x=8, b2=8, ab2=10, kd=10, c2=8, d=10, f2y=8, wab=10, flx=6, d2=8, resp=18, fly=6, wcd=10)
-ORDER = ("pre", "a", "ka", "fx", "gx", "gy", "a2", "b", "c", "kb", "gd", "f2x", "fy", "b2", "kd", "c2", "d", "f2y", "wab", "flx", "d2", "resp", "fly", "wcd")
-COST = dict(pre=20, a=45, ka=40, fx=85, gx=10, gy=10, gd=10, b=30, c=40, d=40, kb=50, kd=40, fy=10, a2=7, b2=7, c2=7, resp=110, f2x=12, f2y=12, d2=7, flx=10, fly=10, wab=24, wcd=24)
+ROOM = dict(pre=8, a=12, fx=18, gx=4, gy=4, gd=4, ka=20, a2=8, b=10, fy=18, c=10, kb=18, f2x=8, b2=8, kd=10, c2=8, d=10, f2y=8, wab=10, flx=6, d2=8, resp=18, fly=6, wcd=10, ea=8, eb=8, ec=8)
+ORDER = ("pre", "a", "ka", "fx", "gx", "gy", "a2", "b", "c", "kb", "f2x", "ea", "gd", "fy", "b2", "d", "kd", "c2", "eb", "f2y", "wab", "flx", "d2", "resp", "fly", "ec", "wcd")
+COST = dict(pre=20, a=45, ka=40, fx=85, gx=10, gy=10, gd=10, b=40, c=40, d=40, kb=50, kd=40, fy=85, a2=7, b2=7, c2=7, resp=110, f2x=12, f2y=12, d2=7, flx=10, fly=10, wab=24, wcd=24, ea=7, eb=7, ec=7)
 
 
 def shift_cells(maps, step_row, step_col):
@@ -231,22 +231,26 @@
     send_ref[...] = jnp.concatenate(parts, axis=0).astype(BF16)
 
 
+def unstacked(ref, padded):
+    code = ref[...].astype(F32)
+    half, left = code.shape[0] // 2, code.shape[1]
+    return jnp.concatenate([code[:half], code[half:, : padded - left]], axis=1)
+
+
+def finish_weight_kernel(width, keep_ref, recv_ref, out_ref):
+    out_ref[...] = keep_ref[...] + take_rows_coded(unstacked(recv_ref, keep_ref.shape[1]), width)
+
+
 def last_weight_kernel(width, side, *refs):
     out_hbm, acc, stage, sem = refs[-4:]
-    keeps = refs[:2]
     blk = lax.axis_index("blk")
-    half, padded = keeps[0].shape
     ch = width // TAPS
-    if refs[2].shape[1] == padded:
-        code = refs[2][...].astype(F32)
-        codes = (code[:half], code[half:])
+    first = blk % 2
+    acc[first] = refs[0][...]
+    if side == 0:
+        acc[1 - first] = refs[1][...]
     else:
-        codes = []
-        for r in refs[2:4]:
-            code = r[...].astype(F32)
-            codes.append(jnp.concatenate([code[:half], code[half:, : padded - r.shape[1]]], axis=1))
-    for jj in range(2):
-        acc[(blk % 2) ^ jj] = keeps[jj][...] + take_rows_coded(codes[jj], width)
+        acc[1 - first] = refs[1][...] + take_rows_coded(unstacked(refs[2], refs[1].shape[1]), width)
     start = pl.multiple_of((blk ^ side) // 2 * (2 * ch), 128)
     copies = []
     for t in range(TAPS):
@@ -576,9 +580,6 @@
             keep["b"], keep["c"], t = later_keep(step, t, *cs["near"], *xs["b"], *xs["c"])
         elif step == "kd":
             keep["d"], t = later_keep(step, t, *cs["near"], *xs["d"])
-        elif step == "ab2":
-            send[step], keep["a2"], keep["b2"], t = second(step, t, keep["a"], recv["a"], keep["b"], recv["b"])
-            recv[step] = swap_layer(send[step], 2)
         elif step in ("a2", "b2", "c2", "d2"):
             k = step[0]
             send[step], keep[step], t = second(step, t, keep[k], recv[k])
@@ -597,11 +598,15 @@
             frame_grad, t = last_frame(step, t, 2, (fkeep[4], frecv[4]), fheld)
         elif step == "resp":
             response, t = respond(step, t, again, near["x"], near["y"], near["d"])
+        elif step in ("ea", "eb", "ec"):
+            k = step[1] + "2"
+            keep[step], t = simple(
+                functools.partial(finish_weight_kernel, width), "weight_end", step, t, (keep[k], recv[k]), (kept,)
+            )
         elif step == "wab":
-            codes = (recv["ab2"],) if "ab2" in recv else (recv["a2"], recv["b2"])
-            held, t = last_weight(step, t, 0, (keep["a2"], keep["b2"], *codes), None)
+            held, t = last_weight(step, t, 0, (keep["ea"], keep["eb"]), None)
         else:
-            weight_grad, t = last_weight(step, t, 2, (keep["c2"], keep["d2"], recv["c2"], recv["d2"]), held)
+            weight_grad, t = last_weight(step, t, 2, (keep["ec"], keep["d2"], recv["d2"]), held)
     return (response, frame_grad, weight_grad)
 
 

time: 94.6 us -> 92 us (0.973)
  starting transfers between devices: 23.8 us -> 19.9 us
  waiting for transfers between devices: 18.6 us -> 19.7 us
    ppermute x8, waiting for transfers between devices: 12 us -> 16.8 us  [swap_layer(): return lax.ppermute(x, 'dp', [(d, d ^ 2 * mask) for d in range(8)])]
    ppermute x7, waiting for transfers between devices: 6.64 us -> 2.91 us  [swap_block(): return lax.ppermute(x, 'blk', [(d, d ^ mask) for d in range(4)])]
    ppermute x8, starting transfers between devices: 13.4 us -> 10.6 us  [swap_layer(): return lax.ppermute(x, 'dp', [(d, d ^ 2 * mask) for d in range(8)])]
    ppermute x7, starting transfers between devices: 9.12 us -> 8.16 us  [swap_block(): return lax.ppermute(x, 'blk', [(d, d ^ mask) for d in range(4)])]
    pallas_call x24 -> x27, Pallas kernels: 48.3 us -> 48.5 us  [run(): pl.pallas_call(body, out_shape=(*outs, shape((8, 128), F32)), in_specs=[m...]
  transfers between devices with their start and end apart: 20 -> 20, of which waited for: 6 -> 6; matrix products, arithmetic and copies ran while one was open for 0% -> 0% of each run, Pallas kernels for 49% -> 51%
where the time goes in v2:
time: 92 us; the launch traced here: 91.8 us
  Pallas kernels  48.5 us (53%)
  starting transfers between devices  19.9 us (22%)
  waiting for transfers between devices  19.7 us (21%)
  local copies, waits for them, and re-layouts  2.59 us (3%)
  between operations  1.09 us (1%)
    pallas_call x27, Pallas kernels, run(): pl.pallas_call(body, out_shape=(*outs, shape((8, 128), F32)), in_specs=[m...  48.5 us
    ppermute x8, waiting for transfers between devices, swap_layer(): return lax.ppermute(x, 'dp', [(d, d ^ 2 * mask) for d in range(8)])  16.8 us
    ppermute x8, starting transfers between devices, swap_layer(): return lax.ppermute(x, 'dp', [(d, d ^ 2 * mask) for d in range(8)])  10.6 us
    ppermute x7, starting transfers between devices, swap_block(): return lax.ppermute(x, 'blk', [(d, d ^ mask) for d in range(4)])  8.16 us
    ppermute x7, waiting for transfers between devices, swap_block(): return lax.ppermute(x, 'blk', [(d, d ^ mask) for d in range(4)])  2.91 us
    unnamed x14, local copies, waits for them, and re-layouts  2.59 us
  transfers between devices with their start and end apart: 20, of which 6 were waited for; matrix products, arithmetic and copies ran while one was open for 0% of the time, Pallas kernels for 51%

profile of v2, /device:TPU:0, one launch (start us, length us, event | category | flops | bytes accessed | tf_op | source)
XLA Modules:
  0.0 91.8 jit_solution(5236165763484400101)
XLA Ops:
  0.6 0.5 collective-permute-start.1
  1.1 2.6 %collective-permute-start.2 = (bf16[4,320,256]{2,1,0:T(8,128)(2,1)}, bf16[4,320,256]{2,1,0:T(8,128)(2,1)S(1)}, u32[]{:S(2)}, u32[]{:S(2)}) collective-permute-start(bf16[4,320,256]{2,1,0:T(8,128)(2,1)} %refs_5_.2), channel_id=1, source_target_pairs={{0,1},{1,0},{2,3},{3,2},{4,5},{5,4},{6,7},{7,6},{8,9},{9,8},{10,11... | collective-permute-start | bytes 1966088 | tf_op jit(solution)/shard_map/ppermute | solution.py:385
  3.7 1.5 %collective-permute-start.3 = (bf16[4,320,256]{2,1,0:T(8,128)(2,1)}, bf16[4,320,256]{2,1,0:T(8,128)(2,1)S(1)}, u32[]{:S(2)}, u32[]{:S(2)}) collective-permute-start(bf16[4,320,256]{2,1,0:T(8,128)(2,1)} %refs_5_.2), channel_id=1, source_target_pairs={{0,2},{1,3},{2,0},{3,1},{4,6},{5,7},{6,4},{7,5},{8,10},{9,11},{10,... | collective-permute-start | bytes 1966088 | tf_op jit(solution)/shard_map/ppermute | solution.py:385
  5.2 1.1 %copy-done = bf16[4,320,256]{2,1,0:T(8,128)(2,1)S(1)} copy-done((bf16[4,320,256]{2,1,0:T(8,128)(2,1)S(1)}, bf16[4,320,256]{2,1,0:T(8,128)(2,1)}, u32[]{:S(2)}) %copy-start) | copy-done | bytes 655384
  6.4 1.1 %copy-done.2 = bf16[4,320,256]{2,1,0:T(8,128)(2,1)S(1)} copy-done((bf16[4,320,256]{2,1,0:T(8,128)(2,1)S(1)}, bf16[4,320,256]{2,1,0:T(8,128)(2,1)}, u32[]{:S(2)}) %copy-start.2) | copy-done | bytes 655384
  7.4 0.7 own_rows.1
  8.2 0.4 copy-done.1
  8.5 2.4 %weight_send.4 = (bf16[1,80,2944]{2,1,0:T(8,128)(2,1)S(1)}, bf16[720,1024]{1,0:T(8,128)(2,1)S(1)}, bf16[320,1024]{1,0:T(8,128)(2,1)S(1)}, bf16[4,320,256]{2,1,0:T(8,128)(2,1)S(1)}, f32[8,128]{1,0:T(8,128)S(1)}) custom-call(f32[8,128]{1,0:T(8,128)S(1)} %get-tuple-element.72.refs_0_, bf16[720,1024]{1,0:T(8,128)(2,1)S(1)} %get-tuple-element.73.refs_1_, ...), custom_call_target="tpu_custom_call" | custom-call | flops 22499999744 | bytes 1024 | tf_op jit(solution)/shard_map/weight_send/pallas_call | solution.py:400
  11.0 1.6 %collective-permute-start.4 = (bf16[1,80,2944]{2,1,0:T(8,128)(2,1)S(1)}, bf16[1,80,2944]{2,1,0:T(8,128)(2,1)S(1)}, u32[]{:S(2)}, u32[]{:S(2)}) collective-permute-start(bf16[1,80,2944]{2,1,0:T(8,128)(2,1)S(1)} %get-tuple-element.83), channel_id=1, source_target_pairs={{0,8},{4,12},{8,0},{12,4},{16,24},{20,28},{24,16},{28,20},{1,9},{5... | collective-permute-start | bytes 1413128 | tf_op jit(solution)/shard_map/ppermute | solution.py:381
  12.6 2.8 %weight_keep.3 = (f32[1,80,2944]{2,1,0:T(8,128)S(1)}, bf16[720,1024]{1,0:T(8,128)(2,1)S(1)}, bf16[720,1024]{1,0:T(8,128)(2,1)S(1)}, bf16[2880,1280]{1,0:T(8,128)(2,1)S(1)}, f32[8,128]{1,0:T(8,128)S(1)}) custom-call(f32[8,128]{1,0:T(8,128)S(1)} %get-tuple-element.75.refs_0_, bf16[4,320,256]{2,1,0:T(8,128)(2,1)S(1)} %copy-done.3, ...), custom_call_target="tpu_custom_call" | custom-call | flops 20000000000 | bytes 1024 | tf_op jit(solution)/shard_map/weight_keep/pallas_call | solution.py:400
  15.5 5.7 %frame_part.2 = (bf16[2,656,256]{2,1,0:T(8,128)(2,1)S(1)}, f32[2,640,256]{2,1,0:T(8,128)S(1)}, f32[8,128]{1,0:T(8,128)S(1)}) custom-call(f32[8,128]{1,0:T(8,128)S(1)} %get-tuple-element.77.refs_0_, bf16[2880,1280]{1,0:T(8,128)(2,1)S(1)} %get-tuple-element.78.refs_1_, bf16[4,320,256]{2,1,0:T(8,128)(2,1)S(1)} %copy-done.3), custom_call_target="tpu_custom_call" | custom-call | flops 42500001792 | bytes 1024 | tf_op jit(solution)/shard_map/frame_part/pallas_call | solution.py:400
  21.3 0.3 collective-permute-start.5
  21.6 0.4 collective-permute-start.6
  22.0 0.5 collective-permute-start.7
  22.5 0.8 collective-permute-start.9
  23.3 0.9 collective-permute-done.4.refs_2_
  24.2 0.6 weight_second.4
  24.8 2.7 %collective-permute-start.8 = (bf16[80,1536]{1,0:T(8,128)(2,1)S(1)}, bf16[80,1536]{1,0:T(8,128)(2,1)S(1)}, u32[]{:S(2)}, u32[]{:S(2)}) collective-permute-start(bf16[80,1536]{1,0:T(8,128)(2,1)S(1)} %get-tuple-element.97), channel_id=1, source_target_pairs={{0,16},{4,20},{8,24},{12,28},{16,0},{20,4},{24,8},{28,12},{1,17},{... | collective-permute-start | bytes 737288 | tf_op jit(solution)/shard_map/ppermute | solution.py:381
  27.5 2.1 %weight_send.5 = (bf16[1,80,2944]{2,1,0:T(8,128)(2,1)S(1)}, f32[8,128]{1,0:T(8,128)S(1)}) custom-call(f32[8,128]{1,0:T(8,128)S(1)} %get-tuple-element.84.refs_0_, bf16[720,1024]{1,0:T(8,128)(2,1)S(1)} %get-tuple-element.73.refs_1_, bf16[720,1024]{1,0:T(8,128)(2,1)S(1)} %get-tuple-element.85.refs_2_, bf16[320,1024]{1,0:T(8,128)(2,1)S(1)} %get-tuple-element.86.refs_3_, ...), custom_call_target="tpu_custom_call" | custom-call | flops 20000000000 | bytes 1024 | tf_op jit(solution)/shard_map/weight_send/pallas_call | solution.py:400
  29.6 1.6 %collective-permute-start.10 = (bf16[1,80,2944]{2,1,0:T(8,128)(2,1)S(1)}, bf16[1,80,2944]{2,1,0:T(8,128)(2,1)S(1)}, u32[]{:S(2)}, u32[]{:S(2)}) collective-permute-start(bf16[1,80,2944]{2,1,0:T(8,128)(2,1)S(1)} %get-tuple-element.102), channel_id=1, source_target_pairs={{0,8},{4,12},{8,0},{12,4},{16,24},{20,28},{24,16},{28,20},{1,9},{5... | collective-permute-start | bytes 1413128 | tf_op jit(solution)/shard_map/ppermute | solution.py:381
  31.2 2.1 %weight_send.6 = (bf16[1,80,2944]{2,1,0:T(8,128)(2,1)S(1)}, f32[8,128]{1,0:T(8,128)S(1)}) custom-call(f32[8,128]{1,0:T(8,128)S(1)} %get-tuple-element.87.refs_0_, bf16[720,1024]{1,0:T(8,128)(2,1)S(1)} %get-tuple-element.73.refs_1_, bf16[720,1024]{1,0:T(8,128)(2,1)S(1)} %get-tuple-element.85.refs_2_, bf16[320,1024]{1,0:T(8,128)(2,1)S(1)} %get-tuple-element.88.refs_3_.refs_5_, ...), custom_call_target="tpu_custom_call" | custom-call | flops 20000000000 | bytes 1024 | tf_op jit(solution)/shard_map/weight_send/pallas_call | solution.py:400
  33.3 0.5 collective-permute-start.12
  33.8 2.6 %weight_keep.4 = (f32[1,80,2944]{2,1,0:T(8,128)S(1)}, f32[1,80,2944]{2,1,0:T(8,128)S(1)}, f32[8,128]{1,0:T(8,128)S(1)}) custom-call(f32[8,128]{1,0:T(8,128)S(1)} %get-tuple-element.89.refs_0_, bf16[720,1024]{1,0:T(8,128)(2,1)S(1)} %get-tuple-element.90.refs_1_, bf16[720,1024]{1,0:T(8,128)(2,1)S(1)} %get-tuple-element.91.refs_2_, ...), custom_call_target="tpu_custom_call" | custom-call | flops 24999999488 | bytes 1024 | tf_op jit(solution)/shard_map/weight_keep/pallas_call | solution.py:400
  36.5 2.7 %collective-permute-done.7.refs_2_ = bf16[2,656,256]{2,1,0:T(8,128)(2,1)S(1)} collective-permute-done((bf16[2,656,256]{2,1,0:T(8,128)(2,1)S(1)}, bf16[2,656,256]{2,1,0:T(8,128)(2,1)S(1)}, u32[]{:S(2)}, u32[]{:S(2)}) %collective-permute-start.7) | collective-permute-done | bytes 671776 | tf_op jit(solution)/shard_map/ppermute | solution.py:385
  39.2 0.7 frame_second.2
  39.9 0.8 collective-permute-start.15
  40.7 0.3 weight_end.3
  41.1 5.7 %frame_part.3 = (bf16[2,656,256]{2,1,0:T(8,128)(2,1)S(1)}, f32[2,640,256]{2,1,0:T(8,128)S(1)}, f32[8,128]{1,0:T(8,128)S(1)}) custom-call(f32[8,128]{1,0:T(8,128)S(1)} %get-tuple-element.99.refs_0_, bf16[2880,1280]{1,0:T(8,128)(2,1)S(1)} %get-tuple-element.78.refs_1_, bf16[4,320,256]{2,1,0:T(8,128)(2,1)S(1)} %copy-done.3), custom_call_target="tpu_custom_call" | custom-call | flops 42500001792 | bytes 1024 | tf_op jit(solution)/shard_map/frame_part/pallas_call | solution.py:400
  46.8 1.4 %collective-permute-start.14 = (bf16[2,656,256]{2,1,0:T(8,128)(2,1)S(1)}, bf16[2,656,256]{2,1,0:T(8,128)(2,1)S(1)}, u32[]{:S(2)}, u32[]{:S(2)}) collective-permute-start(bf16[2,656,256]{2,1,0:T(8,128)(2,1)S(1)} %get-tuple-element.114), channel_id=1, source_target_pairs={{0,2},{1,3},{2,0},{3,1},{4,6},{5,7},{6,4},{7,5},{8,10},{9,11},{10,... | collective-permute-start | bytes 2015240 | tf_op jit(solution)/shard_map/ppermute | solution.py:385
  48.2 0.6 weight_second.5
  48.8 2.7 %collective-permute-start.13 = (bf16[80,1536]{1,0:T(8,128)(2,1)S(1)}, bf16[80,1536]{1,0:T(8,128)(2,1)S(1)}, u32[]{:S(2)}, u32[]{:S(2)}) collective-permute-start(bf16[80,1536]{1,0:T(8,128)(2,1)S(1)} %get-tuple-element.111), channel_id=1, source_target_pairs={{0,16},{4,20},{8,24},{12,28},{16,0},{20,4},{24,8},{28,12},{1,17},{... | collective-permute-start | bytes 737288 | tf_op jit(solution)/shard_map/ppermute | solution.py:381
  51.5 2.1 %weight_send.7 = (bf16[1,80,2944]{2,1,0:T(8,128)(2,1)S(1)}, f32[8,128]{1,0:T(8,128)S(1)}) custom-call(f32[8,128]{1,0:T(8,128)S(1)} %get-tuple-element.103.refs_0_, bf16[720,1024]{1,0:T(8,128)(2,1)S(1)} %get-tuple-element.73.refs_1_, bf16[720,1024]{1,0:T(8,128)(2,1)S(1)} %get-tuple-element.85.refs_2_, bf16[320,1024]{1,0:T(8,128)(2,1)S(1)} %get-tuple-element.104.refs_3_, ...), custom_call_target="tpu_custom_call" | custom-call | flops 20000000000 | bytes 1024 | tf_op jit(solution)/shard_map/weight_send/pallas_call | solution.py:400
  53.6 0.9 collective-permute-start.16
  54.4 1.7 %weight_keep.5 = (f32[1,80,2944]{2,1,0:T(8,128)S(1)}, f32[8,128]{1,0:T(8,128)S(1)}) custom-call(f32[8,128]{1,0:T(8,128)S(1)} %get-tuple-element.105.refs_0_, bf16[720,1024]{1,0:T(8,128)(2,1)S(1)} %get-tuple-element.90.refs_1_, bf16[720,1024]{1,0:T(8,128)(2,1)S(1)} %get-tuple-element.91.refs_2_, bf16[320,1024]{1,0:T(8,128)(2,1)S(1)} %get-tuple-element.104.refs_3_, ...), custom_call_target="tpu_custom_call" | custom-call | flops 20000000000 | bytes 1024 | tf_op jit(solution)/shard_map/weight_keep/pallas_call | solution.py:400
  56.2 4.5 %collective-permute-done.12.refs_2_ = bf16[1,80,2944]{2,1,0:T(8,128)(2,1)S(1)} collective-permute-done((bf16[1,80,2944]{2,1,0:T(8,128)(2,1)S(1)}, bf16[1,80,2944]{2,1,0:T(8,128)(2,1)S(1)}, u32[]{:S(2)}, u32[]{:S(2)}) %collective-permute-start.12) | collective-permute-done | bytes 471072 | tf_op jit(solution)/shard_map/ppermute | solution.py:381
  60.7 0.6 weight_second.6
  61.4 2.5 %collective-permute-done.13.refs_2_ = bf16[80,1536]{1,0:T(8,128)(2,1)S(1)} collective-permute-done((bf16[80,1536]{1,0:T(8,128)(2,1)S(1)}, bf16[80,1536]{1,0:T(8,128)(2,1)S(1)}, u32[]{:S(2)}, u32[]{:S(2)}) %collective-permute-start.13) | collective-permute-done | bytes 245792 | tf_op jit(solution)/shard_map/ppermute | solution.py:381
  64.4 0.7 frame_second.3
  65.1 0.6 collective-permute-start.17
  65.7 1.1 %weight_last.2 = (f32[40,11520]{1,0:T(8,128)}, f32[8,128]{1,0:T(8,128)S(1)}) custom-call(f32[8,128]{1,0:T(8,128)S(1)} %get-tuple-element.115.refs_0_, f32[40,2944]{1,0:T(8,128)S(1)} %get-tuple-element.116.refs_1_, f32[40,2944]{1,0:T(8,128)S(1)} %get-tuple-element.117.refs_2_), custom_call_target="tpu_custom_call" | custom-call | flops 12000000000 | bytes 1024 | tf_op jit(solution)/shard_map/weight_last/pallas_call | solution.py:400
  66.8 0.9 %frame_last.2 = (bf16[4,320,256]{2,1,0:T(8,128)(2,1)}, f32[8,128]{1,0:T(8,128)S(1)}) custom-call(f32[8,128]{1,0:T(8,128)S(1)} %get-tuple-element.118.refs_0_, f32[640,256]{1,0:T(8,128)S(1)} %get-tuple-element.119.refs_1_, bf16[656,256]{1,0:T(8,128)(2,1)S(1)} %collective-permute-done.15.refs_2_), custom_call_target="tpu_custom_call" | custom-call | flops 5000000000 | bytes 1024 | tf_op jit(solution)/shard_map/frame_last/pallas_call | solution.py:400
  67.8 8.8 %collective-permute-done.16.refs_2_ = bf16[1,80,2944]{2,1,0:T(8,128)(2,1)S(1)} collective-permute-done((bf16[1,80,2944]{2,1,0:T(8,128)(2,1)S(1)}, bf16[1,80,2944]{2,1,0:T(8,128)(2,1)S(1)}, u32[]{:S(2)}, u32[]{:S(2)}) %collective-permute-start.16) | collective-permute-done | bytes 471072 | tf_op jit(solution)/shard_map/ppermute | solution.py:381
  76.6 0.6 weight_second.7
  77.3 0.5 collective-permute-start.19
  77.8 10.8 %response.1 = (bf16[4,320,256]{2,1,0:T(8,128)(2,1)}, f32[8,128]{1,0:T(8,128)S(1)}) custom-call(f32[8,128]{1,0:T(8,128)S(1)} %get-tuple-element.124.refs_0_, bf16[2880,1280]{1,0:T(8,128)(2,1)S(1)} %get-tuple-element.78.refs_1_, f32[320]{0:T(512)S(1)} %copy-done.4, bf16[4,320,256]{2,1,0:T(8,128)(2,1)S(1)} %get-tuple-element.125.refs_3_, ...), custom_call_target="tpu_custom_call" | custom-call | flops 54999998464 | bytes 1024 | tf_op jit(solution)/shard_map/response/pallas_call | solution.py:400
  88.5 0.9 %frame_last.3 = (bf16[4,320,256]{2,1,0:T(8,128)(2,1)}, f32[8,128]{1,0:T(8,128)S(1)}) custom-call(f32[8,128]{1,0:T(8,128)S(1)} %get-tuple-element.127.refs_0_, f32[640,256]{1,0:T(8,128)S(1)} %get-tuple-element.128.refs_1_, bf16[656,256]{1,0:T(8,128)(2,1)S(1)} %collective-permute-done.17.refs_2_, ...), custom_call_target="tpu_custom_call", output_to_operand_aliasing={{0}: (3, {})} | custom-call | flops 5000000000 | bytes 1024 | tf_op jit(solution)/shard_map/frame_last/pallas_call | solution.py:400
  89.5 0.3 weight_end.5
  89.8 1.8 %weight_last.3 = (f32[40,11520]{1,0:T(8,128)}, f32[8,128]{1,0:T(8,128)}) custom-call(f32[8,128]{1,0:T(8,128)S(1)} %get-tuple-element.135.refs_0_, f32[40,2944]{1,0:T(8,128)S(1)} %get-tuple-element.136.refs_1_, f32[40,2944]{1,0:T(8,128)S(1)} %get-tuple-element.137.refs_2_, ...), custom_call_target="tpu_custom_call", output_to_operand_aliasing={{0}: (4, {})} | custom-call | flops 12000000000 | bytes 1024 | tf_op jit(solution)/shard_map/weight_last/pallas_call | solution.py:400
  (34 shorter events, 0.9 us)
Async XLA Ops:
  0.6 7.5 %collective-permute-start.1 = (bf16[4,320,256]{2,1,0:T(8,128)(2,1)}, bf16[4,320,256]{2,1,0:T(8,128)(2,1)S(1)}, u32[]{:S(2)}, u32[]{:S(2)}) collective-permute-start(bf16[4,320,256]{2,1,0:T(8,128)(2,1)} %refs_5_.2), channel_id=1, source_target_pairs={{0,4},{4,0},{8,12},{12,8},{16,20},{20,16},{24,28},{28,24},{1,5},{5... | collective-permute-start | bytes 1966088 | tf_op jit(solution)/shard_map/ppermute | solution.py:377
  1.1 20.0 %collective-permute-start.2 = (bf16[4,320,256]{2,1,0:T(8,128)(2,1)}, bf16[4,320,256]{2,1,0:T(8,128)(2,1)S(1)}, u32[]{:S(2)}, u32[]{:S(2)}) collective-permute-start(bf16[4,320,256]{2,1,0:T(8,128)(2,1)} %refs_5_.2), channel_id=1, source_target_pairs={{0,1},{1,0},{2,3},{3,2},{4,5},{5,4},{6,7},{7,6},{8,9},{9,8},{10,11... | collective-permute-start | bytes 1966088 | tf_op jit(solution)/shard_map/ppermute | solution.py:385
  3.7 17.8 %collective-permute-start.3 = (bf16[4,320,256]{2,1,0:T(8,128)(2,1)}, bf16[4,320,256]{2,1,0:T(8,128)(2,1)S(1)}, u32[]{:S(2)}, u32[]{:S(2)}) collective-permute-start(bf16[4,320,256]{2,1,0:T(8,128)(2,1)} %refs_5_.2), channel_id=1, source_target_pairs={{0,2},{1,3},{2,0},{3,1},{4,6},{5,7},{6,4},{7,5},{8,10},{9,11},{10,... | collective-permute-start | bytes 1966088 | tf_op jit(solution)/shard_map/ppermute | solution.py:385
  5.2 2.9 %collective-permute-start = (bf16[4,320,256]{2,1,0:T(8,128)(2,1)}, bf16[4,320,256]{2,1,0:T(8,128)(2,1)S(1)}, u32[]{:S(2)}, u32[]{:S(2)}) collective-permute-start(bf16[4,320,256]{2,1,0:T(8,128)(2,1)} %refs_2_.4), channel_id=1, source_target_pairs={{0,4},{4,0},{8,12},{12,8},{16,20},{20,16},{24,28},{28,24},{1,5},{5... | collective-permute-start | bytes 1966088 | tf_op jit(solution)/shard_map/ppermute | solution.py:377
  5.2 1.1 %copy-start = (bf16[4,320,256]{2,1,0:T(8,128)(2,1)S(1)}, bf16[4,320,256]{2,1,0:T(8,128)(2,1)}, u32[]{:S(2)}) copy-start(bf16[4,320,256]{2,1,0:T(8,128)(2,1)} %refs_5_.2) | copy-start | bytes 1966084
  6.4 1.1 %copy-start.2 = (bf16[4,320,256]{2,1,0:T(8,128)(2,1)S(1)}, bf16[4,320,256]{2,1,0:T(8,128)(2,1)}, u32[]{:S(2)}) copy-start(bf16[4,320,256]{2,1,0:T(8,128)(2,1)} %refs_2_.4) | copy-start | bytes 1966084
  7.4 1.1 %copy-start.1 = (bf16[4,320,256]{2,1,0:T(8,128)(2,1)S(1)}, bf16[4,320,256]{2,1,0:T(8,128)(2,1)}, u32[]{:S(2)}) copy-start(bf16[4,320,256]{2,1,0:T(8,128)(2,1)} %refs_5_.2) | copy-start | bytes 1966084
  7.4 5.2 %slice-start = ((s8[7372800]{0:T(1024)(128)(4,1)}), s8[4194304]{0:T(1024)(128)(4,1)S(1)}, s32[]{:S(2)}) async-start(s8[7372800]{0:T(1024)(128)(4,1)} %bitcast), calls=%async_computation | async-start | bytes 8388608
  8.5 4.1 %slice-start.1 = ((s8[7372800]{0:T(1024)(128)(4,1)}), s8[3178496]{0:T(1024)(128)(4,1)S(1)}, s32[]{:S(2)}) async-start(s8[7372800]{0:T(1024)(128)(4,1)} %bitcast), calls=%async_computation.1 | async-start | bytes 6356992
  8.5 4.1 %copy-start.3 = (bf16[4,320,256]{2,1,0:T(8,128)(2,1)S(1)}, bf16[4,320,256]{2,1,0:T(8,128)(2,1)}, u32[]{:S(2)}) copy-start(bf16[4,320,256]{2,1,0:T(8,128)(2,1)} %refs_2_.4) | copy-start | bytes 1966084
  11.0 13.2 %collective-permute-start.4 = (bf16[1,80,2944]{2,1,0:T(8,128)(2,1)S(1)}, bf16[1,80,2944]{2,1,0:T(8,128)(2,1)S(1)}, u32[]{:S(2)}, u32[]{:S(2)}) collective-permute-start(bf16[1,80,2944]{2,1,0:T(8,128)(2,1)S(1)} %get-tuple-element.83), channel_id=1, source_target_pairs={{0,8},{4,12},{8,0},{12,4},{16,24},{20,28},{24,16},{28,20},{1,9},{5... | collective-permute-start | bytes 1413128 | tf_op jit(solution)/shard_map/ppermute | solution.py:381
  21.3 6.2 %collective-permute-start.5 = (bf16[320,1024]{1,0:T(8,128)(2,1)S(1)}, bf16[320,1024]{1,0:T(8,128)(2,1)S(1)}, u32[]{:S(2)}, u32[]{:S(2)}) collective-permute-start(bf16[320,1024]{1,0:T(8,128)(2,1)S(1)} %get-tuple-element.86.refs_3_), channel_id=1, source_target_pairs={{0,4},{4,0},{8,12},{12,8},{16,20},{20,16},{24,28},{28,24},{1,5},{5... | collective-permute-start | bytes 1966088 | tf_op jit(solution)/shard_map/ppermute | solution.py:377
  21.6 9.6 %collective-permute-start.6 = (bf16[320,1024]{1,0:T(8,128)(2,1)S(1)}, bf16[320,1024]{1,0:T(8,128)(2,1)S(1)}, u32[]{:S(2)}, u32[]{:S(2)}) collective-permute-start(bf16[320,1024]{1,0:T(8,128)(2,1)S(1)} %get-tuple-element.88.refs_3_.refs_5_), channel_id=1, source_target_pairs={{0,4},{4,0},{8,12},{12,8},{16,20},{20,16},{24,28},{28,24},{1,5},{5... | collective-permute-start | bytes 1966088 | tf_op jit(solution)/shard_map/ppermute | solution.py:377
  22.0 17.2 %collective-permute-start.7 = (bf16[2,656,256]{2,1,0:T(8,128)(2,1)S(1)}, bf16[2,656,256]{2,1,0:T(8,128)(2,1)S(1)}, u32[]{:S(2)}, u32[]{:S(2)}) collective-permute-start(bf16[2,656,256]{2,1,0:T(8,128)(2,1)S(1)} %get-tuple-element.94), channel_id=1, source_target_pairs={{0,1},{1,0},{2,3},{3,2},{4,5},{5,4},{6,7},{7,6},{8,9},{9,8},{10,11... | collective-permute-start | bytes 2015240 | tf_op jit(solution)/shard_map/ppermute | solution.py:385
  22.5 18.4 %collective-permute-start.9 = (bf16[4,320,256]{2,1,0:T(8,128)(2,1)S(1)}, bf16[4,320,256]{2,1,0:T(8,128)(2,1)S(1)}, u32[]{:S(2)}, u32[]{:S(2)}) collective-permute-start(bf16[4,320,256]{2,1,0:T(8,128)(2,1)S(1)} %collective-permute-done.2.refs_1_.refs_4_), channel_id=1, source_target_pairs={{0,2},{1,3},{2,0},{3,1},{4,6},{5,7},{6,4},{7,5},{8,10},{9,11},{10,... | collective-permute-start | bytes 1966088 | tf_op jit(solution)/shard_map/ppermute | solution.py:385
  24.8 15.8 %collective-permute-start.8 = (bf16[80,1536]{1,0:T(8,128)(2,1)S(1)}, bf16[80,1536]{1,0:T(8,128)(2,1)S(1)}, u32[]{:S(2)}, u32[]{:S(2)}) collective-permute-start(bf16[80,1536]{1,0:T(8,128)(2,1)S(1)} %get-tuple-element.97), channel_id=1, source_target_pairs={{0,16},{4,20},{8,24},{12,28},{16,0},{20,4},{24,8},{28,12},{1,17},{... | collective-permute-start | bytes 737288 | tf_op jit(solution)/shard_map/ppermute | solution.py:381
  29.6 18.6 %collective-permute-start.10 = (bf16[1,80,2944]{2,1,0:T(8,128)(2,1)S(1)}, bf16[1,80,2944]{2,1,0:T(8,128)(2,1)S(1)}, u32[]{:S(2)}, u32[]{:S(2)}) collective-permute-start(bf16[1,80,2944]{2,1,0:T(8,128)(2,1)S(1)} %get-tuple-element.102), channel_id=1, source_target_pairs={{0,8},{4,12},{8,0},{12,4},{16,24},{20,28},{24,16},{28,20},{1,9},{5... | collective-permute-start | bytes 1413128 | tf_op jit(solution)/shard_map/ppermute | solution.py:381
  33.3 27.4 %collective-permute-start.12 = (bf16[1,80,2944]{2,1,0:T(8,128)(2,1)S(1)}, bf16[1,80,2944]{2,1,0:T(8,128)(2,1)S(1)}, u32[]{:S(2)}, u32[]{:S(2)}) collective-permute-start(bf16[1,80,2944]{2,1,0:T(8,128)(2,1)S(1)} %get-tuple-element.108), channel_id=1, source_target_pairs={{0,8},{4,12},{8,0},{12,4},{16,24},{20,28},{24,16},{28,20},{1,9},{5... | collective-permute-start | bytes 1413128 | tf_op jit(solution)/shard_map/ppermute | solution.py:381
  39.9 27.0 %collective-permute-start.15 = (bf16[656,256]{1,0:T(8,128)(2,1)S(1)}, bf16[656,256]{1,0:T(8,128)(2,1)S(1)}, u32[]{:S(2)}, u32[]{:S(2)}) collective-permute-start(bf16[656,256]{1,0:T(8,128)(2,1)S(1)} %get-tuple-element.120), channel_id=1, source_target_pairs={{0,2},{1,3},{2,0},{3,1},{4,6},{5,7},{6,4},{7,5},{8,10},{9,11},{10,... | collective-permute-start | bytes 1007624 | tf_op jit(solution)/shard_map/ppermute | solution.py:385
  41.0 10.5 %collective-permute-start.11 = (bf16[320,1024]{1,0:T(8,128)(2,1)S(1)}, bf16[320,1024]{1,0:T(8,128)(2,1)S(1)}, u32[]{:S(2)}, u32[]{:S(2)}) collective-permute-start(bf16[320,1024]{1,0:T(8,128)(2,1)S(1)} %get-tuple-element.104.refs_3_), channel_id=1, source_target_pairs={{0,4},{4,0},{8,12},{12,8},{16,20},{20,16},{24,28},{28,24},{1,5},{5... | collective-permute-start | bytes 1966088 | tf_op jit(solution)/shard_map/ppermute | solution.py:377
  46.8 17.5 %collective-permute-start.14 = (bf16[2,656,256]{2,1,0:T(8,128)(2,1)S(1)}, bf16[2,656,256]{2,1,0:T(8,128)(2,1)S(1)}, u32[]{:S(2)}, u32[]{:S(2)}) collective-permute-start(bf16[2,656,256]{2,1,0:T(8,128)(2,1)S(1)} %get-tuple-element.114), channel_id=1, source_target_pairs={{0,2},{1,3},{2,0},{3,1},{4,6},{5,7},{6,4},{7,5},{8,10},{9,11},{10,... | collective-permute-start | bytes 2015240 | tf_op jit(solution)/shard_map/ppermute | solution.py:385
  48.8 15.1 %collective-permute-start.13 = (bf16[80,1536]{1,0:T(8,128)(2,1)S(1)}, bf16[80,1536]{1,0:T(8,128)(2,1)S(1)}, u32[]{:S(2)}, u32[]{:S(2)}) collective-permute-start(bf16[80,1536]{1,0:T(8,128)(2,1)S(1)} %get-tuple-element.111), channel_id=1, source_target_pairs={{0,16},{4,20},{8,24},{12,28},{16,0},{20,4},{24,8},{28,12},{1,17},{... | collective-permute-start | bytes 737288 | tf_op jit(solution)/shard_map/ppermute | solution.py:381
  53.6 23.0 %collective-permute-start.16 = (bf16[1,80,2944]{2,1,0:T(8,128)(2,1)S(1)}, bf16[1,80,2944]{2,1,0:T(8,128)(2,1)S(1)}, u32[]{:S(2)}, u32[]{:S(2)}) collective-permute-start(bf16[1,80,2944]{2,1,0:T(8,128)(2,1)S(1)} %get-tuple-element.123), channel_id=1, source_target_pairs={{0,8},{4,12},{8,0},{12,4},{16,24},{20,28},{24,16},{28,20},{1,9},{5... | collective-permute-start | bytes 1413128 | tf_op jit(solution)/shard_map/ppermute | solution.py:381
  61.3 28.2 %collective-permute-start.18 = (bf16[80,1536]{1,0:T(8,128)(2,1)S(1)}, bf16[80,1536]{1,0:T(8,128)(2,1)S(1)}, u32[]{:S(2)}, u32[]{:S(2)}) collective-permute-start(bf16[80,1536]{1,0:T(8,128)(2,1)S(1)} %get-tuple-element.134), channel_id=1, source_target_pairs={{0,16},{4,20},{8,24},{12,28},{16,0},{20,4},{24,8},{28,12},{1,17},{... | collective-permute-start | bytes 737288 | tf_op jit(solution)/shard_map/ppermute | solution.py:381
  65.1 23.4 %collective-permute-start.17 = (bf16[656,256]{1,0:T(8,128)(2,1)S(1)}, bf16[656,256]{1,0:T(8,128)(2,1)S(1)}, u32[]{:S(2)}, u32[]{:S(2)}) collective-permute-start(bf16[656,256]{1,0:T(8,128)(2,1)S(1)} %get-tuple-element.129), channel_id=1, source_target_pairs={{0,1},{1,0},{2,3},{3,2},{4,5},{5,4},{6,7},{7,6},{8,9},{9,8},{10,11... | collective-permute-start | bytes 1007624 | tf_op jit(solution)/shard_map/ppermute | solution.py:385
  76.6 1.2 %copy-start.4 = (f32[320]{0:T(512)S(1)}, f32[320]{0:T(512)}, u32[]{:S(2)}) copy-start(f32[320]{0:T(512)} %refs_2_.5) | copy-start | bytes 3844
  77.3 12.5 %collective-permute-start.19 = (bf16[80,1536]{1,0:T(8,128)(2,1)S(1)}, bf16[80,1536]{1,0:T(8,128)(2,1)S(1)}, u32[]{:S(2)}, u32[]{:S(2)}) collective-permute-start(bf16[80,1536]{1,0:T(8,128)(2,1)S(1)} %get-tuple-element.138), channel_id=1, source_target_pairs={{0,16},{4,20},{8,24},{12,28},{16,0},{20,4},{24,8},{28,12},{1,17},{... | collective-permute-start | bytes 737288 | tf_op jit(solution)/shard_map/ppermute | solution.py:381

commit v3 on v2

--- a/solution.py
+++ b/solution.py
@@ -17,7 +17,7 @@
 HBM = pl.BlockSpec(memory_space=pltpu.HBM)
 SPAN = 125.0
 RATE = 5e8
-ROOM = dict(pre=8, a=12, fx=18, gx=4, gy=4, gd=4, ka=20, a2=8, b=10, fy=18, c=10, kb=18, f2x=8, b2=8, kd=10, c2=8, d=10, f2y=8, wab=10, flx=6, d2=8, resp=18, fly=6, wcd=10, ea=8, eb=8, ec=8)
+ROOM = dict(pre=61, a=12, fx=18, gx=4, gy=4, gd=4, ka=20, a2=8, b=10, fy=18, c=10, kb=18, f2x=8, b2=8, kd=10, c2=8, d=10, f2y=8, wab=10, flx=6, d2=8, resp=18, fly=6, wcd=10, ea=8, eb=8, ec=8)
 ORDER = ("pre", "a", "ka", "fx", "gx", "gy", "a2", "b", "c", "kb", "f2x", "ea", "gd", "fy", "b2", "d", "kd", "c2", "eb", "f2y", "wab", "flx", "d2", "resp", "fly", "ec", "wcd")
 COST = dict(pre=20, a=45, ka=40, fx=85, gx=10, gy=10, gd=10, b=40, c=40, d=40, kb=50, kd=40, fy=85, a2=7, b2=7, c2=7, resp=110, f2x=12, f2y=12, d2=7, flx=10, fly=10, wab=24, wcd=24, ea=7, eb=7, ec=7)
 
@@ -173,10 +173,9 @@
     frames_in_a_row(x_ref, xs_ref)
 
 
-def first_send_kernel(width, cs_ref, xs_ref, cot2_ref, x2_ref, x_ref, send_ref, cs2_ref, xs2_ref, copy_ref, f_ref):
+def first_send_kernel(width, cs_ref, xs_ref, cot2_ref, x2_ref, send_ref, cs2_ref, xs2_ref, f_ref):
     shifted_rows(True, cot2_ref, cs2_ref)
     frames_in_a_row(x2_ref, xs2_ref)
-    copy_ref[...] = x_ref[...]
     weight_sums(width, (cs_ref, cs2_ref), (xs_ref, xs2_ref), f_ref)
     put_rows_coded(send_ref, (0,), f_ref[0], width)
 
@@ -525,7 +524,7 @@
 
     cot2 = swap_core(cotangent)
     own2 = swap_core(frames)
-    near = {"x": swap_block(frames, 1)}
+    near = {"x": swap_block(frames, 1), "y": swap_block(frames, 2)}
 
     t = None
     send, keep, recv, xs, cs = {}, {}, {}, {}, {}
@@ -534,18 +533,17 @@
         if step == "pre":
             cs_own, xs_own, t = simple(own_rows_kernel, "own_rows", step, t, (cotangent, frames), (row_cs, row_xs))
         elif step == "a":
-            send["a"], cs2, xs2, again, t = simple(
+            send["a"], cs2, xs2, t = simple(
                 functools.partial(first_send_kernel, width),
                 "weight_send",
                 step,
                 t,
-                (cs_own, xs_own, cot2, own2, frames),
-                (code, row_cs, row_xs, shape((nf, ch, cells), BF16)),
+                (cs_own, xs_own, cot2, own2),
+                (code, row_cs, row_xs),
                 [pltpu.VMEM((1, half, padded), F32)],
             )
             cs["far"], xs["a"] = (cs_own, cs2), (xs_own, xs2)
             recv["a"] = swap_layer(send["a"], 1)
-            near["y"] = swap_block(frames, 2)
         elif step in ("gx", "gy", "gd"):
             k = step[1]
             row, t = simple(frames_in_a_row, "rows", step, t, (near[k],), (row_xs,))
@@ -597,7 +595,7 @@
         elif step == "fly":
             frame_grad, t = last_frame(step, t, 2, (fkeep[4], frecv[4]), fheld)
         elif step == "resp":
-            response, t = respond(step, t, again, near["x"], near["y"], near["d"])
+            response, t = respond(step, t, frames, near["x"], near["y"], near["d"])
         elif step in ("ea", "eb", "ec"):
             k = step[1] + "2"
             keep[step], t = simple(

time: 92 us -> 95.8 us (1.041)
  Pallas kernels: 48.5 us -> 51 us
    pallas_call x27, Pallas kernels: 48.5 us -> 51 us  [run(): pl.pallas_call(body, out_shape=(*outs, shape((8, 128), F32)), in_specs=[m...]
    unnamed x14 -> x18, local copies, waits for them, and re-layouts: 2.59 us -> 3.16 us
  transfers between devices with their start and end apart: 20 -> 20, of which waited for: 6 -> 5; matrix products, arithmetic and copies ran while one was open for 0% -> 0% of each run, Pallas kernels for 51% -> 51%
where the time goes in v3:
time: 95.8 us; the launch traced here: 95.6 us
  Pallas kernels  51 us (53%)
  starting transfers between devices  20.7 us (22%)
  waiting for transfers between devices  19.6 us (20%)
  local copies, waits for them, and re-layouts  3.16 us (3%)
  between operations  1.09 us (1%)
    pallas_call x27, Pallas kernels, run(): pl.pallas_call(body, out_shape=(*outs, shape((8, 128), F32)), in_specs=[m...  51 us
    ppermute x8, waiting for transfers between devices, swap_layer(): return lax.ppermute(x, 'dp', [(d, d ^ 2 * mask) for d in range(8)])  16.9 us
    ppermute x8, starting transfers between devices, swap_layer(): return lax.ppermute(x, 'dp', [(d, d ^ 2 * mask) for d in range(8)])  11.5 us
    ppermute x7, starting transfers between devices, swap_block(): return lax.ppermute(x, 'blk', [(d, d ^ mask) for d in range(4)])  7.94 us
    unnamed x18, local copies, waits for them, and re-layouts  3.16 us
    ppermute x7, waiting for transfers between devices, swap_block(): return lax.ppermute(x, 'blk', [(d, d ^ mask) for d in range(4)])  2.7 us
  transfers between devices with their start and end apart: 20, of which 5 were waited for; matrix products, arithmetic and copies ran while one was open for 0% of the time, Pallas kernels for 51%

profile of v3, /device:TPU:0, one launch (start us, length us, event | category | flops | bytes accessed | tf_op | source)
XLA Modules:
  0.0 95.6 jit_solution(813585437159541541)
XLA Ops:
  0.6 0.5 collective-permute-start.1
  1.1 2.6 %collective-permute-start.2 = (bf16[4,320,256]{2,1,0:T(8,128)(2,1)}, bf16[4,320,256]{2,1,0:T(8,128)(2,1)S(1)}, u32[]{:S(2)}, u32[]{:S(2)}) collective-permute-start(bf16[4,320,256]{2,1,0:T(8,128)(2,1)} %refs_3_.1), channel_id=1, source_target_pairs={{0,1},{1,0},{2,3},{3,2},{4,5},{5,4},{6,7},{7,6},{8,9},{9,8},{10,11... | collective-permute-start | bytes 1966088 | tf_op jit(solution)/shard_map/ppermute | solution.py:384
  3.7 1.5 %collective-permute-start.3 = (bf16[4,320,256]{2,1,0:T(8,128)(2,1)}, bf16[4,320,256]{2,1,0:T(8,128)(2,1)S(1)}, u32[]{:S(2)}, u32[]{:S(2)}) collective-permute-start(bf16[4,320,256]{2,1,0:T(8,128)(2,1)} %refs_3_.1), channel_id=1, source_target_pairs={{0,2},{1,3},{2,0},{3,1},{4,6},{5,7},{6,4},{7,5},{8,10},{9,11},{10,... | collective-permute-start | bytes 1966088 | tf_op jit(solution)/shard_map/ppermute | solution.py:384
  5.2 3.2 %own_rows.1 = (bf16[720,1024]{1,0:T(8,128)(2,1)}, bf16[320,1024]{1,0:T(8,128)(2,1)}, f32[8,128]{1,0:T(8,128)}) custom-call(bf16[4,320,256]{2,1,0:T(8,128)(2,1)} %refs_2_.4, bf16[4,320,256]{2,1,0:T(8,128)(2,1)} %refs_3_.1), custom_call_target="tpu_custom_call" | custom-call | flops 10000000000 | bytes 1024 | tf_op jit(solution)/shard_map/own_rows/pallas_call | solution.py:399
  8.5 1.4 %copy-done.4 = bf16[720,1024]{1,0:T(8,128)(2,1)S(1)} copy-done((bf16[720,1024]{1,0:T(8,128)(2,1)S(1)}, bf16[720,1024]{1,0:T(8,128)(2,1)}, u32[]{:S(2)}) %copy-start.4) | copy-done | bytes 1474584
  9.9 1.1 %copy-done.6 = bf16[320,1024]{1,0:T(8,128)(2,1)S(1)} copy-done((bf16[320,1024]{1,0:T(8,128)(2,1)S(1)}, bf16[320,1024]{1,0:T(8,128)(2,1)}, u32[]{:S(2)}) %copy-start.6) | copy-done | bytes 655384
  10.9 0.7 copy-done.8
  11.6 2.4 %weight_send.4 = (bf16[1,80,2944]{2,1,0:T(8,128)(2,1)S(1)}, bf16[720,1024]{1,0:T(8,128)(2,1)S(1)}, bf16[320,1024]{1,0:T(8,128)(2,1)S(1)}, f32[8,128]{1,0:T(8,128)S(1)}) custom-call(f32[8,128]{1,0:T(8,128)S(1)} %copy-done.8, bf16[720,1024]{1,0:T(8,128)(2,1)S(1)} %copy-done.4, bf16[320,1024]{1,0:T(8,128)(2,1)S(1)} %copy-done.6, ...), custom_call_target="tpu_custom_call" | custom-call | flops 22499999744 | bytes 1024 | tf_op jit(solution)/shard_map/weight_send/pallas_call | solution.py:399
  14.1 1.6 %collective-permute-start.4 = (bf16[1,80,2944]{2,1,0:T(8,128)(2,1)S(1)}, bf16[1,80,2944]{2,1,0:T(8,128)(2,1)S(1)}, u32[]{:S(2)}, u32[]{:S(2)}) collective-permute-start(bf16[1,80,2944]{2,1,0:T(8,128)(2,1)S(1)} %get-tuple-element.82), channel_id=1, source_target_pairs={{0,8},{4,12},{8,0},{12,4},{16,24},{20,28},{24,16},{28,20},{1,9},{5... | collective-permute-start | bytes 1413128 | tf_op jit(solution)/shard_map/ppermute | solution.py:380
  15.7 2.8 %weight_keep.3 = (f32[1,80,2944]{2,1,0:T(8,128)S(1)}, bf16[720,1024]{1,0:T(8,128)(2,1)S(1)}, bf16[720,1024]{1,0:T(8,128)(2,1)S(1)}, bf16[2880,1280]{1,0:T(8,128)(2,1)S(1)}, f32[8,128]{1,0:T(8,128)S(1)}) custom-call(f32[8,128]{1,0:T(8,128)S(1)} %get-tuple-element.74.refs_0_, bf16[4,320,256]{2,1,0:T(8,128)(2,1)S(1)} %copy-done.1, ...), custom_call_target="tpu_custom_call" | custom-call | flops 20000000000 | bytes 1024 | tf_op jit(solution)/shard_map/weight_keep/pallas_call | solution.py:399
  18.5 5.7 %frame_part.2 = (bf16[2,656,256]{2,1,0:T(8,128)(2,1)S(1)}, f32[2,640,256]{2,1,0:T(8,128)S(1)}, f32[8,128]{1,0:T(8,128)S(1)}) custom-call(f32[8,128]{1,0:T(8,128)S(1)} %get-tuple-element.76.refs_0_, bf16[2880,1280]{1,0:T(8,128)(2,1)S(1)} %get-tuple-element.77.refs_1_, bf16[4,320,256]{2,1,0:T(8,128)(2,1)S(1)} %copy-done.1), custom_call_target="tpu_custom_call" | custom-call | flops 42500001792 | bytes 1024 | tf_op jit(solution)/shard_map/frame_part/pallas_call | solution.py:399
  24.3 0.3 collective-permute-start.5
  24.7 0.3 collective-permute-start.6
  25.1 0.5 collective-permute-start.7
  25.6 0.5 collective-permute-start.9
  26.1 1.2 %collective-permute-done.4.refs_2_ = bf16[1,80,2944]{2,1,0:T(8,128)(2,1)S(1)} collective-permute-done((bf16[1,80,2944]{2,1,0:T(8,128)(2,1)S(1)}, bf16[1,80,2944]{2,1,0:T(8,128)(2,1)S(1)}, u32[]{:S(2)}, u32[]{:S(2)}) %collective-permute-start.4) | collective-permute-done | bytes 471072 | tf_op jit(solution)/shard_map/ppermute | solution.py:380
  27.3 0.6 weight_second.4
  28.0 2.6 %collective-permute-start.8 = (bf16[80,1536]{1,0:T(8,128)(2,1)S(1)}, bf16[80,1536]{1,0:T(8,128)(2,1)S(1)}, u32[]{:S(2)}, u32[]{:S(2)}) collective-permute-start(bf16[80,1536]{1,0:T(8,128)(2,1)S(1)} %get-tuple-element.96), channel_id=1, source_target_pairs={{0,16},{4,20},{8,24},{12,28},{16,0},{20,4},{24,8},{28,12},{1,17},{... | collective-permute-start | bytes 737288 | tf_op jit(solution)/shard_map/ppermute | solution.py:380
  30.6 2.1 %weight_send.5 = (bf16[1,80,2944]{2,1,0:T(8,128)(2,1)S(1)}, f32[8,128]{1,0:T(8,128)S(1)}) custom-call(f32[8,128]{1,0:T(8,128)S(1)} %get-tuple-element.83.refs_0_, bf16[720,1024]{1,0:T(8,128)(2,1)S(1)} %copy-done.5, bf16[720,1024]{1,0:T(8,128)(2,1)S(1)} %get-tuple-element.84.refs_2_, bf16[320,1024]{1,0:T(8,128)(2,1)S(1)} %get-tuple-element.85.refs_3_, ...), custom_call_target="tpu_custom_call" | custom-call | flops 20000000000 | bytes 1024 | tf_op jit(solution)/shard_map/weight_send/pallas_call | solution.py:399
  32.7 1.6 %collective-permute-start.10 = (bf16[1,80,2944]{2,1,0:T(8,128)(2,1)S(1)}, bf16[1,80,2944]{2,1,0:T(8,128)(2,1)S(1)}, u32[]{:S(2)}, u32[]{:S(2)}) collective-permute-start(bf16[1,80,2944]{2,1,0:T(8,128)(2,1)S(1)} %get-tuple-element.101), channel_id=1, source_target_pairs={{0,8},{4,12},{8,0},{12,4},{16,24},{20,28},{24,16},{28,20},{1,9},{5... | collective-permute-start | bytes 1413128 | tf_op jit(solution)/shard_map/ppermute | solution.py:380
  34.3 2.1 %weight_send.6 = (bf16[1,80,2944]{2,1,0:T(8,128)(2,1)S(1)}, f32[8,128]{1,0:T(8,128)S(1)}) custom-call(f32[8,128]{1,0:T(8,128)S(1)} %get-tuple-element.86.refs_0_, bf16[720,1024]{1,0:T(8,128)(2,1)S(1)} %copy-done.5, bf16[720,1024]{1,0:T(8,128)(2,1)S(1)} %get-tuple-element.84.refs_2_, bf16[320,1024]{1,0:T(8,128)(2,1)S(1)} %get-tuple-element.87.refs_3_.refs_5_, ...), custom_call_target="tpu_custom_call" | custom-call | flops 20000000000 | bytes 1024 | tf_op jit(solution)/shard_map/weight_send/pallas_call | solution.py:399
  36.4 0.5 collective-permute-start.12
  37.0 2.6 %weight_keep.4 = (f32[1,80,2944]{2,1,0:T(8,128)S(1)}, f32[1,80,2944]{2,1,0:T(8,128)S(1)}, f32[8,128]{1,0:T(8,128)S(1)}) custom-call(f32[8,128]{1,0:T(8,128)S(1)} %get-tuple-element.88.refs_0_, bf16[720,1024]{1,0:T(8,128)(2,1)S(1)} %get-tuple-element.89.refs_1_, bf16[720,1024]{1,0:T(8,128)(2,1)S(1)} %get-tuple-element.90.refs_2_, ...), custom_call_target="tpu_custom_call" | custom-call | flops 24999999488 | bytes 1024 | tf_op jit(solution)/shard_map/weight_keep/pallas_call | solution.py:399
  39.6 2.7 %collective-permute-done.7.refs_2_ = bf16[2,656,256]{2,1,0:T(8,128)(2,1)S(1)} collective-permute-done((bf16[2,656,256]{2,1,0:T(8,128)(2,1)S(1)}, bf16[2,656,256]{2,1,0:T(8,128)(2,1)S(1)}, u32[]{:S(2)}, u32[]{:S(2)}) %collective-permute-start.7) | collective-permute-done | bytes 671776 | tf_op jit(solution)/shard_map/ppermute | solution.py:384
  42.3 0.7 frame_second.2
  43.0 0.6 collective-permute-start.15
  43.5 0.3 weight_end.3
  44.0 5.7 %frame_part.3 = (bf16[2,656,256]{2,1,0:T(8,128)(2,1)S(1)}, f32[2,640,256]{2,1,0:T(8,128)S(1)}, f32[8,128]{1,0:T(8,128)S(1)}) custom-call(f32[8,128]{1,0:T(8,128)S(1)} %get-tuple-element.98.refs_0_, bf16[2880,1280]{1,0:T(8,128)(2,1)S(1)} %get-tuple-element.77.refs_1_, bf16[4,320,256]{2,1,0:T(8,128)(2,1)S(1)} %copy-done.1), custom_call_target="tpu_custom_call" | custom-call | flops 42500001792 | bytes 1024 | tf_op jit(solution)/shard_map/frame_part/pallas_call | solution.py:399
  49.7 1.6 %collective-permute-start.14 = (bf16[2,656,256]{2,1,0:T(8,128)(2,1)S(1)}, bf16[2,656,256]{2,1,0:T(8,128)(2,1)S(1)}, u32[]{:S(2)}, u32[]{:S(2)}) collective-permute-start(bf16[2,656,256]{2,1,0:T(8,128)(2,1)S(1)} %get-tuple-element.113), channel_id=1, source_target_pairs={{0,2},{1,3},{2,0},{3,1},{4,6},{5,7},{6,4},{7,5},{8,10},{9,11},{10,... | collective-permute-start | bytes 2015240 | tf_op jit(solution)/shard_map/ppermute | solution.py:384
  51.3 0.6 weight_second.5
  51.9 2.7 %collective-permute-start.13 = (bf16[80,1536]{1,0:T(8,128)(2,1)S(1)}, bf16[80,1536]{1,0:T(8,128)(2,1)S(1)}, u32[]{:S(2)}, u32[]{:S(2)}) collective-permute-start(bf16[80,1536]{1,0:T(8,128)(2,1)S(1)} %get-tuple-element.110), channel_id=1, source_target_pairs={{0,16},{4,20},{8,24},{12,28},{16,0},{20,4},{24,8},{28,12},{1,17},{... | collective-permute-start | bytes 737288 | tf_op jit(solution)/shard_map/ppermute | solution.py:380
  54.6 2.1 %weight_send.7 = (bf16[1,80,2944]{2,1,0:T(8,128)(2,1)S(1)}, f32[8,128]{1,0:T(8,128)S(1)}) custom-call(f32[8,128]{1,0:T(8,128)S(1)} %get-tuple-element.102.refs_0_, bf16[720,1024]{1,0:T(8,128)(2,1)S(1)} %copy-done.5, bf16[720,1024]{1,0:T(8,128)(2,1)S(1)} %get-tuple-element.84.refs_2_, bf16[320,1024]{1,0:T(8,128)(2,1)S(1)} %get-tuple-element.103.refs_3_, ...), custom_call_target="tpu_custom_call" | custom-call | flops 20000000000 | bytes 1024 | tf_op jit(solution)/shard_map/weight_send/pallas_call | solution.py:399
  56.7 1.2 %collective-permute-start.16 = (bf16[1,80,2944]{2,1,0:T(8,128)(2,1)S(1)}, bf16[1,80,2944]{2,1,0:T(8,128)(2,1)S(1)}, u32[]{:S(2)}, u32[]{:S(2)}) collective-permute-start(bf16[1,80,2944]{2,1,0:T(8,128)(2,1)S(1)} %get-tuple-element.122), channel_id=1, source_target_pairs={{0,8},{4,12},{8,0},{12,4},{16,24},{20,28},{24,16},{28,20},{1,9},{5... | collective-permute-start | bytes 1413128 | tf_op jit(solution)/shard_map/ppermute | solution.py:380
  57.9 1.7 %weight_keep.5 = (f32[1,80,2944]{2,1,0:T(8,128)S(1)}, f32[8,128]{1,0:T(8,128)S(1)}) custom-call(f32[8,128]{1,0:T(8,128)S(1)} %get-tuple-element.104.refs_0_, bf16[720,1024]{1,0:T(8,128)(2,1)S(1)} %get-tuple-element.89.refs_1_, bf16[720,1024]{1,0:T(8,128)(2,1)S(1)} %get-tuple-element.90.refs_2_, bf16[320,1024]{1,0:T(8,128)(2,1)S(1)} %get-tuple-element.103.refs_3_, ...), custom_call_target="tpu_custom_call" | custom-call | flops 20000000000 | bytes 1024 | tf_op jit(solution)/shard_map/weight_keep/pallas_call | solution.py:399
  59.6 4.2 %collective-permute-done.12.refs_2_ = bf16[1,80,2944]{2,1,0:T(8,128)(2,1)S(1)} collective-permute-done((bf16[1,80,2944]{2,1,0:T(8,128)(2,1)S(1)}, bf16[1,80,2944]{2,1,0:T(8,128)(2,1)S(1)}, u32[]{:S(2)}, u32[]{:S(2)}) %collective-permute-start.12) | collective-permute-done | bytes 471072 | tf_op jit(solution)/shard_map/ppermute | solution.py:380
  63.8 0.6 weight_second.6
  64.6 2.5 %collective-permute-done.13.refs_2_ = bf16[80,1536]{1,0:T(8,128)(2,1)S(1)} collective-permute-done((bf16[80,1536]{1,0:T(8,128)(2,1)S(1)}, bf16[80,1536]{1,0:T(8,128)(2,1)S(1)}, u32[]{:S(2)}, u32[]{:S(2)}) %collective-permute-start.13) | collective-permute-done | bytes 245792 | tf_op jit(solution)/shard_map/ppermute | solution.py:380
  67.3 0.7 frame_second.3
  68.0 0.6 collective-permute-start.17
  68.7 1.1 %weight_last.2 = (f32[40,11520]{1,0:T(8,128)}, f32[8,128]{1,0:T(8,128)S(1)}) custom-call(f32[8,128]{1,0:T(8,128)S(1)} %get-tuple-element.114.refs_0_, f32[40,2944]{1,0:T(8,128)S(1)} %get-tuple-element.115.refs_1_, f32[40,2944]{1,0:T(8,128)S(1)} %get-tuple-element.116.refs_2_), custom_call_target="tpu_custom_call" | custom-call | flops 12000000000 | bytes 1024 | tf_op jit(solution)/shard_map/weight_last/pallas_call | solution.py:399
  69.8 0.9 frame_last.2
  70.8 9.0 %collective-permute-done.16.refs_2_ = bf16[1,80,2944]{2,1,0:T(8,128)(2,1)S(1)} collective-permute-done((bf16[1,80,2944]{2,1,0:T(8,128)(2,1)S(1)}, bf16[1,80,2944]{2,1,0:T(8,128)(2,1)S(1)}, u32[]{:S(2)}, u32[]{:S(2)}) %collective-permute-start.16) | collective-permute-done | bytes 471072 | tf_op jit(solution)/shard_map/ppermute | solution.py:380
  79.8 0.6 weight_second.7
  80.4 1.1 %collective-permute-start.19 = (bf16[80,1536]{1,0:T(8,128)(2,1)S(1)}, bf16[80,1536]{1,0:T(8,128)(2,1)S(1)}, u32[]{:S(2)}, u32[]{:S(2)}) collective-permute-start(bf16[80,1536]{1,0:T(8,128)(2,1)S(1)} %get-tuple-element.136), channel_id=1, source_target_pairs={{0,16},{4,20},{8,24},{12,28},{16,0},{20,4},{24,8},{28,12},{1,17},{... | collective-permute-start | bytes 737288 | tf_op jit(solution)/shard_map/ppermute | solution.py:380
  81.5 10.8 %response.1 = (bf16[4,320,256]{2,1,0:T(8,128)(2,1)}, f32[8,128]{1,0:T(8,128)S(1)}) custom-call(f32[8,128]{1,0:T(8,128)S(1)} %get-tuple-element.123.refs_0_, bf16[2880,1280]{1,0:T(8,128)(2,1)S(1)} %get-tuple-element.77.refs_1_, f32[320]{0:T(512)S(1)} %copy-done.3, bf16[4,320,256]{2,1,0:T(8,128)(2,1)S(1)} %copy-done.2, ...), custom_call_target="tpu_custom_call" | custom-call | flops 54999998464 | bytes 1024 | tf_op jit(solution)/shard_map/response/pallas_call | solution.py:399
  92.3 0.9 frame_last.3
  93.3 0.3 weight_end.5
  93.5 1.8 %weight_last.3 = (f32[40,11520]{1,0:T(8,128)}, f32[8,128]{1,0:T(8,128)}) custom-call(f32[8,128]{1,0:T(8,128)S(1)} %get-tuple-element.133.refs_0_, f32[40,2944]{1,0:T(8,128)S(1)} %get-tuple-element.134.refs_1_, f32[40,2944]{1,0:T(8,128)S(1)} %get-tuple-element.135.refs_2_, ...), custom_call_target="tpu_custom_call", output_to_operand_aliasing={{0}: (4, {})} | custom-call | flops 12000000000 | bytes 1024 | tf_op jit(solution)/shard_map/weight_last/pallas_call | solution.py:399
  (37 shorter events, 0.7 us)
Async XLA Ops:
  0.6 7.8 %collective-permute-start.1 = (bf16[4,320,256]{2,1,0:T(8,128)(2,1)}, bf16[4,320,256]{2,1,0:T(8,128)(2,1)S(1)}, u32[]{:S(2)}, u32[]{:S(2)}) collective-permute-start(bf16[4,320,256]{2,1,0:T(8,128)(2,1)} %refs_3_.1), channel_id=1, source_target_pairs={{0,4},{4,0},{8,12},{12,8},{16,20},{20,16},{24,28},{28,24},{1,5},{5... | collective-permute-start | bytes 1966088 | tf_op jit(solution)/shard_map/ppermute | solution.py:376
  1.1 23.1 %collective-permute-start.2 = (bf16[4,320,256]{2,1,0:T(8,128)(2,1)}, bf16[4,320,256]{2,1,0:T(8,128)(2,1)S(1)}, u32[]{:S(2)}, u32[]{:S(2)}) collective-permute-start(bf16[4,320,256]{2,1,0:T(8,128)(2,1)} %refs_3_.1), channel_id=1, source_target_pairs={{0,1},{1,0},{2,3},{3,2},{4,5},{5,4},{6,7},{7,6},{8,9},{9,8},{10,11... | collective-permute-start | bytes 1966088 | tf_op jit(solution)/shard_map/ppermute | solution.py:384
  3.7 20.9 %collective-permute-start.3 = (bf16[4,320,256]{2,1,0:T(8,128)(2,1)}, bf16[4,320,256]{2,1,0:T(8,128)(2,1)S(1)}, u32[]{:S(2)}, u32[]{:S(2)}) collective-permute-start(bf16[4,320,256]{2,1,0:T(8,128)(2,1)} %refs_3_.1), channel_id=1, source_target_pairs={{0,2},{1,3},{2,0},{3,1},{4,6},{5,7},{6,4},{7,5},{8,10},{9,11},{10,... | collective-permute-start | bytes 1966088 | tf_op jit(solution)/shard_map/ppermute | solution.py:384
  5.2 3.2 %collective-permute-start = (bf16[4,320,256]{2,1,0:T(8,128)(2,1)}, bf16[4,320,256]{2,1,0:T(8,128)(2,1)S(1)}, u32[]{:S(2)}, u32[]{:S(2)}) collective-permute-start(bf16[4,320,256]{2,1,0:T(8,128)(2,1)} %refs_2_.4), channel_id=1, source_target_pairs={{0,4},{4,0},{8,12},{12,8},{16,20},{20,16},{24,28},{28,24},{1,5},{5... | collective-permute-start | bytes 1966088 | tf_op jit(solution)/shard_map/ppermute | solution.py:376
  8.5 1.4 %copy-start.4 = (bf16[720,1024]{1,0:T(8,128)(2,1)S(1)}, bf16[720,1024]{1,0:T(8,128)(2,1)}, u32[]{:S(2)}) copy-start(bf16[720,1024]{1,0:T(8,128)(2,1)} %get-tuple-element.72.refs_1_) | copy-start | bytes 4423684
  9.9 1.1 %copy-start.6 = (bf16[320,1024]{1,0:T(8,128)(2,1)S(1)}, bf16[320,1024]{1,0:T(8,128)(2,1)}, u32[]{:S(2)}) copy-start(bf16[320,1024]{1,0:T(8,128)(2,1)} %get-tuple-element.73.refs_2_.refs_3_) | copy-start | bytes 1966084
  10.9 0.7 copy-start.8
  11.6 4.1 %copy-start = (bf16[320,11520]{1,0:T(8,128)(2,1)S(1)}, bf16[320,11520]{1,0:T(8,128)(2,1)}, u32[]{:S(2)}) copy-start(bf16[320,11520]{1,0:T(8,128)(2,1)} %refs_5_.1) | copy-start | bytes 22118404
  11.6 4.1 %copy-start.1 = (bf16[4,320,256]{2,1,0:T(8,128)(2,1)S(1)}, bf16[4,320,256]{2,1,0:T(8,128)(2,1)}, u32[]{:S(2)}) copy-start(bf16[4,320,256]{2,1,0:T(8,128)(2,1)} %refs_2_.4) | copy-start | bytes 1966084
  11.6 4.1 %copy-start.7 = (bf16[320,1024]{1,0:T(8,128)(2,1)S(1)}, bf16[320,1024]{1,0:T(8,128)(2,1)}, u32[]{:S(2)}) copy-start(bf16[320,1024]{1,0:T(8,128)(2,1)} %get-tuple-element.73.refs_2_.refs_3_) | copy-start | bytes 1966084
  14.1 13.3 %collective-permute-start.4 = (bf16[1,80,2944]{2,1,0:T(8,128)(2,1)S(1)}, bf16[1,80,2944]{2,1,0:T(8,128)(2,1)S(1)}, u32[]{:S(2)}, u32[]{:S(2)}) collective-permute-start(bf16[1,80,2944]{2,1,0:T(8,128)(2,1)S(1)} %get-tuple-element.82), channel_id=1, source_target_pairs={{0,8},{4,12},{8,0},{12,4},{16,24},{20,28},{24,16},{28,20},{1,9},{5... | collective-permute-start | bytes 1413128 | tf_op jit(solution)/shard_map/ppermute | solution.py:380
  24.3 6.3 %collective-permute-start.5 = (bf16[320,1024]{1,0:T(8,128)(2,1)S(1)}, bf16[320,1024]{1,0:T(8,128)(2,1)S(1)}, u32[]{:S(2)}, u32[]{:S(2)}) collective-permute-start(bf16[320,1024]{1,0:T(8,128)(2,1)S(1)} %get-tuple-element.85.refs_3_), channel_id=1, source_target_pairs={{0,4},{4,0},{8,12},{12,8},{16,20},{20,16},{24,28},{28,24},{1,5},{5... | collective-permute-start | bytes 1966088 | tf_op jit(solution)/shard_map/ppermute | solution.py:376
  24.7 9.6 %collective-permute-start.6 = (bf16[320,1024]{1,0:T(8,128)(2,1)S(1)}, bf16[320,1024]{1,0:T(8,128)(2,1)S(1)}, u32[]{:S(2)}, u32[]{:S(2)}) collective-permute-start(bf16[320,1024]{1,0:T(8,128)(2,1)S(1)} %get-tuple-element.87.refs_3_.refs_5_), channel_id=1, source_target_pairs={{0,4},{4,0},{8,12},{12,8},{16,20},{20,16},{24,28},{28,24},{1,5},{5... | collective-permute-start | bytes 1966088 | tf_op jit(solution)/shard_map/ppermute | solution.py:376
  25.1 17.2 %collective-permute-start.7 = (bf16[2,656,256]{2,1,0:T(8,128)(2,1)S(1)}, bf16[2,656,256]{2,1,0:T(8,128)(2,1)S(1)}, u32[]{:S(2)}, u32[]{:S(2)}) collective-permute-start(bf16[2,656,256]{2,1,0:T(8,128)(2,1)S(1)} %get-tuple-element.93), channel_id=1, source_target_pairs={{0,1},{1,0},{2,3},{3,2},{4,5},{5,4},{6,7},{7,6},{8,9},{9,8},{10,11... | collective-permute-start | bytes 2015240 | tf_op jit(solution)/shard_map/ppermute | solution.py:384
  25.6 18.2 %collective-permute-start.9 = (bf16[4,320,256]{2,1,0:T(8,128)(2,1)S(1)}, bf16[4,320,256]{2,1,0:T(8,128)(2,1)S(1)}, u32[]{:S(2)}, u32[]{:S(2)}) collective-permute-start(bf16[4,320,256]{2,1,0:T(8,128)(2,1)S(1)} %collective-permute-done.2.refs_1_.refs_4_), channel_id=1, source_target_pairs={{0,2},{1,3},{2,0},{3,1},{4,6},{5,7},{6,4},{7,5},{8,10},{9,11},{10,... | collective-permute-start | bytes 1966088 | tf_op jit(solution)/shard_map/ppermute | solution.py:384
  27.3 3.3 %copy-start.5 = (bf16[720,1024]{1,0:T(8,128)(2,1)S(1)}, bf16[720,1024]{1,0:T(8,128)(2,1)}, u32[]{:S(2)}) copy-start(bf16[720,1024]{1,0:T(8,128)(2,1)} %get-tuple-element.72.refs_1_) | copy-start | bytes 4423684
  28.0 15.6 %collective-permute-start.8 = (bf16[80,1536]{1,0:T(8,128)(2,1)S(1)}, bf16[80,1536]{1,0:T(8,128)(2,1)S(1)}, u32[]{:S(2)}, u32[]{:S(2)}) collective-permute-start(bf16[80,1536]{1,0:T(8,128)(2,1)S(1)} %get-tuple-element.96), channel_id=1, source_target_pairs={{0,16},{4,20},{8,24},{12,28},{16,0},{20,4},{24,8},{28,12},{1,17},{... | collective-permute-start | bytes 737288 | tf_op jit(solution)/shard_map/ppermute | solution.py:380
  32.7 18.6 %collective-permute-start.10 = (bf16[1,80,2944]{2,1,0:T(8,128)(2,1)S(1)}, bf16[1,80,2944]{2,1,0:T(8,128)(2,1)S(1)}, u32[]{:S(2)}, u32[]{:S(2)}) collective-permute-start(bf16[1,80,2944]{2,1,0:T(8,128)(2,1)S(1)} %get-tuple-element.101), channel_id=1, source_target_pairs={{0,8},{4,12},{8,0},{12,4},{16,24},{20,28},{24,16},{28,20},{1,9},{5... | collective-permute-start | bytes 1413128 | tf_op jit(solution)/shard_map/ppermute | solution.py:380
  36.4 27.4 %collective-permute-start.12 = (bf16[1,80,2944]{2,1,0:T(8,128)(2,1)S(1)}, bf16[1,80,2944]{2,1,0:T(8,128)(2,1)S(1)}, u32[]{:S(2)}, u32[]{:S(2)}) collective-permute-start(bf16[1,80,2944]{2,1,0:T(8,128)(2,1)S(1)} %get-tuple-element.107), channel_id=1, source_target_pairs={{0,8},{4,12},{8,0},{12,4},{16,24},{20,28},{24,16},{28,20},{1,9},{5... | collective-permute-start | bytes 1413128 | tf_op jit(solution)/shard_map/ppermute | solution.py:380
  43.0 26.8 %collective-permute-start.15 = (bf16[656,256]{1,0:T(8,128)(2,1)S(1)}, bf16[656,256]{1,0:T(8,128)(2,1)S(1)}, u32[]{:S(2)}, u32[]{:S(2)}) collective-permute-start(bf16[656,256]{1,0:T(8,128)(2,1)S(1)} %get-tuple-element.119), channel_id=1, source_target_pairs={{0,2},{1,3},{2,0},{3,1},{4,6},{5,7},{6,4},{7,5},{8,10},{9,11},{10,... | collective-permute-start | bytes 1007624 | tf_op jit(solution)/shard_map/ppermute | solution.py:384
  43.9 10.7 %collective-permute-start.11 = (bf16[320,1024]{1,0:T(8,128)(2,1)S(1)}, bf16[320,1024]{1,0:T(8,128)(2,1)S(1)}, u32[]{:S(2)}, u32[]{:S(2)}) collective-permute-start(bf16[320,1024]{1,0:T(8,128)(2,1)S(1)} %get-tuple-element.103.refs_3_), channel_id=1, source_target_pairs={{0,4},{4,0},{8,12},{12,8},{16,20},{20,16},{24,28},{28,24},{1,5},{5... | collective-permute-start | bytes 1966088 | tf_op jit(solution)/shard_map/ppermute | solution.py:376
  49.7 17.6 %collective-permute-start.14 = (bf16[2,656,256]{2,1,0:T(8,128)(2,1)S(1)}, bf16[2,656,256]{2,1,0:T(8,128)(2,1)S(1)}, u32[]{:S(2)}, u32[]{:S(2)}) collective-permute-start(bf16[2,656,256]{2,1,0:T(8,128)(2,1)S(1)} %get-tuple-element.113), channel_id=1, source_target_pairs={{0,2},{1,3},{2,0},{3,1},{4,6},{5,7},{6,4},{7,5},{8,10},{9,11},{10,... | collective-permute-start | bytes 2015240 | tf_op jit(solution)/shard_map/ppermute | solution.py:384
  51.9 15.1 %collective-permute-start.13 = (bf16[80,1536]{1,0:T(8,128)(2,1)S(1)}, bf16[80,1536]{1,0:T(8,128)(2,1)S(1)}, u32[]{:S(2)}, u32[]{:S(2)}) collective-permute-start(bf16[80,1536]{1,0:T(8,128)(2,1)S(1)} %get-tuple-element.110), channel_id=1, source_target_pairs={{0,16},{4,20},{8,24},{12,28},{16,0},{20,4},{24,8},{28,12},{1,17},{... | collective-permute-start | bytes 737288 | tf_op jit(solution)/shard_map/ppermute | solution.py:380
  56.7 23.1 %collective-permute-start.16 = (bf16[1,80,2944]{2,1,0:T(8,128)(2,1)S(1)}, bf16[1,80,2944]{2,1,0:T(8,128)(2,1)S(1)}, u32[]{:S(2)}, u32[]{:S(2)}) collective-permute-start(bf16[1,80,2944]{2,1,0:T(8,128)(2,1)S(1)} %get-tuple-element.122), channel_id=1, source_target_pairs={{0,8},{4,12},{8,0},{12,4},{16,24},{20,28},{24,16},{28,20},{1,9},{5... | collective-permute-start | bytes 1413128 | tf_op jit(solution)/shard_map/ppermute | solution.py:380
  64.5 28.8 %collective-permute-start.18 = (bf16[80,1536]{1,0:T(8,128)(2,1)S(1)}, bf16[80,1536]{1,0:T(8,128)(2,1)S(1)}, u32[]{:S(2)}, u32[]{:S(2)}) collective-permute-start(bf16[80,1536]{1,0:T(8,128)(2,1)S(1)} %get-tuple-element.132), channel_id=1, source_target_pairs={{0,16},{4,20},{8,24},{12,28},{16,0},{20,4},{24,8},{28,12},{1,17},{... | collective-permute-start | bytes 737288 | tf_op jit(solution)/shard_map/ppermute | solution.py:380
  68.0 24.3 %collective-permute-start.17 = (bf16[656,256]{1,0:T(8,128)(2,1)S(1)}, bf16[656,256]{1,0:T(8,128)(2,1)S(1)}, u32[]{:S(2)}, u32[]{:S(2)}) collective-permute-start(bf16[656,256]{1,0:T(8,128)(2,1)S(1)} %get-tuple-element.127), channel_id=1, source_target_pairs={{0,1},{1,0},{2,3},{3,2},{4,5},{5,4},{6,7},{7,6},{8,9},{9,8},{10,11... | collective-permute-start | bytes 1007624 | tf_op jit(solution)/shard_map/ppermute | solution.py:384
  79.8 1.8 %copy-start.2 = (bf16[4,320,256]{2,1,0:T(8,128)(2,1)S(1)}, bf16[4,320,256]{2,1,0:T(8,128)(2,1)}, u32[]{:S(2)}) copy-start(bf16[4,320,256]{2,1,0:T(8,128)(2,1)} %refs_3_.1) | copy-start | bytes 1966084
  79.8 1.8 %copy-start.3 = (f32[320]{0:T(512)S(1)}, f32[320]{0:T(512)}, u32[]{:S(2)}) copy-start(f32[320]{0:T(512)} %refs_2_.5) | copy-start | bytes 3844
  80.4 13.1 %collective-permute-start.19 = (bf16[80,1536]{1,0:T(8,128)(2,1)S(1)}, bf16[80,1536]{1,0:T(8,128)(2,1)S(1)}, u32[]{:S(2)}, u32[]{:S(2)}) collective-permute-start(bf16[80,1536]{1,0:T(8,128)(2,1)S(1)} %get-tuple-element.136), channel_id=1, source_target_pairs={{0,16},{4,20},{8,24},{12,28},{16,0},{20,4},{24,8},{28,12},{1,17},{... | collective-permute-start | bytes 737288 | tf_op jit(solution)/shard_map/ppermute | solution.py:380
